TPU v7x, 32 devices: a whole 2x2x4 slice. The times are simulated.
32 devices in a mesh: sens: 4 (over x, core), par: 8 (over z, y).
Axes of the slice: x: 2, y: 2, z: 4, core: 2. Of those that a mesh axis runs over, the one named last changes fastest.
Arguments:
- model: bfloat16 [4, 128, 256], P('sens', 'par'), may hold values from -6 to 6
- kernel: bfloat16 [512, 128, 256], P('sens', 'par'), may hold values from -0.03125 to 0.03125
- observed: float32 [4, 512, 256], P(None, 'sens'), may hold values from -6 to 6
- weights: float32 [512], P('sens'), may hold values from 0.25 to 4
Outputs:
- gradient: float32 [4, 128, 256], P('sens', 'par')
- misfit: float32 [], replicated
All inputs are finite; a program needn't handle non-finite values.
Results may differ from a plain program's by a relative error of at most 0.0027.
Values may be sent and summed in bfloat16 or wider, within the bound.
No kernel may reach another device: no remote copies, remote signals or barrier semaphores. Data moves between devices by JAX's collectives and lax.ppermute only.
A program may use at most 192 MiB of HBM per device.

v0:
```python
import jax
import jax.numpy as jnp
from jax import lax
from jax.sharding import PartitionSpec as P


def causal_rows(series):
    length_steps = series.shape[-1]
    padded = jnp.concatenate([series, jnp.zeros_like(series)], axis=-1)
    reps = (1,) * (series.ndim - 1) + (length_steps,)
    flat = jnp.tile(padded, reps)
    stride = 2 * length_steps - 1
    flat = flat[..., : length_steps * stride].reshape(series.shape[:-1] + (length_steps, stride))
    return flat[..., :length_steps]


def leading_rows(series):
    length_steps = series.shape[-1]
    padded = jnp.concatenate([series, jnp.zeros_like(series)], axis=-1)
    reps = (1,) * (series.ndim - 1) + (length_steps + 1,)
    flat = jnp.tile(padded, reps)
    stride = 2 * length_steps + 1
    flat = flat[..., : length_steps * stride].reshape(series.shape[:-1] + (length_steps, stride))
    return flat[..., :length_steps]


def local(model, kernel, observed, weights):
    full_model = lax.all_gather(model, "sens", axis=0, tiled=True)
    toeplitz_operator = causal_rows(full_model)
    summed_terms = jnp.einsum(
        "oua,luaz->loz", kernel, toeplitz_operator, preferred_element_type=jnp.float32
    )
    vectors = full_model.shape[0]
    sensors = weights.shape[0]
    steps = full_model.shape[2]
    entries = vectors * sensors * lax.axis_size("sens") * steps
    predicted = lax.psum(summed_terms, "par")
    mismatch = predicted - observed
    weighted_residual = weights[None, :, None] * mismatch
    residual = weighted_residual.astype(jnp.bfloat16)
    squared = lax.psum(jnp.sum(weighted_residual * mismatch), "sens")
    misfit = 0.5 * squared / entries

    def single_adjoint(series):
        shifted = leading_rows(series)
        return jnp.einsum("spk,skt->pt", kernel, shifted, preferred_element_type=jnp.float32)

    adjoint_pieces = lax.map(single_adjoint, residual)
    gradient = lax.psum_scatter(adjoint_pieces, "sens", scatter_dimension=0, tiled=True)
    return (gradient, misfit)


def solution(mesh):
    return jax.shard_map(
        local,
        mesh=mesh,
        in_specs=(P("sens", "par", None), P("sens", "par", None), P(None, "sens", None), P("sens")),
        out_specs=(P("sens", "par", None), P()),
        check_vma=False,
    )
```

profile of v0, /device:TPU:0, one launch (start us, length us, event | category | flops | bytes accessed | tf_op | source)
XLA Modules:
  0.0 528.0 jit_solution(12950488942787575887)
XLA Ops:
  7.2 0.0 all-reduce.4.cloned.1.call-start
  7.2 6.4 %all_gather.3 = bf16[4,16,256]{2,1,0:T(8,128)(2,1)S(1)} all-gather(bf16[1,16,256]{2,1,0:T(8,128)(2,1)} %param.6), channel_id=1, replica_groups=mesh['sens'=4,'par'=8] {'sens'}, dimensions={0}, use_global_device_ids=true | all-gather | bytes 40960 | tf_op jit(solution)/shard_map/all_gather | solution.py:28
  13.6 5.9 %tile.8 = bf16[4,16,256,512]{3,2,1,0:T(8,128)(2,1)} broadcast(bf16[4,16,512]{2,1,0:T(8,128)(2,1)S(1)} %concatenate.6), dimensions={0,1,3} | broadcast | bytes 16842752 | tf_op jit(solution)/shard_map/tile | solution.py:11
  19.5 17.0 %tile.9 = bf16[4,16,131072]{2,1,0:T(8,128)(2,1)} reshape(bf16[4,16,256,512]{3,2,1,0:T(8,128)(2,1)} %tile.8) | data formatting | bytes 33554432 | tf_op jit(solution)/shard_map/tile | solution.py:11
  36.5 13.7 %slice.16 = bf16[4,16,130816]{2,1,0:T(8,128)(2,1)} slice(bf16[4,16,131072]{2,1,0:T(8,128)(2,1)} %tile.9), slice={[0:4], [0:16], [0:130816]} | slice | bytes 33488896 | tf_op jit(solution)/shard_map/slice | solution.py:13
  50.2 36.2 %reshape.19 = bf16[4,16,256,511]{3,2,1,0:T(8,128)(2,1)} reshape(bf16[4,16,130816]{2,1,0:T(8,128)(2,1)} %slice.16) | data formatting | bytes 33488896 | tf_op jit(solution)/shard_map/reshape | solution.py:13
  86.4 6.6 %fusion.10 = f32[4,128,256]{1,2,0:T(8,128)} fusion(bf16[4,16,256,511]{3,2,1,0:T(8,128)(2,1)} %reshape.19, bf16[128,16,256]{2,1,0:T(8,128)(2,1)S(1)} %copy-done), kind=kOutput, calls=%fused_computation.7 | convolution fusion | flops 1073741824 | bytes 9961472 | tf_op jit(solution)/shard_map/oua,luaz->loz/dot_general | solution.py:30
  93.0 0.0 all-reduce.4.cloned.1.call-update
  93.1 0.0 reduce-scatter.2.cloned.1.call-start
  93.1 1.6 copy.19
  94.8 0.2 copy.18
  95.0 72.3 %all-reduce.4.cloned.1.call-done = f32[4,128,256]{1,2,0:T(8,128)} async-done(((f32[4,128,256]{1,2,0:T(8,128)}), f32[4,128,256]{1,2,0:T(8,128)}) %all-reduce.4.cloned.1.call-update) | async-done | bytes 524304 | tf_op jit(solution)/shard_map/psum | solution.py:37
  167.3 1.9 fusion.15
  169.2 332.0 %while.10 = (s32[]{:T(128)}, f32[4,16,256]{2,1,0:T(8,128)}, bf16[4,128,256]{1,2,0:T(8,128)(2,1)S(1)}, bf16[128,16,256]{0,1,2:T(8,128)(2,1)S(1)}, s32[]{:T(128)}, /*index=5*/bf16[]{:T(256)}) while((s32[]{:T(128)}, f32[4,16,256]{2,1,0:T(8,128)}, bf16[4,128,256]{1,2,0:T(8,128)(2,1)S(1)}, bf16[128,16,256]{0,1,2:T(8,128)(2,1)S(1)}, s32[]{:T(128)}, ...), condition=%wide.region_2.0_spmd, body=%wide.region_1.0_spmd.sunk | while | flops 268435456 | bytes 186466896 | solution.py:48
  169.2 13.5 %tile.21 = bf16[128,257,512]{0,2,1:T(8,128)(2,1)} broadcast(bf16[128,512]{0,1:T(8,128)(2,1)S(1)} %concatenate.8), dimensions={0,2} | broadcast | bytes 33816576 | tf_op jit(solution)/shard_map/while/body/eval_jaxpr/tile | solution.py:21
  182.7 22.9 %slice.31 = bf16[128,131328]{0,1:T(8,128)(2,1)} slice(bf16[128,131584]{0,1:T(8,128)(2,1)} %bitcast.32), slice={[0:128], [0:131328]} | slice | bytes 67239936 | tf_op jit(solution)/shard_map/while/body/eval_jaxpr/slice | solution.py:23
  205.6 37.7 %reshape.24 = bf16[128,256,513]{0,2,1:T(8,128)(2,1)} reshape(bf16[128,131328]{0,1:T(8,128)(2,1)} %slice.31) | data formatting | bytes 67239936 | tf_op jit(solution)/shard_map/while/body/eval_jaxpr/reshape | solution.py:23
  243.2 8.9 %fusion.22 = f32[4,16,256]{2,1,0:T(8,128)} fusion(f32[4,16,256]{2,1,0:T(8,128)} %get-tuple-element.79, s32[]{:T(128)} %get-tuple-element.78, bf16[128,16,256]{0,1,2:T(8,128)(2,1)S(1)} %get-tuple-element.87, bf16[128,256,513]{0,2,1:T(8,128)(2,1)} %reshape.24), kind=kOutput, calls=%fused_computation.3.clone.1 | convolution fusion | flops 268435456 | bytes 17842688 | tf_op jit(solution)/shard_map/while/body/eval_jaxpr/spk,skt->pt/dot_general | solution.py:46
  252.2 13.5 %tile.21 = bf16[128,257,512]{0,2,1:T(8,128)(2,1)} broadcast(bf16[128,512]{0,1:T(8,128)(2,1)S(1)} %concatenate.8), dimensions={0,2} | broadcast | bytes 33816576 | tf_op jit(solution)/shard_map/while/body/eval_jaxpr/tile | solution.py:21
  265.7 22.9 %slice.31 = bf16[128,131328]{0,1:T(8,128)(2,1)} slice(bf16[128,131584]{0,1:T(8,128)(2,1)} %bitcast.32), slice={[0:128], [0:131328]} | slice | bytes 67239936 | tf_op jit(solution)/shard_map/while/body/eval_jaxpr/slice | solution.py:23
  288.6 37.7 %reshape.24 = bf16[128,256,513]{0,2,1:T(8,128)(2,1)} reshape(bf16[128,131328]{0,1:T(8,128)(2,1)} %slice.31) | data formatting | bytes 67239936 | tf_op jit(solution)/shard_map/while/body/eval_jaxpr/reshape | solution.py:23
  326.2 8.9 %fusion.22 = f32[4,16,256]{2,1,0:T(8,128)} fusion(f32[4,16,256]{2,1,0:T(8,128)} %get-tuple-element.79, s32[]{:T(128)} %get-tuple-element.78, bf16[128,16,256]{0,1,2:T(8,128)(2,1)S(1)} %get-tuple-element.87, bf16[128,256,513]{0,2,1:T(8,128)(2,1)} %reshape.24), kind=kOutput, calls=%fused_computation.3.clone.1 | convolution fusion | flops 268435456 | bytes 17842688 | tf_op jit(solution)/shard_map/while/body/eval_jaxpr/spk,skt->pt/dot_general | solution.py:46
  335.2 13.5 %tile.21 = bf16[128,257,512]{0,2,1:T(8,128)(2,1)} broadcast(bf16[128,512]{0,1:T(8,128)(2,1)S(1)} %concatenate.8), dimensions={0,2} | broadcast | bytes 33816576 | tf_op jit(solution)/shard_map/while/body/eval_jaxpr/tile | solution.py:21
  348.7 22.9 %slice.31 = bf16[128,131328]{0,1:T(8,128)(2,1)} slice(bf16[128,131584]{0,1:T(8,128)(2,1)} %bitcast.32), slice={[0:128], [0:131328]} | slice | bytes 67239936 | tf_op jit(solution)/shard_map/while/body/eval_jaxpr/slice | solution.py:23
  371.6 37.7 %reshape.24 = bf16[128,256,513]{0,2,1:T(8,128)(2,1)} reshape(bf16[128,131328]{0,1:T(8,128)(2,1)} %slice.31) | data formatting | bytes 67239936 | tf_op jit(solution)/shard_map/while/body/eval_jaxpr/reshape | solution.py:23
  409.2 8.9 %fusion.22 = f32[4,16,256]{2,1,0:T(8,128)} fusion(f32[4,16,256]{2,1,0:T(8,128)} %get-tuple-element.79, s32[]{:T(128)} %get-tuple-element.78, bf16[128,16,256]{0,1,2:T(8,128)(2,1)S(1)} %get-tuple-element.87, bf16[128,256,513]{0,2,1:T(8,128)(2,1)} %reshape.24), kind=kOutput, calls=%fused_computation.3.clone.1 | convolution fusion | flops 268435456 | bytes 17842688 | tf_op jit(solution)/shard_map/while/body/eval_jaxpr/spk,skt->pt/dot_general | solution.py:46
  418.2 13.5 %tile.21 = bf16[128,257,512]{0,2,1:T(8,128)(2,1)} broadcast(bf16[128,512]{0,1:T(8,128)(2,1)S(1)} %concatenate.8), dimensions={0,2} | broadcast | bytes 33816576 | tf_op jit(solution)/shard_map/while/body/eval_jaxpr/tile | solution.py:21
  431.7 22.9 %slice.31 = bf16[128,131328]{0,1:T(8,128)(2,1)} slice(bf16[128,131584]{0,1:T(8,128)(2,1)} %bitcast.32), slice={[0:128], [0:131328]} | slice | bytes 67239936 | tf_op jit(solution)/shard_map/while/body/eval_jaxpr/slice | solution.py:23
  454.6 37.7 %reshape.24 = bf16[128,256,513]{0,2,1:T(8,128)(2,1)} reshape(bf16[128,131328]{0,1:T(8,128)(2,1)} %slice.31) | data formatting | bytes 67239936 | tf_op jit(solution)/shard_map/while/body/eval_jaxpr/reshape | solution.py:23
  492.2 8.9 %fusion.22 = f32[4,16,256]{2,1,0:T(8,128)} fusion(f32[4,16,256]{2,1,0:T(8,128)} %get-tuple-element.79, s32[]{:T(128)} %get-tuple-element.78, bf16[128,16,256]{0,1,2:T(8,128)(2,1)S(1)} %get-tuple-element.87, bf16[128,256,513]{0,2,1:T(8,128)(2,1)} %reshape.24), kind=kOutput, calls=%fused_computation.3.clone.1 | convolution fusion | flops 268435456 | bytes 17842688 | tf_op jit(solution)/shard_map/while/body/eval_jaxpr/spk,skt->pt/dot_general | solution.py:46
  501.2 6.2 %psum.15 = f32[]{:T(128)} all-reduce(f32[]{:T(128)} %get-tuple-element.45), channel_id=1, replica_groups=mesh['sens'=4,'par'=8] {'sens'}, use_global_device_ids=true, to_apply=%region_5.6 | all-reduce | flops 1 | bytes 8 | tf_op jit(solution)/shard_map/psum | solution.py:41
  508.0 12.0 %reduce-scatter.2.cloned.1.call-done = f32[1,16,256]{2,1,0:T(8,128)} async-done(((f32[4,16,256]{2,1,0:T(8,128)}), f32[1,16,256]{2,1,0:T(8,128)}) %reduce-scatter.2.cloned.1.call-update) | async-done | bytes 16400 | tf_op jit(solution)/shard_map/reduce_scatter | solution.py:49
  (17 shorter events, 0.1 us)
Async XLA Ops:
  7.2 160.1 %all-reduce.4.cloned.1.call-start = ((), (), s32[]{:S(2)}) async-start(), calls=%async_computation.1 | async-start | bytes 1048576 | tf_op jit(solution)/shard_map/psum | solution.py:37
  50.2 36.2 %copy-start = (bf16[128,16,256]{2,1,0:T(8,128)(2,1)S(1)}, bf16[128,16,256]{2,1,0:T(8,128)(2,1)}, u32[]{:S(2)}) copy-start(bf16[128,16,256]{2,1,0:T(8,128)(2,1)} %param.7) | copy-start | bytes 3145732
  86.4 8.4 %copy-start.1 = (f32[4,128,256]{2,1,0:T(8,128)S(1)}, f32[4,128,256]{2,1,0:T(8,128)}, u32[]{:S(2)}) copy-start(f32[4,128,256]{2,1,0:T(8,128)} %param.8) | copy-start | bytes 1572868
  86.4 80.9 %copy-start.2 = (f32[128]{0:T(128)S(1)}, f32[128]{0:T(128)}, u32[]{:S(2)}) copy-start(f32[128]{0:T(128)} %param.9) | copy-start | bytes 1540
  93.1 427.0 %reduce-scatter.2.cloned.1.call-start = ((), (), s32[]{:S(2)}) async-start(), calls=%async_computation.2 | async-start | bytes 81920 | tf_op jit(solution)/shard_map/reduce_scatter | solution.py:49
Sparse Core Ops, SparseCore 0:
  93.2 74.0 all-reduce.3
  501.3 18.6 reduce-scatter.1
where the time goes:
time: 532 us; the launch traced here: 528 us
  local copies, waits for them, and re-layouts  371 us (70%)
  waiting for transfers between devices  84.4 us (16%)
  matrix products  42.3 us (8%)
  between operations  15.9 us (3%)
  blocking collectives  12.6 us (2%)
    reshape x4, local copies, waits for them, and re-layouts, leading_rows(): flat[..., :length_steps * stride]  151 us
    slice x4, local copies, waits for them, and re-layouts, leading_rows(): flat[..., :length_steps * stride]  91.4 us
    psum x1, waiting for transfers between devices, local(): predicted = lax.psum(summed_terms, 'par')  72.3 us
    another operation x4, local copies, waits for them, and re-layouts, leading_rows(): flat = jnp.tile(padded, reps)  54.2 us
    reshape x1, local copies, waits for them, and re-layouts, causal_rows(): flat[..., :length_steps * stride]  36.2 us
    dot_general x4, matrix products, single_adjoint(): jnp.einsum('spk,skt->pt', kernel, shifted, preferred_element_type=jnp.flo...  35.6 us
    another operation x2, local copies, waits for them, and re-layouts, causal_rows(): flat = jnp.tile(padded, reps)  22.9 us
    slice x1, local copies, waits for them, and re-layouts, causal_rows(): flat[..., :length_steps * stride]  13.7 us
  transfers between devices with their start and end apart: 2, of which 2 were waited for; matrix products, arithmetic and copies ran while one was open for 0% of the time, Pallas kernels for 0%

commit v1 on v0

v1 whole, which is shorter than its diff:
```python
import functools

import jax
import jax.numpy as jnp
from jax import lax
from jax.experimental import pallas as pl
from jax.experimental.pallas import tpu as pltpu
from jax.sharding import PartitionSpec as P

EXTRA_ROWS = 16
MISFIT_ROWS = 8
VMEM_LIMIT = 24 * 1024 * 1024


def partners(size, step):
    return [(i, i ^ step) for i in range(size)]


def forward_body(vectors, lags, *refs):
    models, (x_ref, out_ref, ut_ref, u_ref, acc_ref) = refs[:vectors], refs[vectors:]
    steps, points, sensors = x_ref.shape
    lane = lax.broadcasted_iota(jnp.int32, (points, steps), 1)
    for v in range(vectors):
        series = models[v][0].astype(jnp.float32)
        for kl in range(lags):
            moved = series if kl == 0 else jnp.where(lane >= kl, pltpu.roll(series, kl, 1), 0.0)
            ut_ref[v, kl * points : (kl + 1) * points, :] = moved
        u_ref[v] = ut_ref[v].T.astype(jnp.bfloat16)
    for k0 in range(0, steps, 2 * lags):
        left = steps - k0
        pair = [x_ref[k : k + lags].reshape(lags * points, sensors) for k in (k0, k0 + lags)]
        rows = u_ref[:, :left, :].reshape(vectors * left, lags * points)
        term = jnp.dot(rows, jnp.concatenate(pair, axis=1), preferred_element_type=jnp.float32)
        term = term.reshape(vectors, left, 2 * sensors)
        if k0 == 0:
            acc_ref[...] = term[:, :, :sensors]
        else:
            acc_ref[:, k0:, :] += term[:, :, :sensors]
        acc_ref[:, k0 + lags :, :] += term[:, : left - lags, sensors:]
    out_ref[...] = acc_ref[...].astype(jnp.bfloat16)


def residual_body(terms_ref, observed_ref, weights_ref, out_ref):
    pieces, rows, sensors = terms_ref.shape
    predicted = terms_ref[0].astype(jnp.float32)
    for piece in range(1, pieces):
        predicted += terms_ref[piece].astype(jnp.float32)
    mismatch = predicted - observed_ref[...]
    weighted = weights_ref[...] * mismatch
    out_ref[:rows, :] = weighted.astype(jnp.bfloat16)
    squared = jnp.sum(weighted * mismatch, axis=0, keepdims=True)
    high = squared.astype(jnp.bfloat16).astype(jnp.float32)
    rest = squared - high
    middle = rest.astype(jnp.bfloat16).astype(jnp.float32)
    low = rest - middle
    row = lax.broadcasted_iota(jnp.int32, (EXTRA_ROWS, sensors), 0)
    parts = jnp.where(row == 0, high, jnp.where(row == 1, middle, jnp.where(row == 2, low, 0.0)))
    out_ref[rows:, :] = parts.astype(jnp.bfloat16)


def adjoint_body(vectors, lags, gathered_ref, x_ref, *refs):
    outs, (a_ref, r_ref) = refs[:vectors], refs[vectors:]
    steps, points, sensors = x_ref.shape
    pieces, rows = gathered_ref.shape[0], gathered_ref.shape[1] - EXTRA_ROWS
    blocks = steps // lags
    per_vector = steps // rows
    for d in range(lags):
        for c in range(blocks):
            a_ref[c * points : (c + 1) * points, d * sensors : (d + 1) * sensors] = x_ref[c * lags + d]
    extra = gathered_ref[0, rows:, :].astype(jnp.float32)
    for piece in range(1, pieces):
        extra += gathered_ref[piece, rows:, :].astype(jnp.float32)
    squared = jnp.sum(extra)
    lane = lax.broadcasted_iota(jnp.int32, (sensors, steps), 1)
    lane_p = lax.broadcasted_iota(jnp.int32, (points, steps), 1)
    for v in range(vectors):
        chunks = [gathered_ref[v * per_vector + i, :rows, :].astype(jnp.float32) for i in range(per_vector)]
        series = jnp.concatenate(chunks, axis=0).T
        for d in range(lags):
            moved = series
            if d > 0:
                moved = jnp.where(lane < steps - d, pltpu.roll(series, steps - d, 1), 0.0)
            r_ref[v, d * sensors : (d + 1) * sensors, :] = moved.astype(jnp.bfloat16)
        terms = jnp.dot(a_ref[...], r_ref[v], preferred_element_type=jnp.float32)
        total = terms[:points]
        for c in range(1, blocks):
            moved = pltpu.roll(terms[c * points : (c + 1) * points], steps - c * lags, 1)
            total += jnp.where(lane_p < steps - c * lags, moved, 0.0)
        outs[v][:points, :] = total
        outs[v][points:, :] = jnp.full((MISFIT_ROWS, steps), squared, jnp.float32)


def local(model, kernel, observed, weights):
    n_sens, n_par = lax.axis_size("sens"), lax.axis_size("par")
    me, j = lax.axis_index("sens"), lax.axis_index("par")
    sensors, points, steps = kernel.shape
    vectors = n_sens * model.shape[0]
    lags = 256 // points
    rows = vectors * steps // n_par
    vmem = pl.BlockSpec(memory_space=pltpu.VMEM)
    params = pltpu.CompilerParams(vmem_limit_bytes=VMEM_LIMIT)
    flops = 2 * vectors * sensors * points * steps * steps

    models = [model] + [lax.ppermute(model, "sens", partners(n_sens, step)) for step in range(1, n_sens)]
    x = jnp.transpose(kernel, (2, 1, 0))
    first = j * rows
    source = me ^ (first // steps)
    own = lax.dynamic_slice(observed, (source, 0, first % steps), (1, sensors, rows))
    own = own[0].T

    terms = pl.pallas_call(
        functools.partial(forward_body, vectors, lags),
        out_shape=jax.ShapeDtypeStruct((vectors, steps, sensors), jnp.bfloat16),
        in_specs=[vmem] * (vectors + 1),
        out_specs=vmem,
        scratch_shapes=[
            pltpu.VMEM((vectors, lags * points, steps), jnp.float32),
            pltpu.VMEM((vectors, steps, lags * points), jnp.bfloat16),
            pltpu.VMEM((vectors, steps, sensors), jnp.float32),
        ],
        compiler_params=params,
        cost_estimate=pl.CostEstimate(flops=flops, bytes_accessed=2 * kernel.size, transcendentals=0),
    )(*models, x)

    pieces = lax.all_to_all(terms.reshape(n_par, rows, sensors), "par", 0, 0)
    own_residual = pl.pallas_call(
        residual_body,
        out_shape=jax.ShapeDtypeStruct((rows + EXTRA_ROWS, sensors), jnp.bfloat16),
        in_specs=[vmem] * 3,
        out_specs=vmem,
        compiler_params=params,
    )(pieces, own, weights[None, :])
    gathered = lax.all_gather(own_residual, "par", axis=0)

    partials = pl.pallas_call(
        functools.partial(adjoint_body, vectors, lags),
        out_shape=[jax.ShapeDtypeStruct((points + MISFIT_ROWS, steps), jnp.float32)] * vectors,
        in_specs=[vmem] * 2,
        out_specs=[vmem] * vectors,
        scratch_shapes=[
            pltpu.VMEM((steps // lags * points, lags * sensors), jnp.bfloat16),
            pltpu.VMEM((vectors, lags * sensors, steps), jnp.bfloat16),
        ],
        compiler_params=params,
        cost_estimate=pl.CostEstimate(flops=flops, bytes_accessed=2 * kernel.size, transcendentals=0),
    )(gathered, x)
    total = partials[0]
    for step in range(1, n_sens):
        total += lax.ppermute(partials[step], "sens", partners(n_sens, step))
    entries = vectors * sensors * n_sens * steps
    misfit = total[points, 0] * (0.5 / entries)
    return (total[None, :points, :], misfit)


def solution(mesh):
    return jax.shard_map(
        local,
        mesh=mesh,
        in_specs=(P("sens", "par", None), P("sens", "par", None), P(None, "sens", None), P("sens")),
        out_specs=(P("sens", "par", None), P()),
        check_vma=False,
    )
```

time: 532 us -> 65.4 us (0.12)
  local copies, waits for them, and re-layouts: 371 us -> 4.35 us
  waiting for transfers between devices: 84.4 us -> 12.1 us
  matrix products: 42.3 us -> 0 us
  blocking collectives: 12.6 us -> 31.1 us
  between operations: 15.9 us -> 2.49 us
  starting transfers between devices: 0.08 us -> 10.9 us
    reshape x5 -> x0, local copies, waits for them, and re-layouts: 187 us -> none  [the longest x4 151 us: leading_rows(): flat[..., :length_steps * stride]]
    slice x5 -> x1, local copies, waits for them, and re-layouts: 105 us -> 0.51 us  [local(): misfit = total[points, 0] * (0.5 / entries)]
    another operation x6 -> x0, local copies, waits for them, and re-layouts: 77.1 us -> none  [the longest x4 54.2 us: leading_rows(): flat = jnp.tile(padded, reps)]
    psum x1 -> x0, waiting for transfers between devices: 72.3 us -> none  [local(): predicted = lax.psum(summed_terms, 'par')]
    dot_general x5 -> x0, matrix products: 42.3 us -> none  [the longest x4 35.6 us: single_adjoint(): jnp.einsum('spk,skt->pt', kernel, shifted, preferred_element_type=jnp.flo...]
    all_gather x1, blocking collectives: 6.39 us -> 31.1 us  [local(): gathered = lax.all_gather(own_residual, 'par', axis=0)]
    reduce_scatter x1 -> x0, waiting for transfers between devices: 12 us -> none  [local(): lax.psum_scatter(adjoint_pieces, 'sens', scatter_dimension=0, tiled=True)]
    all_to_all x0 -> x1, waiting for transfers between devices: none -> 9.13 us  [local(): pieces = lax.all_to_all(terms.reshape(n_par, rows, sensors), 'par', 0, 0)]
  transfers between devices with their start and end apart: 2 -> 7, of which waited for: 2 -> 4; matrix products, arithmetic and copies ran while one was open for 0% -> 4% of each run, Pallas kernels for 0% -> 0%
where the time goes in v1:
time: 65.4 us; the launch traced here: 65.1 us
  blocking collectives  31.1 us (48%)
  waiting for transfers between devices  12.1 us (19%)
  starting transfers between devices  10.9 us (17%)
  local copies, waits for them, and re-layouts  4.35 us (7%)
  Pallas kernels  4.15 us (6%)
  between operations  2.49 us (4%)
    all_gather x1, blocking collectives, local(): gathered = lax.all_gather(own_residual, 'par', axis=0)  31.1 us
    all_to_all x1, waiting for transfers between devices, local(): pieces = lax.all_to_all(terms.reshape(n_par, rows, sensors), 'par', 0, 0)  9.13 us
    all_to_all x1, starting transfers between devices, local(): pieces = lax.all_to_all(terms.reshape(n_par, rows, sensors), 'par', 0, 0)  5.84 us
    ppermute x3, starting transfers between devices, local(): lax.ppermute(model, 'sens', partners(n_sens, step))  3.15 us
    unnamed x7, local copies, waits for them, and re-layouts  3.13 us
    ppermute x3, waiting for transfers between devices, local(): total += lax.ppermute(partials[step], 'sens', partners(n_sens, step))  2.28 us
    pallas_call x1, Pallas kernels, local(): pl.pallas_call(functools.partial(adjoint_body, vectors, lags), out_shape=...  2.18 us
    ppermute x3, starting transfers between devices, local(): total += lax.ppermute(partials[step], 'sens', partners(n_sens, step))  1.92 us
  transfers between devices with their start and end apart: 7, of which 4 were waited for; matrix products, arithmetic and copies ran while one was open for 4% of the time, Pallas kernels for 0%

profile of v1, /device:TPU:0, one launch (start us, length us, event | category | flops | bytes accessed | tf_op | source)
XLA Modules:
  0.0 65.1 jit_solution(17399140398933779044)
XLA Ops:
  0.6 0.0 copy-start
  0.6 0.0 copy-start.2
  0.7 0.5 collective-permute-start
  1.2 2.6 %collective-permute-start.1 = (bf16[1,16,256]{2,1,0:T(8,128)(2,1)}, bf16[1,16,256]{2,1,0:T(8,128)(2,1)S(1)}, u32[]{:S(2)}, u32[]{:S(2)}) collective-permute-start(bf16[1,16,256]{2,1,0:T(8,128)(2,1)} %refs_0_.1), channel_id=1, source_target_pairs={{0,16},{8,24},{16,0},{24,8},{1,17},{9,25},{17,1},{25,9},{2,18},{10... | collective-permute-start | bytes 24584 | tf_op jit(solution)/shard_map/ppermute | solution.py:104
  3.7 0.1 collective-permute-start.2
  3.8 2.5 %copy.6 = bf16[128,16,256]{0,1,2:T(8,128)(2,1)S(1)} copy(bf16[128,16,256]{2,1,0:T(8,128)(2,1)} %param.5) | data formatting | bytes 2097152 | tf_op args[1]
  6.3 0.0 collective-permute-done.refs_1_
  6.3 0.0 collective-permute-done.1.refs_2_
  6.3 0.7 %collective-permute-done.2.refs_3_ = bf16[1,16,256]{2,1,0:T(8,128)(2,1)S(1)} collective-permute-done((bf16[1,16,256]{2,1,0:T(8,128)(2,1)}, bf16[1,16,256]{2,1,0:T(8,128)(2,1)S(1)}, u32[]{:S(2)}, u32[]{:S(2)}) %collective-permute-start.2) | collective-permute-done | bytes 8224 | tf_op jit(solution)/shard_map/ppermute | solution.py:104
  7.0 0.0 copy-done.2
  7.0 1.9 %shard_map.59 = bf16[4,256,128]{2,1,0:T(8,128)(2,1)} custom-call(bf16[1,16,256]{2,1,0:T(8,128)(2,1)S(1)} %copy-done.2, bf16[1,16,256]{2,1,0:T(8,128)(2,1)S(1)} %collective-permute-done.refs_1_, bf16[1,16,256]{2,1,0:T(8,128)(2,1)S(1)} %collective-permute-done.1.refs_2_, bf16[1,16,256]{2,1,0:T(8,128)(2,1)S(1)} %collective-permute-done.2.refs_3_, ...), custom_call_target="tpu_custom_call" | custom-call | flops 1073741824 | bytes 1048576 | tf_op jit(solution)/shard_map/pallas_call | solution.py:111
  8.9 5.8 %all-to-all-start = ((bf16[8,128,128]{2,1,0:T(8,128)(2,1)}), bf16[8,128,128]{2,1,0:T(8,128)(2,1)S(1)}, u32[]{:S(2)}, u32[]{:S(2)}) async-start(bf16[8,128,128]{2,1,0:T(8,128)(2,1)} %bitcast.1), calls=%async_computation | async-start | bytes 524288 | tf_op jit(solution)/shard_map/all_to_all | solution.py:125
  14.8 0.0 copy-done
  14.8 0.1 copy.7
  14.9 9.1 %all-to-all-done.terms_ref = bf16[8,128,128]{2,1,0:T(8,128)(2,1)S(1)} async-done(((bf16[8,128,128]{2,1,0:T(8,128)(2,1)}), bf16[8,128,128]{2,1,0:T(8,128)(2,1)S(1)}, u32[]{:S(2)}, u32[]{:S(2)}) %all-to-all-start) | async-done | bytes 262176 | tf_op jit(solution)/shard_map/all_to_all | solution.py:125
  24.0 0.0 copy-start.1
  24.0 0.7 %copy-done.1 = f32[128]{0:T(128)S(1)} copy-done((f32[128]{0:T(128)S(1)}, f32[128]{0:T(128)}, u32[]{:S(2)}) %copy-start.1) | copy-done | bytes 536
  24.7 0.1 shard_map.60
  24.7 31.1 %all-gather = bf16[1152,128]{1,0:T(8,128)(2,1)S(1)} all-gather(bf16[144,128]{1,0:T(8,128)(2,1)S(1)} %shard_map.60), channel_id=2, replica_groups=mesh['sens'=4,'par'=8] {'par'}, dimensions={0}, use_global_device_ids=true | all-gather | bytes 331776 | tf_op jit(solution)/shard_map/all_gather | solution.py:133
  55.8 2.2 %shard_map.61 = (f32[24,256]{1,0:T(8,128)S(1)}, f32[24,256]{1,0:T(8,128)S(1)}, f32[24,256]{1,0:T(8,128)S(1)}, f32[24,256]{1,0:T(8,128)S(1)}) custom-call(bf16[8,144,128]{2,1,0:T(8,128)(2,1)S(1)} %bitcast.12, bf16[256,16,128]{2,1,0:T(8,128)(2,1)S(1)} %bitcast.11), custom_call_target="tpu_custom_call" | custom-call | flops 1073741824 | bytes 1048576 | tf_op jit(solution)/shard_map/pallas_call | solution.py:135
  58.0 0.1 collective-permute-start.5
  58.1 1.0 %collective-permute-start.4 = (f32[24,256]{1,0:T(8,128)S(1)}, f32[24,256]{1,0:T(8,128)S(1)}, u32[]{:S(2)}, u32[]{:S(2)}) collective-permute-start(f32[24,256]{1,0:T(8,128)S(1)} %get-tuple-element.8), channel_id=1, source_target_pairs={{0,16},{8,24},{16,0},{24,8},{1,17},{9,25},{17,1},{25,9},{2,18},{10... | collective-permute-start | bytes 73736 | tf_op jit(solution)/shard_map/ppermute | solution.py:149
  59.1 0.9 %collective-permute-start.3 = (f32[24,256]{1,0:T(8,128)S(1)}, f32[24,256]{1,0:T(8,128)S(1)}, u32[]{:S(2)}, u32[]{:S(2)}) collective-permute-start(f32[24,256]{1,0:T(8,128)S(1)} %get-tuple-element.7), channel_id=1, source_target_pairs={{0,8},{8,0},{16,24},{24,16},{1,9},{9,1},{17,25},{25,17},{2,10},{10... | collective-permute-start | bytes 73736 | tf_op jit(solution)/shard_map/ppermute | solution.py:149
  59.9 1.4 %collective-permute-done.5 = f32[24,256]{1,0:T(8,128)S(1)} collective-permute-done((f32[24,256]{1,0:T(8,128)S(1)}, f32[24,256]{1,0:T(8,128)S(1)}, u32[]{:S(2)}, u32[]{:S(2)}) %collective-permute-start.5) | collective-permute-done | bytes 24608 | tf_op jit(solution)/shard_map/ppermute | solution.py:149
  61.3 0.9 %collective-permute-done.4 = f32[24,256]{1,0:T(8,128)S(1)} collective-permute-done((f32[24,256]{1,0:T(8,128)S(1)}, f32[24,256]{1,0:T(8,128)S(1)}, u32[]{:S(2)}, u32[]{:S(2)}) %collective-permute-start.4) | collective-permute-done | bytes 24608 | tf_op jit(solution)/shard_map/ppermute | solution.py:149
  62.2 0.0 collective-permute-done.3
  62.2 0.6 slice_bitcast_fusion
  62.8 0.5 slice.9
  (2 shorter events, 0.0 us)
Async XLA Ops:
  0.6 14.1 %copy-start = (f32[4,128,256]{2,1,0:T(8,128)S(1)}, f32[4,128,256]{2,1,0:T(8,128)}, u32[]{:S(2)}) copy-start(f32[4,128,256]{2,1,0:T(8,128)} %param.6) | copy-start | bytes 1572868
  0.6 6.4 %copy-start.2 = (bf16[1,16,256]{2,1,0:T(8,128)(2,1)S(1)}, bf16[1,16,256]{2,1,0:T(8,128)(2,1)}, u32[]{:S(2)}) copy-start(bf16[1,16,256]{2,1,0:T(8,128)(2,1)} %refs_0_.1) | copy-start | bytes 24580
  0.7 5.6 %collective-permute-start = (bf16[1,16,256]{2,1,0:T(8,128)(2,1)}, bf16[1,16,256]{2,1,0:T(8,128)(2,1)S(1)}, u32[]{:S(2)}, u32[]{:S(2)}) collective-permute-start(bf16[1,16,256]{2,1,0:T(8,128)(2,1)} %refs_0_.1), channel_id=1, source_target_pairs={{0,8},{8,0},{16,24},{24,16},{1,9},{9,1},{17,25},{25,17},{2,10},{10... | collective-permute-start | bytes 24584 | tf_op jit(solution)/shard_map/ppermute | solution.py:104
  1.2 5.1 %collective-permute-start.1 = (bf16[1,16,256]{2,1,0:T(8,128)(2,1)}, bf16[1,16,256]{2,1,0:T(8,128)(2,1)S(1)}, u32[]{:S(2)}, u32[]{:S(2)}) collective-permute-start(bf16[1,16,256]{2,1,0:T(8,128)(2,1)} %refs_0_.1), channel_id=1, source_target_pairs={{0,16},{8,24},{16,0},{24,8},{1,17},{9,25},{17,1},{25,9},{2,18},{10... | collective-permute-start | bytes 24584 | tf_op jit(solution)/shard_map/ppermute | solution.py:104
  3.7 3.3 %collective-permute-start.2 = (bf16[1,16,256]{2,1,0:T(8,128)(2,1)}, bf16[1,16,256]{2,1,0:T(8,128)(2,1)S(1)}, u32[]{:S(2)}, u32[]{:S(2)}) collective-permute-start(bf16[1,16,256]{2,1,0:T(8,128)(2,1)} %refs_0_.1), channel_id=1, source_target_pairs={{0,24},{8,16},{16,8},{24,0},{1,25},{9,17},{17,9},{25,1},{2,26},{10... | collective-permute-start | bytes 24584 | tf_op jit(solution)/shard_map/ppermute | solution.py:104
  8.9 15.1 %all-to-all-start = ((bf16[8,128,128]{2,1,0:T(8,128)(2,1)}), bf16[8,128,128]{2,1,0:T(8,128)(2,1)S(1)}, u32[]{:S(2)}, u32[]{:S(2)}) async-start(bf16[8,128,128]{2,1,0:T(8,128)(2,1)} %bitcast.1), calls=%async_computation | async-start | bytes 524288 | tf_op jit(solution)/shard_map/all_to_all | solution.py:125
  24.0 0.7 %copy-start.1 = (f32[128]{0:T(128)S(1)}, f32[128]{0:T(128)}, u32[]{:S(2)}) copy-start(f32[128]{0:T(128)} %param.7) | copy-start | bytes 1540
  58.0 3.3 %collective-permute-start.5 = (f32[24,256]{1,0:T(8,128)S(1)}, f32[24,256]{1,0:T(8,128)S(1)}, u32[]{:S(2)}, u32[]{:S(2)}) collective-permute-start(f32[24,256]{1,0:T(8,128)S(1)} %get-tuple-element.9), channel_id=1, source_target_pairs={{0,24},{8,16},{16,8},{24,0},{1,25},{9,17},{17,9},{25,1},{2,26},{10... | collective-permute-start | bytes 73736 | tf_op jit(solution)/shard_map/ppermute | solution.py:149
  58.1 4.1 %collective-permute-start.4 = (f32[24,256]{1,0:T(8,128)S(1)}, f32[24,256]{1,0:T(8,128)S(1)}, u32[]{:S(2)}, u32[]{:S(2)}) collective-permute-start(f32[24,256]{1,0:T(8,128)S(1)} %get-tuple-element.8), channel_id=1, source_target_pairs={{0,16},{8,24},{16,0},{24,8},{1,17},{9,25},{17,1},{25,9},{2,18},{10... | collective-permute-start | bytes 73736 | tf_op jit(solution)/shard_map/ppermute | solution.py:149
  59.1 3.2 %collective-permute-start.3 = (f32[24,256]{1,0:T(8,128)S(1)}, f32[24,256]{1,0:T(8,128)S(1)}, u32[]{:S(2)}, u32[]{:S(2)}) collective-permute-start(f32[24,256]{1,0:T(8,128)S(1)} %get-tuple-element.7), channel_id=1, source_target_pairs={{0,8},{8,0},{16,24},{24,16},{1,9},{9,1},{17,25},{25,17},{2,10},{10... | collective-permute-start | bytes 73736 | tf_op jit(solution)/shard_map/ppermute | solution.py:149

commit v2 on v1

v2 whole, which is shorter than its diff:
```python
import functools

import jax
import jax.numpy as jnp
from jax import lax
from jax.experimental import pallas as pl
from jax.experimental.pallas import tpu as pltpu
from jax.sharding import PartitionSpec as P

EXTRA_ROWS = 16
WEIGHT_ROWS = 8
MISFIT_ROWS = 8
VMEM_LIMIT = 24 * 1024 * 1024


def swap(value, axis, step):
    return lax.ppermute(value, axis, [(i, i ^ step) for i in range(lax.axis_size(axis))])


def forward_body(vectors, pieces, lags, *refs):
    models, refs = refs[:vectors], refs[vectors:]
    x_ref, observed_ref, weights_ref, own_ref = refs[:4]
    sent, refs = refs[4 : 3 + pieces], refs[3 + pieces :]
    ut_ref, u_ref, acc_ref, seen_ref, scale_ref, sems = refs
    steps, points, sensors = x_ref.shape
    rows = vectors * steps // pieces
    me, j = lax.axis_index("sens"), lax.axis_index("par")
    first = j * rows
    fetch_seen = pltpu.make_async_copy(observed_ref.at[me ^ (first // steps)], seen_ref, sems.at[0])
    fetch_scale = pltpu.make_async_copy(weights_ref, scale_ref, sems.at[1])
    fetch_seen.start()
    fetch_scale.start()
    lane = lax.broadcasted_iota(jnp.int32, (points, steps), 1)
    for v in range(vectors):
        series = models[v][0].astype(jnp.float32)
        for kl in range(lags):
            moved = series if kl == 0 else jnp.where(lane >= kl, pltpu.roll(series, kl, 1), 0.0)
            ut_ref[v, kl * points : (kl + 1) * points, :] = moved
        u_ref[v] = ut_ref[v].T.astype(jnp.bfloat16)
    for k0 in range(0, steps, 2 * lags):
        left = steps - k0
        pair = [x_ref[k : k + lags].reshape(lags * points, sensors) for k in (k0, k0 + lags)]
        some = u_ref[:, :left, :].reshape(vectors * left, lags * points)
        term = jnp.dot(some, jnp.concatenate(pair, axis=1), preferred_element_type=jnp.float32)
        for v in range(vectors):
            at, end = v * steps, (v + 1) * steps
            part = term[v * left : (v + 1) * left]
            if k0 == 0:
                acc_ref[at:end, :] = part[:, :sensors]
            else:
                acc_ref[at + k0 : end, :] += part[:, :sensors]
            acc_ref[at + k0 + lags : end, :] += part[: left - lags, sensors:]
    for step in range(1, pieces):
        there = pl.multiple_of((j ^ step) * rows, rows)
        sent[step - 1][...] = acc_ref[pl.ds(there, rows), :].astype(jnp.bfloat16)
    fetch_seen.wait()
    fetch_scale.wait()
    ut_ref[0, :, :sensors] = seen_ref[...].T
    here = pl.multiple_of(first, rows)
    seen = ut_ref[0, pl.ds(pl.multiple_of(first % steps, rows), rows), :sensors]
    own_ref[:rows, :] = acc_ref[pl.ds(here, rows), :] - seen
    own_ref[rows:, :] = jnp.broadcast_to(scale_ref[...], (WEIGHT_ROWS, sensors))


def residual_body(own_ref, *refs):
    terms, out_ref = refs[:-1], refs[-1]
    rows, sensors = terms[0].shape
    mismatch = own_ref[:rows, :]
    for term in terms:
        mismatch += term[...].astype(jnp.float32)
    weighted = own_ref[rows : rows + 1, :] * mismatch
    out_ref[:rows, :] = weighted.astype(jnp.bfloat16)
    squared = jnp.sum(weighted * mismatch, axis=0, keepdims=True)
    high = squared.astype(jnp.bfloat16).astype(jnp.float32)
    rest = squared - high
    middle = rest.astype(jnp.bfloat16).astype(jnp.float32)
    low = rest - middle
    row = lax.broadcasted_iota(jnp.int32, (EXTRA_ROWS, sensors), 0)
    parts = jnp.where(row == 0, high, jnp.where(row == 1, middle, jnp.where(row == 2, low, 0.0)))
    out_ref[rows:, :] = parts.astype(jnp.bfloat16)


def adjoint_body(vectors, pieces, lags, *refs):
    gathered, x_ref = refs[:pieces], refs[pieces]
    outs, (a_ref, r_ref, all_ref) = refs[pieces + 1 : pieces + 1 + vectors], refs[pieces + 1 + vectors :]
    steps, points, sensors = x_ref.shape
    rows = vectors * steps // pieces
    blocks = steps // lags
    j = lax.axis_index("par")
    for d in range(lags):
        for c in range(blocks):
            a_ref[c * points : (c + 1) * points, d * sensors : (d + 1) * sensors] = x_ref[c * lags + d]
    extra = jnp.zeros((EXTRA_ROWS, sensors), jnp.float32)
    for step in range(pieces):
        there = pl.multiple_of((j ^ step) * rows, rows)
        all_ref[pl.ds(there, rows), :] = gathered[step][:rows, :].astype(jnp.float32)
        extra += gathered[step][rows:, :].astype(jnp.float32)
    squared = jnp.sum(extra)
    lane = lax.broadcasted_iota(jnp.int32, (sensors, steps), 1)
    lane_p = lax.broadcasted_iota(jnp.int32, (points, steps), 1)
    for v in range(vectors):
        series = all_ref[v * steps : (v + 1) * steps, :].T
        for d in range(lags):
            moved = series
            if d > 0:
                moved = jnp.where(lane < steps - d, pltpu.roll(series, steps - d, 1), 0.0)
            r_ref[v, d * sensors : (d + 1) * sensors, :] = moved.astype(jnp.bfloat16)
        terms = jnp.dot(a_ref[...], r_ref[v], preferred_element_type=jnp.float32)
        total = terms[:points]
        for c in range(1, blocks):
            moved = pltpu.roll(terms[c * points : (c + 1) * points], steps - c * lags, 1)
            total += jnp.where(lane_p < steps - c * lags, moved, 0.0)
        outs[v][:points, :] = total
        outs[v][points:, :] = jnp.full((MISFIT_ROWS, steps), squared, jnp.float32)


def total_body(scale, *refs):
    terms, (gradient_ref, misfit_ref) = refs[:-2], refs[-2:]
    points = gradient_ref.shape[1]
    total = terms[0][...]
    for term in terms[1:]:
        total += term[...]
    gradient_ref[0] = total[:points]
    misfit_ref[...] = total[points : points + 1, :1] * scale


def local(model, kernel, observed, weights):
    n_sens, n_par = lax.axis_size("sens"), lax.axis_size("par")
    sensors, points, steps = kernel.shape
    vectors = n_sens * model.shape[0]
    lags = 256 // points
    rows = vectors * steps // n_par
    vmem = pl.BlockSpec(memory_space=pltpu.VMEM)
    anywhere = pl.BlockSpec(memory_space=pl.ANY)
    params = pltpu.CompilerParams(vmem_limit_bytes=VMEM_LIMIT)
    flops = 2 * vectors * sensors * points * steps * steps
    cost = pl.CostEstimate(flops=flops, bytes_accessed=2 * kernel.size, transcendentals=0)

    models = [model] + [swap(model, "sens", step) for step in range(1, n_sens)]
    x = jnp.transpose(kernel, (2, 1, 0))

    piece = jax.ShapeDtypeStruct((rows, sensors), jnp.bfloat16)
    own, *sent = pl.pallas_call(
        functools.partial(forward_body, vectors, n_par, lags),
        out_shape=[jax.ShapeDtypeStruct((rows + WEIGHT_ROWS, sensors), jnp.float32)] + [piece] * (n_par - 1),
        in_specs=[vmem] * (vectors + 1) + [anywhere] * 2,
        out_specs=[vmem] * n_par,
        scratch_shapes=[
            pltpu.VMEM((vectors, lags * points, steps), jnp.float32),
            pltpu.VMEM((vectors, steps, lags * points), jnp.bfloat16),
            pltpu.VMEM((vectors * steps, sensors), jnp.float32),
            pltpu.VMEM((sensors, steps), jnp.float32),
            pltpu.VMEM((1, sensors), jnp.float32),
            pltpu.SemaphoreType.DMA((2,)),
        ],
        compiler_params=params,
        cost_estimate=cost,
    )(*models, x, observed, weights[None, :])

    terms = [swap(sent[step - 1], "par", step) for step in range(n_par - 1, 0, -1)]
    residual = pl.pallas_call(
        residual_body,
        out_shape=jax.ShapeDtypeStruct((rows + EXTRA_ROWS, sensors), jnp.bfloat16),
        in_specs=[vmem] * n_par,
        out_specs=vmem,
        compiler_params=params,
    )(own, *terms)
    gathered = [swap(residual, "par", step) for step in range(n_par - 1, 0, -1)]

    partials = pl.pallas_call(
        functools.partial(adjoint_body, vectors, n_par, lags),
        out_shape=[jax.ShapeDtypeStruct((points + MISFIT_ROWS, steps), jnp.float32)] * vectors,
        in_specs=[vmem] * (n_par + 1),
        out_specs=[vmem] * vectors,
        scratch_shapes=[
            pltpu.VMEM((steps // lags * points, lags * sensors), jnp.bfloat16),
            pltpu.VMEM((vectors, lags * sensors, steps), jnp.bfloat16),
            pltpu.VMEM((vectors * steps, sensors), jnp.float32),
        ],
        compiler_params=params,
        cost_estimate=cost,
    )(residual, *gathered[::-1], x)

    received = [swap(partials[step], "sens", step) for step in range(n_sens - 1, 0, -1)]
    entries = vectors * sensors * n_sens * steps
    gradient, misfit = pl.pallas_call(
        functools.partial(total_body, 0.5 / entries),
        out_shape=[
            jax.ShapeDtypeStruct((1, points, steps), jnp.float32),
            jax.ShapeDtypeStruct((1, 1), jnp.float32),
        ],
        in_specs=[vmem] * n_sens,
        out_specs=[vmem] * 2,
    )(partials[0], *received)
    return (gradient, misfit[0, 0])


def solution(mesh):
    return jax.shard_map(
        local,
        mesh=mesh,
        in_specs=(P("sens", "par", None), P("sens", "par", None), P(None, "sens", None), P("sens")),
        out_specs=(P("sens", "par", None), P()),
        check_vma=False,
    )
```

time: 65.4 us -> 46.4 us (0.71)
  blocking collectives: 31.1 us -> 0 us
  starting transfers between devices: 10.9 us -> 27.5 us
  waiting for transfers between devices: 12.1 us -> 8.45 us
  between operations: 2.49 us -> 0.72 us
  Pallas kernels: 4.15 us -> 5.2 us
    all_gather x1 -> x0, blocking collectives: 31.1 us -> none  [local(): gathered = lax.all_gather(own_residual, 'par', axis=0)]
    ppermute x6 -> x20, starting transfers between devices: 5.07 us -> 27.5 us  [swap(): lax.ppermute(value, axis, [(i, i ^ step) for i in range(lax.axis_size(axi...]
    all_to_all x1 -> x0, waiting for transfers between devices: 9.13 us -> none  [local(): pieces = lax.all_to_all(terms.reshape(n_par, rows, sensors), 'par', 0, 0)]
    all_to_all x1 -> x0, starting transfers between devices: 5.84 us -> none  [local(): pieces = lax.all_to_all(terms.reshape(n_par, rows, sensors), 'par', 0, 0)]
    ppermute x6 -> x20, waiting for transfers between devices: 3.02 us -> 8.45 us  [swap(): lax.ppermute(value, axis, [(i, i ^ step) for i in range(lax.axis_size(axi...]
    unnamed x7 -> x15, local copies, waits for them, and re-layouts: 3.13 us -> 4.32 us
    pallas_call x2 -> x3, Pallas kernels: 4.08 us -> 5.15 us  [the longest x1 2.23 us: local(): pl.pallas_call(functools.partial(adjoint_body, vectors, n_par, lags), out...]
  transfers between devices with their start and end apart: 7 -> 20, of which waited for: 4 -> 10; matrix products, arithmetic and copies ran while one was open for 4% -> 5% of each run, Pallas kernels for 0% -> 0%
where the time goes in v2:
time: 46.4 us; the launch traced here: 46.2 us
  starting transfers between devices  27.5 us (59%)
  waiting for transfers between devices  8.45 us (18%)
  Pallas kernels  5.2 us (11%)
  local copies, waits for them, and re-layouts  4.32 us (9%)
  between operations  0.72 us (2%)
    ppermute x20, starting transfers between devices, swap(): lax.ppermute(value, axis, [(i, i ^ step) for i in range(lax.axis_size(axi...  27.5 us
    ppermute x20, waiting for transfers between devices, swap(): lax.ppermute(value, axis, [(i, i ^ step) for i in range(lax.axis_size(axi...  8.45 us
    unnamed x15, local copies, waits for them, and re-layouts  4.32 us
    pallas_call x1, Pallas kernels, local(): pl.pallas_call(functools.partial(adjoint_body, vectors, n_par, lags), out...  2.23 us
    pallas_call x1, Pallas kernels, local(): pl.pallas_call(functools.partial(forward_body, vectors, n_par, lags), out...  1.52 us
    pallas_call x1, Pallas kernels, local(): pl.pallas_call(functools.partial(total_body, 0.5 / entries), out_shape=[j...  1.4 us
  transfers between devices with their start and end apart: 20, of which 10 were waited for; matrix products, arithmetic and copies ran while one was open for 5% of the time, Pallas kernels for 0%

profile of v2, /device:TPU:0, one launch (start us, length us, event | category | flops | bytes accessed | tf_op | source)
XLA Modules:
  0.0 46.2 jit_solution(16769827621590790810)
XLA Ops:
  0.6 3.0 %collective-permute-start.1 = (bf16[1,16,256]{2,1,0:T(8,128)(2,1)}, bf16[1,16,256]{2,1,0:T(8,128)(2,1)S(1)}, u32[]{:S(2)}, u32[]{:S(2)}) collective-permute-start(bf16[1,16,256]{2,1,0:T(8,128)(2,1)} %refs_0_.1), channel_id=1, source_target_pairs={{0,16},{8,24},{16,0},{24,8},{1,17},{9,25},{17,1},{25,9},{2,18},{10... | collective-permute-start | bytes 24584 | tf_op jit(solution)/shard_map/ppermute | solution.py:17
  3.9 2.5 %copy.6 = bf16[128,16,256]{0,1,2:T(8,128)(2,1)S(1)} copy(bf16[128,16,256]{2,1,0:T(8,128)(2,1)} %param.5) | data formatting | bytes 2097152 | tf_op args[1]
  6.3 0.6 %collective-permute-done.2.refs_3_ = bf16[1,16,256]{2,1,0:T(8,128)(2,1)S(1)} collective-permute-done((bf16[1,16,256]{2,1,0:T(8,128)(2,1)}, bf16[1,16,256]{2,1,0:T(8,128)(2,1)S(1)}, u32[]{:S(2)}, u32[]{:S(2)}) %collective-permute-start.2) | collective-permute-done | bytes 8224 | tf_op jit(solution)/shard_map/ppermute | solution.py:17
  7.0 0.6 %copy-done.3 = f32[128]{0:T(128)S(1)} copy-done((f32[128]{0:T(128)S(1)}, f32[128]{0:T(128)}, u32[]{:S(2)}) %copy-start.3) | copy-done | bytes 536
  7.6 1.5 %shard_map.59 = (f32[136,128]{1,0:T(8,128)S(1)}, bf16[128,128]{1,0:T(8,128)(2,1)S(1)}, bf16[128,128]{1,0:T(8,128)(2,1)S(1)}, bf16[128,128]{1,0:T(8,128)(2,1)S(1)...) custom-call(bf16[1,16,256]{2,1,0:T(8,128)(2,1)S(1)} %copy-done.2, ...), custom_call_target="tpu_custom_call" | custom-call | flops 1073741824 | bytes 1048576 | tf_op jit(solution)/shard_map/pallas_call | solution.py:143
  9.1 4.6 %collective-permute-start.3 = (bf16[128,128]{1,0:T(8,128)(2,1)S(1)}, bf16[128,128]{1,0:T(8,128)(2,1)S(1)}, u32[]{:S(2)}, u32[]{:S(2)}) collective-permute-start(bf16[128,128]{1,0:T(8,128)(2,1)S(1)} %get-tuple-element.17), channel_id=1, source_target_pairs={{0,7},{1,6},{2,5},{3,4},{4,3},{5,2},{6,1},{7,0},{8,15},{9,14},{10,... | collective-permute-start | bytes 98312 | tf_op jit(solution)/shard_map/ppermute | solution.py:17
  14.0 0.7 %collective-permute-start.5 = (bf16[128,128]{1,0:T(8,128)(2,1)S(1)}, bf16[128,128]{1,0:T(8,128)(2,1)S(1)}, u32[]{:S(2)}, u32[]{:S(2)}) collective-permute-start(bf16[128,128]{1,0:T(8,128)(2,1)S(1)} %get-tuple-element.19), channel_id=1, source_target_pairs={{0,5},{1,4},{2,7},{3,6},{4,1},{5,0},{6,3},{7,2},{8,13},{9,12},{10,... | collective-permute-start | bytes 98312 | tf_op jit(solution)/shard_map/ppermute | solution.py:17
  14.7 2.1 %collective-permute-start.6 = (bf16[128,128]{1,0:T(8,128)(2,1)S(1)}, bf16[128,128]{1,0:T(8,128)(2,1)S(1)}, u32[]{:S(2)}, u32[]{:S(2)}) collective-permute-start(bf16[128,128]{1,0:T(8,128)(2,1)S(1)} %get-tuple-element.20), channel_id=1, source_target_pairs={{0,4},{1,5},{2,6},{3,7},{4,0},{5,1},{6,2},{7,3},{8,12},{9,13},{10,... | collective-permute-start | bytes 98312 | tf_op jit(solution)/shard_map/ppermute | solution.py:17
  16.8 2.2 %collective-permute-start.7 = (bf16[128,128]{1,0:T(8,128)(2,1)S(1)}, bf16[128,128]{1,0:T(8,128)(2,1)S(1)}, u32[]{:S(2)}, u32[]{:S(2)}) collective-permute-start(bf16[128,128]{1,0:T(8,128)(2,1)S(1)} %get-tuple-element.21), channel_id=1, source_target_pairs={{0,3},{1,2},{2,1},{3,0},{4,7},{5,6},{6,5},{7,4},{8,11},{9,10},{10,... | collective-permute-start | bytes 98312 | tf_op jit(solution)/shard_map/ppermute | solution.py:17
  19.0 0.8 %collective-permute-start.8 = (bf16[128,128]{1,0:T(8,128)(2,1)S(1)}, bf16[128,128]{1,0:T(8,128)(2,1)S(1)}, u32[]{:S(2)}, u32[]{:S(2)}) collective-permute-start(bf16[128,128]{1,0:T(8,128)(2,1)S(1)} %get-tuple-element.22), channel_id=1, source_target_pairs={{0,2},{1,3},{2,0},{3,1},{4,6},{5,7},{6,4},{7,5},{8,10},{9,11},{10,... | collective-permute-start | bytes 98312 | tf_op jit(solution)/shard_map/ppermute | solution.py:17
  19.8 0.5 %collective-permute-start.9 = (bf16[128,128]{1,0:T(8,128)(2,1)S(1)}, bf16[128,128]{1,0:T(8,128)(2,1)S(1)}, u32[]{:S(2)}, u32[]{:S(2)}) collective-permute-start(bf16[128,128]{1,0:T(8,128)(2,1)S(1)} %get-tuple-element.23), channel_id=1, source_target_pairs={{0,1},{1,0},{2,3},{3,2},{4,5},{5,4},{6,7},{7,6},{8,9},{9,8},{10,11... | collective-permute-start | bytes 98312 | tf_op jit(solution)/shard_map/ppermute | solution.py:17
  20.3 0.2 collective-permute-done.5.refs_2_
  20.6 1.4 %collective-permute-done.7.refs_4_ = bf16[128,128]{1,0:T(8,128)(2,1)S(1)} collective-permute-done((bf16[128,128]{1,0:T(8,128)(2,1)S(1)}, bf16[128,128]{1,0:T(8,128)(2,1)S(1)}, u32[]{:S(2)}, u32[]{:S(2)}) %collective-permute-start.7) | collective-permute-done | bytes 32800 | tf_op jit(solution)/shard_map/ppermute | solution.py:17
  22.0 1.0 %collective-permute-done.8.refs_5_ = bf16[128,128]{1,0:T(8,128)(2,1)S(1)} collective-permute-done((bf16[128,128]{1,0:T(8,128)(2,1)S(1)}, bf16[128,128]{1,0:T(8,128)(2,1)S(1)}, u32[]{:S(2)}, u32[]{:S(2)}) %collective-permute-start.8) | collective-permute-done | bytes 32800 | tf_op jit(solution)/shard_map/ppermute | solution.py:17
  23.0 0.8 %collective-permute-done.9.refs_6_ = bf16[128,128]{1,0:T(8,128)(2,1)S(1)} collective-permute-done((bf16[128,128]{1,0:T(8,128)(2,1)S(1)}, bf16[128,128]{1,0:T(8,128)(2,1)S(1)}, u32[]{:S(2)}, u32[]{:S(2)}) %collective-permute-start.9) | collective-permute-done | bytes 32800 | tf_op jit(solution)/shard_map/ppermute | solution.py:17
  23.8 3.6 %collective-permute-start.16 = (bf16[144,128]{1,0:T(8,128)(2,1)S(1)}, bf16[144,128]{1,0:T(8,128)(2,1)S(1)}, u32[]{:S(2)}, u32[]{:S(2)}) collective-permute-start(bf16[144,128]{1,0:T(8,128)(2,1)S(1)} %shard_map.60.refs_0_), channel_id=1, source_target_pairs={{0,7},{1,6},{2,5},{3,4},{4,3},{5,2},{6,1},{7,0},{8,15},{9,14},{10,... | collective-permute-start | bytes 110600 | tf_op jit(solution)/shard_map/ppermute | solution.py:17
  27.6 1.4 %collective-permute-start.14 = (bf16[144,128]{1,0:T(8,128)(2,1)S(1)}, bf16[144,128]{1,0:T(8,128)(2,1)S(1)}, u32[]{:S(2)}, u32[]{:S(2)}) collective-permute-start(bf16[144,128]{1,0:T(8,128)(2,1)S(1)} %shard_map.60.refs_0_), channel_id=1, source_target_pairs={{0,5},{1,4},{2,7},{3,6},{4,1},{5,0},{6,3},{7,2},{8,13},{9,12},{10,... | collective-permute-start | bytes 110600 | tf_op jit(solution)/shard_map/ppermute | solution.py:17
  29.0 2.5 %collective-permute-start.13 = (bf16[144,128]{1,0:T(8,128)(2,1)S(1)}, bf16[144,128]{1,0:T(8,128)(2,1)S(1)}, u32[]{:S(2)}, u32[]{:S(2)}) collective-permute-start(bf16[144,128]{1,0:T(8,128)(2,1)S(1)} %shard_map.60.refs_0_), channel_id=1, source_target_pairs={{0,4},{1,5},{2,6},{3,7},{4,0},{5,1},{6,2},{7,3},{8,12},{9,13},{10,... | collective-permute-start | bytes 110600 | tf_op jit(solution)/shard_map/ppermute | solution.py:17
  31.5 1.2 %collective-permute-start.12 = (bf16[144,128]{1,0:T(8,128)(2,1)S(1)}, bf16[144,128]{1,0:T(8,128)(2,1)S(1)}, u32[]{:S(2)}, u32[]{:S(2)}) collective-permute-start(bf16[144,128]{1,0:T(8,128)(2,1)S(1)} %shard_map.60.refs_0_), channel_id=1, source_target_pairs={{0,3},{1,2},{2,1},{3,0},{4,7},{5,6},{6,5},{7,4},{8,11},{9,10},{10,... | collective-permute-start | bytes 110600 | tf_op jit(solution)/shard_map/ppermute | solution.py:17
  32.8 0.7 %collective-permute-start.11 = (bf16[144,128]{1,0:T(8,128)(2,1)S(1)}, bf16[144,128]{1,0:T(8,128)(2,1)S(1)}, u32[]{:S(2)}, u32[]{:S(2)}) collective-permute-start(bf16[144,128]{1,0:T(8,128)(2,1)S(1)} %shard_map.60.refs_0_), channel_id=1, source_target_pairs={{0,2},{1,3},{2,0},{3,1},{4,6},{5,7},{6,4},{7,5},{8,10},{9,11},{10,... | collective-permute-start | bytes 110600 | tf_op jit(solution)/shard_map/ppermute | solution.py:17
  33.5 1.5 %collective-permute-start.10 = (bf16[144,128]{1,0:T(8,128)(2,1)S(1)}, bf16[144,128]{1,0:T(8,128)(2,1)S(1)}, u32[]{:S(2)}, u32[]{:S(2)}) collective-permute-start(bf16[144,128]{1,0:T(8,128)(2,1)S(1)} %shard_map.60.refs_0_), channel_id=1, source_target_pairs={{0,1},{1,0},{2,3},{3,2},{4,5},{5,4},{6,7},{7,6},{8,9},{9,8},{10,11... | collective-permute-start | bytes 110600 | tf_op jit(solution)/shard_map/ppermute | solution.py:17
  35.0 1.4 %collective-permute-done.12.refs_3_ = bf16[144,128]{1,0:T(8,128)(2,1)S(1)} collective-permute-done((bf16[144,128]{1,0:T(8,128)(2,1)S(1)}, bf16[144,128]{1,0:T(8,128)(2,1)S(1)}, u32[]{:S(2)}, u32[]{:S(2)}) %collective-permute-start.12) | collective-permute-done | bytes 36896 | tf_op jit(solution)/shard_map/ppermute | solution.py:17
  36.4 0.3 collective-permute-done.11.refs_2_
  36.7 0.7 %collective-permute-done.10.refs_1_ = bf16[144,128]{1,0:T(8,128)(2,1)S(1)} collective-permute-done((bf16[144,128]{1,0:T(8,128)(2,1)S(1)}, bf16[144,128]{1,0:T(8,128)(2,1)S(1)}, u32[]{:S(2)}, u32[]{:S(2)}) %collective-permute-start.10) | collective-permute-done | bytes 36896 | tf_op jit(solution)/shard_map/ppermute | solution.py:17
  37.5 2.2 %shard_map.61 = (f32[24,256]{1,0:T(8,128)S(1)}, f32[24,256]{1,0:T(8,128)S(1)}, f32[24,256]{1,0:T(8,128)S(1)}, f32[24,256]{1,0:T(8,128)S(1)}) custom-call(bf16[144,128]{1,0:T(8,128)(2,1)S(1)} %shard_map.60.refs_0_, bf16[144,128]{1,0:T(8,128)(2,1)S(1)} %collective-permute-done.10.refs_1_, bf16[144,128]{1,0:T(8,128)(2,1)S(1)} %collective-permute-done.11.refs_2_, ...), custom_call_target="tpu_custom_call" | custom-call | flops 1073741824 | bytes 1048576 | tf_op jit(solution)/shard_map/pallas_call | solution.py:170
  39.7 0.6 %copy-done = f32[24,256]{1,0:T(8,128)} copy-done((f32[24,256]{1,0:T(8,128)}, f32[24,256]{1,0:T(8,128)S(1)}, u32[]{:S(2)}) %copy-start) | copy-done | bytes 24600
  40.3 1.4 %collective-permute-start.18 = (f32[24,256]{1,0:T(8,128)S(1)}, f32[24,256]{1,0:T(8,128)S(1)}, u32[]{:S(2)}, u32[]{:S(2)}) collective-permute-start(f32[24,256]{1,0:T(8,128)S(1)} %get-tuple-element.26), channel_id=1, source_target_pairs={{0,16},{8,24},{16,0},{24,8},{1,17},{9,25},{17,1},{25,9},{2,18},{10... | collective-permute-start | bytes 73736 | tf_op jit(solution)/shard_map/ppermute | solution.py:17
  41.7 0.5 %collective-permute-start.19 = (f32[24,256]{1,0:T(8,128)S(1)}, f32[24,256]{1,0:T(8,128)S(1)}, u32[]{:S(2)}, u32[]{:S(2)}) collective-permute-start(f32[24,256]{1,0:T(8,128)S(1)} %get-tuple-element.27), channel_id=1, source_target_pairs={{0,8},{8,0},{16,24},{24,16},{1,9},{9,1},{17,25},{25,17},{2,10},{10... | collective-permute-start | bytes 73736 | tf_op jit(solution)/shard_map/ppermute | solution.py:17
  42.1 1.6 %collective-permute-done.17.refs_1_ = f32[24,256]{1,0:T(8,128)S(1)} collective-permute-done((f32[24,256]{1,0:T(8,128)S(1)}, f32[24,256]{1,0:T(8,128)S(1)}, u32[]{:S(2)}, u32[]{:S(2)}) %collective-permute-start.17) | collective-permute-done | bytes 24608 | tf_op jit(solution)/shard_map/ppermute | solution.py:17
  43.7 0.4 collective-permute-done.18.refs_2_
  44.3 0.5 copy-done.5
  44.8 1.4 %shard_map.62 = (f32[1,16,256]{2,1,0:T(8,128)}, f32[1,1]{1,0:T(1,128)}) custom-call(f32[24,256]{1,0:T(8,128)} %copy-done, f32[24,256]{1,0:T(8,128)} %copy-done.4, f32[24,256]{1,0:T(8,128)} %copy-done.5, f32[24,256]{1,0:T(8,128)} %copy-done.6), custom_call_target="tpu_custom_call" | custom-call | tf_op jit(solution)/shard_map/pallas_call | solution.py:186
  (27 shorter events, 0.9 us)
Async XLA Ops:
  0.6 6.3 %copy-start.2 = (bf16[1,16,256]{2,1,0:T(8,128)(2,1)S(1)}, bf16[1,16,256]{2,1,0:T(8,128)(2,1)}, u32[]{:S(2)}) copy-start(bf16[1,16,256]{2,1,0:T(8,128)(2,1)} %refs_0_.1) | copy-start | bytes 24580
  0.6 6.3 %copy-start.1 = (f32[4,128,256]{2,1,0:T(8,128)S(1)}, f32[4,128,256]{2,1,0:T(8,128)}, u32[]{:S(2)}) copy-start(f32[4,128,256]{2,1,0:T(8,128)} %refs_5_.1) | copy-start | bytes 1572868
  0.6 5.7 %collective-permute-start.1 = (bf16[1,16,256]{2,1,0:T(8,128)(2,1)}, bf16[1,16,256]{2,1,0:T(8,128)(2,1)S(1)}, u32[]{:S(2)}, u32[]{:S(2)}) collective-permute-start(bf16[1,16,256]{2,1,0:T(8,128)(2,1)} %refs_0_.1), channel_id=1, source_target_pairs={{0,16},{8,24},{16,0},{24,8},{1,17},{9,25},{17,1},{25,9},{2,18},{10... | collective-permute-start | bytes 24584 | tf_op jit(solution)/shard_map/ppermute | solution.py:17
  3.7 2.7 %collective-permute-start = (bf16[1,16,256]{2,1,0:T(8,128)(2,1)}, bf16[1,16,256]{2,1,0:T(8,128)(2,1)S(1)}, u32[]{:S(2)}, u32[]{:S(2)}) collective-permute-start(bf16[1,16,256]{2,1,0:T(8,128)(2,1)} %refs_0_.1), channel_id=1, source_target_pairs={{0,8},{8,0},{16,24},{24,16},{1,9},{9,1},{17,25},{25,17},{2,10},{10... | collective-permute-start | bytes 24584 | tf_op jit(solution)/shard_map/ppermute | solution.py:17
  3.7 3.3 %collective-permute-start.2 = (bf16[1,16,256]{2,1,0:T(8,128)(2,1)}, bf16[1,16,256]{2,1,0:T(8,128)(2,1)S(1)}, u32[]{:S(2)}, u32[]{:S(2)}) collective-permute-start(bf16[1,16,256]{2,1,0:T(8,128)(2,1)} %refs_0_.1), channel_id=1, source_target_pairs={{0,24},{8,16},{16,8},{24,0},{1,25},{9,17},{17,9},{25,1},{2,26},{10... | collective-permute-start | bytes 24584 | tf_op jit(solution)/shard_map/ppermute | solution.py:17
  6.9 0.7 %copy-start.3 = (f32[128]{0:T(128)S(1)}, f32[128]{0:T(128)}, u32[]{:S(2)}) copy-start(f32[128]{0:T(128)} %param.7) | copy-start | bytes 1540
  9.1 9.9 %collective-permute-start.3 = (bf16[128,128]{1,0:T(8,128)(2,1)S(1)}, bf16[128,128]{1,0:T(8,128)(2,1)S(1)}, u32[]{:S(2)}, u32[]{:S(2)}) collective-permute-start(bf16[128,128]{1,0:T(8,128)(2,1)S(1)} %get-tuple-element.17), channel_id=1, source_target_pairs={{0,7},{1,6},{2,5},{3,4},{4,3},{5,2},{6,1},{7,0},{8,15},{9,14},{10,... | collective-permute-start | bytes 98312 | tf_op jit(solution)/shard_map/ppermute | solution.py:17
  13.7 6.1 %collective-permute-start.4 = (bf16[128,128]{1,0:T(8,128)(2,1)S(1)}, bf16[128,128]{1,0:T(8,128)(2,1)S(1)}, u32[]{:S(2)}, u32[]{:S(2)}) collective-permute-start(bf16[128,128]{1,0:T(8,128)(2,1)S(1)} %get-tuple-element.18), channel_id=1, source_target_pairs={{0,6},{1,7},{2,4},{3,5},{4,2},{5,3},{6,0},{7,1},{8,14},{9,15},{10,... | collective-permute-start | bytes 98312 | tf_op jit(solution)/shard_map/ppermute | solution.py:17
  14.0 6.6 %collective-permute-start.5 = (bf16[128,128]{1,0:T(8,128)(2,1)S(1)}, bf16[128,128]{1,0:T(8,128)(2,1)S(1)}, u32[]{:S(2)}, u32[]{:S(2)}) collective-permute-start(bf16[128,128]{1,0:T(8,128)(2,1)S(1)} %get-tuple-element.19), channel_id=1, source_target_pairs={{0,5},{1,4},{2,7},{3,6},{4,1},{5,0},{6,3},{7,2},{8,13},{9,12},{10,... | collective-permute-start | bytes 98312 | tf_op jit(solution)/shard_map/ppermute | solution.py:17
  14.7 5.9 %collective-permute-start.6 = (bf16[128,128]{1,0:T(8,128)(2,1)S(1)}, bf16[128,128]{1,0:T(8,128)(2,1)S(1)}, u32[]{:S(2)}, u32[]{:S(2)}) collective-permute-start(bf16[128,128]{1,0:T(8,128)(2,1)S(1)} %get-tuple-element.20), channel_id=1, source_target_pairs={{0,4},{1,5},{2,6},{3,7},{4,0},{5,1},{6,2},{7,3},{8,12},{9,13},{10,... | collective-permute-start | bytes 98312 | tf_op jit(solution)/shard_map/ppermute | solution.py:17
  16.8 5.2 %collective-permute-start.7 = (bf16[128,128]{1,0:T(8,128)(2,1)S(1)}, bf16[128,128]{1,0:T(8,128)(2,1)S(1)}, u32[]{:S(2)}, u32[]{:S(2)}) collective-permute-start(bf16[128,128]{1,0:T(8,128)(2,1)S(1)} %get-tuple-element.21), channel_id=1, source_target_pairs={{0,3},{1,2},{2,1},{3,0},{4,7},{5,6},{6,5},{7,4},{8,11},{9,10},{10,... | collective-permute-start | bytes 98312 | tf_op jit(solution)/shard_map/ppermute | solution.py:17
  19.0 3.9 %collective-permute-start.8 = (bf16[128,128]{1,0:T(8,128)(2,1)S(1)}, bf16[128,128]{1,0:T(8,128)(2,1)S(1)}, u32[]{:S(2)}, u32[]{:S(2)}) collective-permute-start(bf16[128,128]{1,0:T(8,128)(2,1)S(1)} %get-tuple-element.22), channel_id=1, source_target_pairs={{0,2},{1,3},{2,0},{3,1},{4,6},{5,7},{6,4},{7,5},{8,10},{9,11},{10,... | collective-permute-start | bytes 98312 | tf_op jit(solution)/shard_map/ppermute | solution.py:17
  19.8 3.9 %collective-permute-start.9 = (bf16[128,128]{1,0:T(8,128)(2,1)S(1)}, bf16[128,128]{1,0:T(8,128)(2,1)S(1)}, u32[]{:S(2)}, u32[]{:S(2)}) collective-permute-start(bf16[128,128]{1,0:T(8,128)(2,1)S(1)} %get-tuple-element.23), channel_id=1, source_target_pairs={{0,1},{1,0},{2,3},{3,2},{4,5},{5,4},{6,7},{7,6},{8,9},{9,8},{10,11... | collective-permute-start | bytes 98312 | tf_op jit(solution)/shard_map/ppermute | solution.py:17
  23.8 8.9 %collective-permute-start.16 = (bf16[144,128]{1,0:T(8,128)(2,1)S(1)}, bf16[144,128]{1,0:T(8,128)(2,1)S(1)}, u32[]{:S(2)}, u32[]{:S(2)}) collective-permute-start(bf16[144,128]{1,0:T(8,128)(2,1)S(1)} %shard_map.60.refs_0_), channel_id=1, source_target_pairs={{0,7},{1,6},{2,5},{3,4},{4,3},{5,2},{6,1},{7,0},{8,15},{9,14},{10,... | collective-permute-start | bytes 110600 | tf_op jit(solution)/shard_map/ppermute | solution.py:17
  27.4 6.1 %collective-permute-start.15 = (bf16[144,128]{1,0:T(8,128)(2,1)S(1)}, bf16[144,128]{1,0:T(8,128)(2,1)S(1)}, u32[]{:S(2)}, u32[]{:S(2)}) collective-permute-start(bf16[144,128]{1,0:T(8,128)(2,1)S(1)} %shard_map.60.refs_0_), channel_id=1, source_target_pairs={{0,6},{1,7},{2,4},{3,5},{4,2},{5,3},{6,0},{7,1},{8,14},{9,15},{10,... | collective-permute-start | bytes 110600 | tf_op jit(solution)/shard_map/ppermute | solution.py:17
  27.6 7.4 %collective-permute-start.14 = (bf16[144,128]{1,0:T(8,128)(2,1)S(1)}, bf16[144,128]{1,0:T(8,128)(2,1)S(1)}, u32[]{:S(2)}, u32[]{:S(2)}) collective-permute-start(bf16[144,128]{1,0:T(8,128)(2,1)S(1)} %shard_map.60.refs_0_), channel_id=1, source_target_pairs={{0,5},{1,4},{2,7},{3,6},{4,1},{5,0},{6,3},{7,2},{8,13},{9,12},{10,... | collective-permute-start | bytes 110600 | tf_op jit(solution)/shard_map/ppermute | solution.py:17
  29.0 6.0 %collective-permute-start.13 = (bf16[144,128]{1,0:T(8,128)(2,1)S(1)}, bf16[144,128]{1,0:T(8,128)(2,1)S(1)}, u32[]{:S(2)}, u32[]{:S(2)}) collective-permute-start(bf16[144,128]{1,0:T(8,128)(2,1)S(1)} %shard_map.60.refs_0_), channel_id=1, source_target_pairs={{0,4},{1,5},{2,6},{3,7},{4,0},{5,1},{6,2},{7,3},{8,12},{9,13},{10,... | collective-permute-start | bytes 110600 | tf_op jit(solution)/shard_map/ppermute | solution.py:17
  31.5 4.9 %collective-permute-start.12 = (bf16[144,128]{1,0:T(8,128)(2,1)S(1)}, bf16[144,128]{1,0:T(8,128)(2,1)S(1)}, u32[]{:S(2)}, u32[]{:S(2)}) collective-permute-start(bf16[144,128]{1,0:T(8,128)(2,1)S(1)} %shard_map.60.refs_0_), channel_id=1, source_target_pairs={{0,3},{1,2},{2,1},{3,0},{4,7},{5,6},{6,5},{7,4},{8,11},{9,10},{10,... | collective-permute-start | bytes 110600 | tf_op jit(solution)/shard_map/ppermute | solution.py:17
  32.8 4.0 %collective-permute-start.11 = (bf16[144,128]{1,0:T(8,128)(2,1)S(1)}, bf16[144,128]{1,0:T(8,128)(2,1)S(1)}, u32[]{:S(2)}, u32[]{:S(2)}) collective-permute-start(bf16[144,128]{1,0:T(8,128)(2,1)S(1)} %shard_map.60.refs_0_), channel_id=1, source_target_pairs={{0,2},{1,3},{2,0},{3,1},{4,6},{5,7},{6,4},{7,5},{8,10},{9,11},{10,... | collective-permute-start | bytes 110600 | tf_op jit(solution)/shard_map/ppermute | solution.py:17
  33.5 4.0 %collective-permute-start.10 = (bf16[144,128]{1,0:T(8,128)(2,1)S(1)}, bf16[144,128]{1,0:T(8,128)(2,1)S(1)}, u32[]{:S(2)}, u32[]{:S(2)}) collective-permute-start(bf16[144,128]{1,0:T(8,128)(2,1)S(1)} %shard_map.60.refs_0_), channel_id=1, source_target_pairs={{0,1},{1,0},{2,3},{3,2},{4,5},{5,4},{6,7},{7,6},{8,9},{9,8},{10,11... | collective-permute-start | bytes 110600 | tf_op jit(solution)/shard_map/ppermute | solution.py:17
  39.7 0.6 %copy-start = (f32[24,256]{1,0:T(8,128)}, f32[24,256]{1,0:T(8,128)S(1)}, u32[]{:S(2)}) copy-start(f32[24,256]{1,0:T(8,128)S(1)} %get-tuple-element.24.refs_0_) | copy-start | bytes 73732
  40.3 3.4 %collective-permute-start.17 = (f32[24,256]{1,0:T(8,128)S(1)}, f32[24,256]{1,0:T(8,128)S(1)}, u32[]{:S(2)}, u32[]{:S(2)}) collective-permute-start(f32[24,256]{1,0:T(8,128)S(1)} %get-tuple-element.25), channel_id=1, source_target_pairs={{0,24},{8,16},{16,8},{24,0},{1,25},{9,17},{17,9},{25,1},{2,26},{10... | collective-permute-start | bytes 73736 | tf_op jit(solution)/shard_map/ppermute | solution.py:17
  40.3 3.9 %collective-permute-start.18 = (f32[24,256]{1,0:T(8,128)S(1)}, f32[24,256]{1,0:T(8,128)S(1)}, u32[]{:S(2)}, u32[]{:S(2)}) collective-permute-start(f32[24,256]{1,0:T(8,128)S(1)} %get-tuple-element.26), channel_id=1, source_target_pairs={{0,16},{8,24},{16,0},{24,8},{1,17},{9,25},{17,1},{25,9},{2,18},{10... | collective-permute-start | bytes 73736 | tf_op jit(solution)/shard_map/ppermute | solution.py:17
  41.7 2.5 %collective-permute-start.19 = (f32[24,256]{1,0:T(8,128)S(1)}, f32[24,256]{1,0:T(8,128)S(1)}, u32[]{:S(2)}, u32[]{:S(2)}) collective-permute-start(f32[24,256]{1,0:T(8,128)S(1)} %get-tuple-element.27), channel_id=1, source_target_pairs={{0,8},{8,0},{16,24},{24,16},{1,9},{9,1},{17,25},{25,17},{2,10},{10... | collective-permute-start | bytes 73736 | tf_op jit(solution)/shard_map/ppermute | solution.py:17
  43.7 0.6 %copy-start.4 = (f32[24,256]{1,0:T(8,128)}, f32[24,256]{1,0:T(8,128)S(1)}, u32[]{:S(2)}) copy-start(f32[24,256]{1,0:T(8,128)S(1)} %collective-permute-done.17.refs_1_) | copy-start | bytes 73732
  44.1 0.6 %copy-start.5 = (f32[24,256]{1,0:T(8,128)}, f32[24,256]{1,0:T(8,128)S(1)}, u32[]{:S(2)}) copy-start(f32[24,256]{1,0:T(8,128)S(1)} %collective-permute-done.18.refs_2_) | copy-start | bytes 73732
  44.1 0.6 %copy-start.6 = (f32[24,256]{1,0:T(8,128)}, f32[24,256]{1,0:T(8,128)S(1)}, u32[]{:S(2)}) copy-start(f32[24,256]{1,0:T(8,128)S(1)} %collective-permute-done.19.refs_3_) | copy-start | bytes 73732

commit v3 on v2

--- a/solution.py
+++ b/solution.py
@@ -11,19 +11,27 @@
 WEIGHT_ROWS = 8
 MISFIT_ROWS = 8
 VMEM_LIMIT = 24 * 1024 * 1024
+SMALL_LIMIT = 4 * 1024 * 1024
 
 
 def swap(value, axis, step):
     return lax.ppermute(value, axis, [(i, i ^ step) for i in range(lax.axis_size(axis))])
 
 
-def forward_body(vectors, pieces, lags, *refs):
+def levels(size):
+    near = 1
+    while near * near * 4 <= size:
+        near *= 2
+    return near, size // near
+
+
+def forward_body(vectors, near, far, lags, *refs):
     models, refs = refs[:vectors], refs[vectors:]
     x_ref, observed_ref, weights_ref, own_ref = refs[:4]
-    sent, refs = refs[4 : 3 + pieces], refs[3 + pieces :]
+    sent, refs = refs[4 : 3 + near], refs[3 + near :]
     ut_ref, u_ref, acc_ref, seen_ref, scale_ref, sems = refs
     steps, points, sensors = x_ref.shape
-    rows = vectors * steps // pieces
+    rows = vectors * steps // (near * far)
     me, j = lax.axis_index("sens"), lax.axis_index("par")
     first = j * rows
     fetch_seen = pltpu.make_async_copy(observed_ref.at[me ^ (first // steps)], seen_ref, sems.at[0])
@@ -50,16 +58,33 @@
             else:
                 acc_ref[at + k0 : end, :] += part[:, :sensors]
             acc_ref[at + k0 + lags : end, :] += part[: left - lags, sensors:]
-    for step in range(1, pieces):
-        there = pl.multiple_of((j ^ step) * rows, rows)
-        sent[step - 1][...] = acc_ref[pl.ds(there, rows), :].astype(jnp.bfloat16)
+    for b in range(far):
+        for a in range(near):
+            there = pl.multiple_of((j ^ (b * near + a)) * rows, rows)
+            part = acc_ref[pl.ds(there, rows), :]
+            if a == 0:
+                own_ref[b * rows : (b + 1) * rows, :] = part
+            else:
+                sent[a - 1][b * rows : (b + 1) * rows, :] = part.astype(jnp.bfloat16)
     fetch_seen.wait()
     fetch_scale.wait()
     ut_ref[0, :, :sensors] = seen_ref[...].T
-    here = pl.multiple_of(first, rows)
-    seen = ut_ref[0, pl.ds(pl.multiple_of(first % steps, rows), rows), :sensors]
-    own_ref[:rows, :] = acc_ref[pl.ds(here, rows), :] - seen
-    own_ref[rows:, :] = jnp.broadcast_to(scale_ref[...], (WEIGHT_ROWS, sensors))
+    own_ref[:rows, :] -= ut_ref[0, pl.ds(pl.multiple_of(first % steps, rows), rows), :sensors]
+    own_ref[far * rows :, :] = jnp.broadcast_to(scale_ref[...], (WEIGHT_ROWS, sensors))
+
+
+def middle_body(near, far, own_ref, *refs):
+    terms, out_ref, sent = refs[: near - 1], refs[near - 1], refs[near:]
+    rows = (own_ref.shape[0] - WEIGHT_ROWS) // far
+    for b in range(far):
+        part = own_ref[b * rows : (b + 1) * rows, :]
+        for term in terms:
+            part += term[b * rows : (b + 1) * rows, :].astype(jnp.float32)
+        if b == 0:
+            out_ref[:rows, :] = part
+        else:
+            sent[b - 1][...] = part.astype(jnp.bfloat16)
+    out_ref[rows:, :] = own_ref[far * rows :, :]
 
 
 def residual_body(own_ref, *refs):
@@ -80,21 +105,30 @@
     out_ref[rows:, :] = parts.astype(jnp.bfloat16)
 
 
-def adjoint_body(vectors, pieces, lags, *refs):
-    gathered, x_ref = refs[:pieces], refs[pieces]
-    outs, (a_ref, r_ref, all_ref) = refs[pieces + 1 : pieces + 1 + vectors], refs[pieces + 1 + vectors :]
+def join_body(*refs):
+    parts, out_ref = refs[:-1], refs[-1]
+    rows = parts[0].shape[0]
+    for b, part in enumerate(parts):
+        out_ref[b * rows : (b + 1) * rows, :] = part[...]
+
+
+def adjoint_body(vectors, near, far, lags, *refs):
+    gathered, x_ref = refs[:near], refs[near]
+    outs, (a_ref, r_ref, all_ref) = refs[near + 1 : near + 1 + vectors], refs[near + 1 + vectors :]
     steps, points, sensors = x_ref.shape
-    rows = vectors * steps // pieces
+    rows = vectors * steps // (near * far)
     blocks = steps // lags
     j = lax.axis_index("par")
     for d in range(lags):
         for c in range(blocks):
             a_ref[c * points : (c + 1) * points, d * sensors : (d + 1) * sensors] = x_ref[c * lags + d]
     extra = jnp.zeros((EXTRA_ROWS, sensors), jnp.float32)
-    for step in range(pieces):
-        there = pl.multiple_of((j ^ step) * rows, rows)
-        all_ref[pl.ds(there, rows), :] = gathered[step][:rows, :].astype(jnp.float32)
-        extra += gathered[step][rows:, :].astype(jnp.float32)
+    for b in range(far):
+        for a in range(near):
+            there = pl.multiple_of((j ^ (b * near + a)) * rows, rows)
+            at = b * (rows + EXTRA_ROWS)
+            all_ref[pl.ds(there, rows), :] = gathered[a][at : at + rows, :].astype(jnp.float32)
+            extra += gathered[a][at + rows : at + rows + EXTRA_ROWS, :].astype(jnp.float32)
     squared = jnp.sum(extra)
     lane = lax.broadcasted_iota(jnp.int32, (sensors, steps), 1)
     lane_p = lax.broadcasted_iota(jnp.int32, (points, steps), 1)
@@ -124,27 +158,39 @@
     misfit_ref[...] = total[points : points + 1, :1] * scale
 
 
+def call(body, out_shape, operands, limit=SMALL_LIMIT, **options):
+    vmem = pl.BlockSpec(memory_space=pltpu.VMEM)
+    options.setdefault("in_specs", [vmem] * len(operands))
+    return pl.pallas_call(
+        body,
+        out_shape=out_shape,
+        out_specs=jax.tree.map(lambda _: vmem, out_shape),
+        compiler_params=pltpu.CompilerParams(vmem_limit_bytes=limit),
+        **options,
+    )(*operands)
+
+
 def local(model, kernel, observed, weights):
     n_sens, n_par = lax.axis_size("sens"), lax.axis_size("par")
+    near, far = levels(n_par)
     sensors, points, steps = kernel.shape
     vectors = n_sens * model.shape[0]
     lags = 256 // points
     rows = vectors * steps // n_par
-    vmem = pl.BlockSpec(memory_space=pltpu.VMEM)
-    anywhere = pl.BlockSpec(memory_space=pl.ANY)
-    params = pltpu.CompilerParams(vmem_limit_bytes=VMEM_LIMIT)
     flops = 2 * vectors * sensors * points * steps * steps
     cost = pl.CostEstimate(flops=flops, bytes_accessed=2 * kernel.size, transcendentals=0)
 
     models = [model] + [swap(model, "sens", step) for step in range(1, n_sens)]
     x = jnp.transpose(kernel, (2, 1, 0))
 
-    piece = jax.ShapeDtypeStruct((rows, sensors), jnp.bfloat16)
-    own, *sent = pl.pallas_call(
-        functools.partial(forward_body, vectors, n_par, lags),
-        out_shape=[jax.ShapeDtypeStruct((rows + WEIGHT_ROWS, sensors), jnp.float32)] + [piece] * (n_par - 1),
-        in_specs=[vmem] * (vectors + 1) + [anywhere] * 2,
-        out_specs=[vmem] * n_par,
+    vmem, hbm = pl.BlockSpec(memory_space=pltpu.VMEM), pl.BlockSpec(memory_space=pltpu.HBM)
+    own, *sent = call(
+        functools.partial(forward_body, vectors, near, far, lags),
+        [jax.ShapeDtypeStruct((far * rows + WEIGHT_ROWS, sensors), jnp.float32)]
+        + [jax.ShapeDtypeStruct((far * rows, sensors), jnp.bfloat16)] * (near - 1),
+        (*models, x, observed, weights[None, :]),
+        VMEM_LIMIT,
+        in_specs=[vmem] * (vectors + 1) + [hbm] * 2,
         scratch_shapes=[
             pltpu.VMEM((vectors, lags * points, steps), jnp.float32),
             pltpu.VMEM((vectors, steps, lags * points), jnp.bfloat16),
@@ -153,45 +199,50 @@
             pltpu.VMEM((1, sensors), jnp.float32),
             pltpu.SemaphoreType.DMA((2,)),
         ],
-        compiler_params=params,
         cost_estimate=cost,
-    )(*models, x, observed, weights[None, :])
-
-    terms = [swap(sent[step - 1], "par", step) for step in range(n_par - 1, 0, -1)]
-    residual = pl.pallas_call(
+    )
+
+    terms = [swap(sent[a - 1], "par", a) for a in range(1, near)]
+    own, *sent = call(
+        functools.partial(middle_body, near, far),
+        [jax.ShapeDtypeStruct((rows + WEIGHT_ROWS, sensors), jnp.float32)]
+        + [jax.ShapeDtypeStruct((rows, sensors), jnp.bfloat16)] * (far - 1),
+        (own, *terms),
+    )
+    terms = [swap(sent[b - 1], "par", b * near) for b in range(far - 1, 0, -1)]
+    residual = call(
         residual_body,
-        out_shape=jax.ShapeDtypeStruct((rows + EXTRA_ROWS, sensors), jnp.bfloat16),
-        in_specs=[vmem] * n_par,
-        out_specs=vmem,
-        compiler_params=params,
-    )(own, *terms)
-    gathered = [swap(residual, "par", step) for step in range(n_par - 1, 0, -1)]
-
-    partials = pl.pallas_call(
-        functools.partial(adjoint_body, vectors, n_par, lags),
-        out_shape=[jax.ShapeDtypeStruct((points + MISFIT_ROWS, steps), jnp.float32)] * vectors,
-        in_specs=[vmem] * (n_par + 1),
-        out_specs=[vmem] * vectors,
+        jax.ShapeDtypeStruct((rows + EXTRA_ROWS, sensors), jnp.bfloat16),
+        (own, *terms),
+    )
+    parts = [swap(residual, "par", b * near) for b in range(far - 1, 0, -1)]
+    block = call(
+        join_body,
+        jax.ShapeDtypeStruct((far * (rows + EXTRA_ROWS), sensors), jnp.bfloat16),
+        (residual, *parts[::-1]),
+    )
+    gathered = [block] + [swap(block, "par", a) for a in range(1, near)]
+
+    partials = call(
+        functools.partial(adjoint_body, vectors, near, far, lags),
+        [jax.ShapeDtypeStruct((points + MISFIT_ROWS, steps), jnp.float32)] * vectors,
+        (*gathered, x),
+        VMEM_LIMIT,
         scratch_shapes=[
             pltpu.VMEM((steps // lags * points, lags * sensors), jnp.bfloat16),
             pltpu.VMEM((vectors, lags * sensors, steps), jnp.bfloat16),
             pltpu.VMEM((vectors * steps, sensors), jnp.float32),
         ],
-        compiler_params=params,
         cost_estimate=cost,
-    )(residual, *gathered[::-1], x)
+    )
 
     received = [swap(partials[step], "sens", step) for step in range(n_sens - 1, 0, -1)]
     entries = vectors * sensors * n_sens * steps
-    gradient, misfit = pl.pallas_call(
+    gradient, misfit = call(
         functools.partial(total_body, 0.5 / entries),
-        out_shape=[
-            jax.ShapeDtypeStruct((1, points, steps), jnp.float32),
-            jax.ShapeDtypeStruct((1, 1), jnp.float32),
-        ],
-        in_specs=[vmem] * n_sens,
-        out_specs=[vmem] * 2,
-    )(partials[0], *received)
+        [jax.ShapeDtypeStruct((1, points, steps), jnp.float32), jax.ShapeDtypeStruct((1, 1), jnp.float32)],
+        (partials[0], *received),
+    )
     return (gradient, misfit[0, 0])
 
 

time: 46.4 us -> 42.8 us (0.922)
  starting transfers between devices: 27.5 us -> 17.2 us
  waiting for transfers between devices: 8.45 us -> 17.2 us
  local copies, waits for them, and re-layouts: 4.32 us -> 3.12 us
  Pallas kernels: 5.2 us -> 4.45 us
    ppermute x20 -> x14, starting transfers between devices: 27.5 us -> 17.2 us  [swap(): lax.ppermute(value, axis, [(i, i ^ step) for i in range(lax.axis_size(axi...]
    ppermute x20 -> x14, waiting for transfers between devices: 8.45 us -> 17.2 us  [swap(): lax.ppermute(value, axis, [(i, i ^ step) for i in range(lax.axis_size(axi...]
    unnamed x15 -> x7, local copies, waits for them, and re-layouts: 4.32 us -> 3.12 us
    pallas_call x4 -> x6, Pallas kernels: 5.2 us -> 4.45 us  [call(): pl.pallas_call(body, out_shape=out_shape, out_specs=jax.tree.map(lambda _...]
  transfers between devices with their start and end apart: 20 -> 14, of which waited for: 10 -> 10; matrix products, arithmetic and copies ran while one was open for 5% -> 6% of each run, Pallas kernels for 0% -> 0%
where the time goes in v3:
time: 42.8 us; the launch traced here: 42.7 us
  starting transfers between devices  17.2 us (40%)
  waiting for transfers between devices  17.2 us (40%)
  Pallas kernels  4.45 us (10%)
  local copies, waits for them, and re-layouts  3.12 us (7%)
  between operations  0.71 us (2%)
    ppermute x14, starting transfers between devices, swap(): lax.ppermute(value, axis, [(i, i ^ step) for i in range(lax.axis_size(axi...  17.2 us
    ppermute x14, waiting for transfers between devices, swap(): lax.ppermute(value, axis, [(i, i ^ step) for i in range(lax.axis_size(axi...  17.2 us
    pallas_call x6, Pallas kernels, call(): pl.pallas_call(body, out_shape=out_shape, out_specs=jax.tree.map(lambda _...  4.45 us
    unnamed x7, local copies, waits for them, and re-layouts  3.12 us
  transfers between devices with their start and end apart: 14, of which 10 were waited for; matrix products, arithmetic and copies ran while one was open for 6% of the time, Pallas kernels for 0%

profile of v3, /device:TPU:0, one launch (start us, length us, event | category | flops | bytes accessed | tf_op | source)
XLA Modules:
  0.0 42.7 jit_solution(14976254458669772585)
XLA Ops:
  0.6 3.0 %collective-permute-start.1 = (bf16[1,16,256]{2,1,0:T(8,128)(2,1)}, bf16[1,16,256]{2,1,0:T(8,128)(2,1)S(1)}, u32[]{:S(2)}, u32[]{:S(2)}) collective-permute-start(bf16[1,16,256]{2,1,0:T(8,128)(2,1)} %refs_0_.1), channel_id=1, source_target_pairs={{0,16},{8,24},{16,0},{24,8},{1,17},{9,25},{17,1},{25,9},{2,18},{10... | collective-permute-start | bytes 24584 | tf_op jit(solution)/shard_map/ppermute | solution.py:18
  3.7 0.0 collective-permute-start
  3.7 0.2 collective-permute-start.2
  3.9 2.5 %copy.6 = bf16[128,16,256]{0,1,2:T(8,128)(2,1)S(1)} copy(bf16[128,16,256]{2,1,0:T(8,128)(2,1)} %param.5) | data formatting | bytes 2097152 | tf_op args[1]
  6.3 0.0 collective-permute-done.1.refs_2_
  6.3 0.0 collective-permute-done.refs_1_
  6.3 0.6 %collective-permute-done.2.refs_3_ = bf16[1,16,256]{2,1,0:T(8,128)(2,1)S(1)} collective-permute-done((bf16[1,16,256]{2,1,0:T(8,128)(2,1)}, bf16[1,16,256]{2,1,0:T(8,128)(2,1)S(1)}, u32[]{:S(2)}, u32[]{:S(2)}) %collective-permute-start.2) | collective-permute-done | bytes 8224 | tf_op jit(solution)/shard_map/ppermute | solution.py:18
  7.0 0.6 %copy-done.2 = f32[128]{0:T(128)S(1)} copy-done((f32[128]{0:T(128)S(1)}, f32[128]{0:T(128)}, u32[]{:S(2)}) %copy-start.2) | copy-done | bytes 536
  7.6 1.5 %shard_map.59 = (f32[520,128]{1,0:T(8,128)S(1)}, bf16[512,128]{1,0:T(8,128)(2,1)S(1)}) custom-call(bf16[1,16,256]{2,1,0:T(8,128)(2,1)S(1)} %copy-done.1, bf16[1,16,256]{2,1,0:T(8,128)(2,1)S(1)} %collective-permute-done.refs_1_, bf16[1,16,256]{2,1,0:T(8,128)(2,1)S(1)} %collective-permute-done.1.refs_2_, ...), custom_call_target="tpu_custom_call" | custom-call | flops 1073741824 | bytes 1048576 | tf_op jit(solution)/shard_map/pallas_call | solution.py:164
  9.1 1.6 %collective-permute-start.3 = (bf16[512,128]{1,0:T(8,128)(2,1)S(1)}, bf16[512,128]{1,0:T(8,128)(2,1)S(1)}, u32[]{:S(2)}, u32[]{:S(2)}) collective-permute-start(bf16[512,128]{1,0:T(8,128)(2,1)S(1)} %get-tuple-element.15), channel_id=1, source_target_pairs={{0,1},{1,0},{2,3},{3,2},{4,5},{5,4},{6,7},{7,6},{8,9},{9,8},{10,11... | collective-permute-start | bytes 393224 | tf_op jit(solution)/shard_map/ppermute | solution.py:18
  10.7 4.4 %collective-permute-done.3.refs_0_ = bf16[512,128]{1,0:T(8,128)(2,1)S(1)} collective-permute-done((bf16[512,128]{1,0:T(8,128)(2,1)S(1)}, bf16[512,128]{1,0:T(8,128)(2,1)S(1)}, u32[]{:S(2)}, u32[]{:S(2)}) %collective-permute-start.3) | collective-permute-done | bytes 131104 | tf_op jit(solution)/shard_map/ppermute | solution.py:18
  15.1 3.7 %collective-permute-start.4 = (bf16[128,128]{1,0:T(8,128)(2,1)S(1)}, bf16[128,128]{1,0:T(8,128)(2,1)S(1)}, u32[]{:S(2)}, u32[]{:S(2)}) collective-permute-start(bf16[128,128]{1,0:T(8,128)(2,1)S(1)} %get-tuple-element.17), channel_id=1, source_target_pairs={{0,6},{1,7},{2,4},{3,5},{4,2},{5,3},{6,0},{7,1},{8,14},{9,15},{10,... | collective-permute-start | bytes 98312 | tf_op jit(solution)/shard_map/ppermute | solution.py:18
  18.8 0.0 collective-permute-start.5
  18.8 0.8 %collective-permute-start.6 = (bf16[128,128]{1,0:T(8,128)(2,1)S(1)}, bf16[128,128]{1,0:T(8,128)(2,1)S(1)}, u32[]{:S(2)}, u32[]{:S(2)}) collective-permute-start(bf16[128,128]{1,0:T(8,128)(2,1)S(1)} %get-tuple-element.19), channel_id=1, source_target_pairs={{0,2},{1,3},{2,0},{3,1},{4,6},{5,7},{6,4},{7,5},{8,10},{9,11},{10,... | collective-permute-start | bytes 98312 | tf_op jit(solution)/shard_map/ppermute | solution.py:18
  19.6 1.5 %collective-permute-done.4.refs_0_ = bf16[128,128]{1,0:T(8,128)(2,1)S(1)} collective-permute-done((bf16[128,128]{1,0:T(8,128)(2,1)S(1)}, bf16[128,128]{1,0:T(8,128)(2,1)S(1)}, u32[]{:S(2)}, u32[]{:S(2)}) %collective-permute-start.4) | collective-permute-done | bytes 32800 | tf_op jit(solution)/shard_map/ppermute | solution.py:18
  21.1 2.5 %collective-permute-done.5.refs_1_ = bf16[128,128]{1,0:T(8,128)(2,1)S(1)} collective-permute-done((bf16[128,128]{1,0:T(8,128)(2,1)S(1)}, bf16[128,128]{1,0:T(8,128)(2,1)S(1)}, u32[]{:S(2)}, u32[]{:S(2)}) %collective-permute-start.5) | collective-permute-done | bytes 32800 | tf_op jit(solution)/shard_map/ppermute | solution.py:18
  23.6 0.0 collective-permute-done.6.refs_2_
  23.7 1.5 %collective-permute-start.9 = (bf16[144,128]{1,0:T(8,128)(2,1)S(1)}, bf16[144,128]{1,0:T(8,128)(2,1)S(1)}, u32[]{:S(2)}, u32[]{:S(2)}) collective-permute-start(bf16[144,128]{1,0:T(8,128)(2,1)S(1)} %shard_map.61.refs_0_), channel_id=1, source_target_pairs={{0,6},{1,7},{2,4},{3,5},{4,2},{5,3},{6,0},{7,1},{8,14},{9,15},{10,... | collective-permute-start | bytes 110600 | tf_op jit(solution)/shard_map/ppermute | solution.py:18
  25.2 0.6 %collective-permute-start.8 = (bf16[144,128]{1,0:T(8,128)(2,1)S(1)}, bf16[144,128]{1,0:T(8,128)(2,1)S(1)}, u32[]{:S(2)}, u32[]{:S(2)}) collective-permute-start(bf16[144,128]{1,0:T(8,128)(2,1)S(1)} %shard_map.61.refs_0_), channel_id=1, source_target_pairs={{0,4},{1,5},{2,6},{3,7},{4,0},{5,1},{6,2},{7,3},{8,12},{9,13},{10,... | collective-permute-start | bytes 110600 | tf_op jit(solution)/shard_map/ppermute | solution.py:18
  25.8 2.3 %collective-permute-start.7 = (bf16[144,128]{1,0:T(8,128)(2,1)S(1)}, bf16[144,128]{1,0:T(8,128)(2,1)S(1)}, u32[]{:S(2)}, u32[]{:S(2)}) collective-permute-start(bf16[144,128]{1,0:T(8,128)(2,1)S(1)} %shard_map.61.refs_0_), channel_id=1, source_target_pairs={{0,2},{1,3},{2,0},{3,1},{4,6},{5,7},{6,4},{7,5},{8,10},{9,11},{10,... | collective-permute-start | bytes 110600 | tf_op jit(solution)/shard_map/ppermute | solution.py:18
  28.1 1.4 %collective-permute-done.9.refs_3_ = bf16[144,128]{1,0:T(8,128)(2,1)S(1)} collective-permute-done((bf16[144,128]{1,0:T(8,128)(2,1)S(1)}, bf16[144,128]{1,0:T(8,128)(2,1)S(1)}, u32[]{:S(2)}, u32[]{:S(2)}) %collective-permute-start.9) | collective-permute-done | bytes 36896 | tf_op jit(solution)/shard_map/ppermute | solution.py:18
  29.5 0.6 %collective-permute-done.8.refs_2_ = bf16[144,128]{1,0:T(8,128)(2,1)S(1)} collective-permute-done((bf16[144,128]{1,0:T(8,128)(2,1)S(1)}, bf16[144,128]{1,0:T(8,128)(2,1)S(1)}, u32[]{:S(2)}, u32[]{:S(2)}) %collective-permute-start.8) | collective-permute-done | bytes 36896 | tf_op jit(solution)/shard_map/ppermute | solution.py:18
  30.1 0.4 collective-permute-done.7.refs_1_
  30.5 1.6 %collective-permute-start.10 = (bf16[576,128]{1,0:T(8,128)(2,1)S(1)}, bf16[576,128]{1,0:T(8,128)(2,1)S(1)}, u32[]{:S(2)}, u32[]{:S(2)}) collective-permute-start(bf16[576,128]{1,0:T(8,128)(2,1)S(1)} %shard_map.62.refs_0_), channel_id=1, source_target_pairs={{0,1},{1,0},{2,3},{3,2},{4,5},{5,4},{6,7},{7,6},{8,9},{9,8},{10,11... | collective-permute-start | bytes 442376 | tf_op jit(solution)/shard_map/ppermute | solution.py:18
  32.0 3.6 %collective-permute-done.10.refs_1_ = bf16[576,128]{1,0:T(8,128)(2,1)S(1)} collective-permute-done((bf16[576,128]{1,0:T(8,128)(2,1)S(1)}, bf16[576,128]{1,0:T(8,128)(2,1)S(1)}, u32[]{:S(2)}, u32[]{:S(2)}) %collective-permute-start.10) | collective-permute-done | bytes 147488 | tf_op jit(solution)/shard_map/ppermute | solution.py:18
  35.7 2.2 %shard_map.63 = (f32[24,256]{1,0:T(8,128)S(1)}, f32[24,256]{1,0:T(8,128)S(1)}, f32[24,256]{1,0:T(8,128)S(1)}, f32[24,256]{1,0:T(8,128)S(1)}) custom-call(bf16[576,128]{1,0:T(8,128)(2,1)S(1)} %shard_map.62.refs_0_, bf16[576,128]{1,0:T(8,128)(2,1)S(1)} %collective-permute-done.10.refs_1_, bf16[256,16,128]{2,1,0:T(8,128)(2,1)S(1)} %bitcast.4), custom_call_target="tpu_custom_call" | custom-call | flops 1073741824 | bytes 1048576 | tf_op jit(solution)/shard_map/pallas_call | solution.py:164
  37.9 0.1 collective-permute-start.11
  38.0 0.9 %collective-permute-start.12 = (f32[24,256]{1,0:T(8,128)S(1)}, f32[24,256]{1,0:T(8,128)S(1)}, u32[]{:S(2)}, u32[]{:S(2)}) collective-permute-start(f32[24,256]{1,0:T(8,128)S(1)} %get-tuple-element.22), channel_id=1, source_target_pairs={{0,16},{8,24},{16,0},{24,8},{1,17},{9,25},{17,1},{25,9},{2,18},{10... | collective-permute-start | bytes 73736 | tf_op jit(solution)/shard_map/ppermute | solution.py:18
  38.9 0.9 %collective-permute-start.13 = (f32[24,256]{1,0:T(8,128)S(1)}, f32[24,256]{1,0:T(8,128)S(1)}, u32[]{:S(2)}, u32[]{:S(2)}) collective-permute-start(f32[24,256]{1,0:T(8,128)S(1)} %get-tuple-element.23), channel_id=1, source_target_pairs={{0,8},{8,0},{16,24},{24,16},{1,9},{9,1},{17,25},{25,17},{2,10},{10... | collective-permute-start | bytes 73736 | tf_op jit(solution)/shard_map/ppermute | solution.py:18
  39.8 1.4 %collective-permute-done.11.refs_1_ = f32[24,256]{1,0:T(8,128)S(1)} collective-permute-done((f32[24,256]{1,0:T(8,128)S(1)}, f32[24,256]{1,0:T(8,128)S(1)}, u32[]{:S(2)}, u32[]{:S(2)}) %collective-permute-start.11) | collective-permute-done | bytes 24608 | tf_op jit(solution)/shard_map/ppermute | solution.py:18
  41.2 0.8 %collective-permute-done.12.refs_2_ = f32[24,256]{1,0:T(8,128)S(1)} collective-permute-done((f32[24,256]{1,0:T(8,128)S(1)}, f32[24,256]{1,0:T(8,128)S(1)}, u32[]{:S(2)}, u32[]{:S(2)}) %collective-permute-start.12) | collective-permute-done | bytes 24608 | tf_op jit(solution)/shard_map/ppermute | solution.py:18
  42.1 0.6 %shard_map.64 = (f32[1,16,256]{2,1,0:T(8,128)}, f32[1,1]{1,0:T(1,128)}) custom-call(f32[24,256]{1,0:T(8,128)S(1)} %get-tuple-element.20.refs_0_, f32[24,256]{1,0:T(8,128)S(1)} %collective-permute-done.11.refs_1_, f32[24,256]{1,0:T(8,128)S(1)} %collective-permute-done.12.refs_2_, f32[24,256]{1,0:T(8,128)S(1)} %collective-permute-done.13.refs_3_), custom_call_target="tpu_custom_call" | custom-call | tf_op jit(solution)/shard_map/pallas_call | solution.py:164
  (9 shorter events, 0.1 us)
Async XLA Ops:
  0.6 6.3 %copy-start.1 = (bf16[1,16,256]{2,1,0:T(8,128)(2,1)S(1)}, bf16[1,16,256]{2,1,0:T(8,128)(2,1)}, u32[]{:S(2)}) copy-start(bf16[1,16,256]{2,1,0:T(8,128)(2,1)} %refs_0_.1) | copy-start | bytes 24580
  0.6 6.3 %copy-start = (f32[4,128,256]{2,1,0:T(8,128)S(1)}, f32[4,128,256]{2,1,0:T(8,128)}, u32[]{:S(2)}) copy-start(f32[4,128,256]{2,1,0:T(8,128)} %refs_5_.1) | copy-start | bytes 1572868
  0.6 5.7 %collective-permute-start.1 = (bf16[1,16,256]{2,1,0:T(8,128)(2,1)}, bf16[1,16,256]{2,1,0:T(8,128)(2,1)S(1)}, u32[]{:S(2)}, u32[]{:S(2)}) collective-permute-start(bf16[1,16,256]{2,1,0:T(8,128)(2,1)} %refs_0_.1), channel_id=1, source_target_pairs={{0,16},{8,24},{16,0},{24,8},{1,17},{9,25},{17,1},{25,9},{2,18},{10... | collective-permute-start | bytes 24584 | tf_op jit(solution)/shard_map/ppermute | solution.py:18
  3.7 2.7 %collective-permute-start = (bf16[1,16,256]{2,1,0:T(8,128)(2,1)}, bf16[1,16,256]{2,1,0:T(8,128)(2,1)S(1)}, u32[]{:S(2)}, u32[]{:S(2)}) collective-permute-start(bf16[1,16,256]{2,1,0:T(8,128)(2,1)} %refs_0_.1), channel_id=1, source_target_pairs={{0,8},{8,0},{16,24},{24,16},{1,9},{9,1},{17,25},{25,17},{2,10},{10... | collective-permute-start | bytes 24584 | tf_op jit(solution)/shard_map/ppermute | solution.py:18
  3.7 3.3 %collective-permute-start.2 = (bf16[1,16,256]{2,1,0:T(8,128)(2,1)}, bf16[1,16,256]{2,1,0:T(8,128)(2,1)S(1)}, u32[]{:S(2)}, u32[]{:S(2)}) collective-permute-start(bf16[1,16,256]{2,1,0:T(8,128)(2,1)} %refs_0_.1), channel_id=1, source_target_pairs={{0,24},{8,16},{16,8},{24,0},{1,25},{9,17},{17,9},{25,1},{2,26},{10... | collective-permute-start | bytes 24584 | tf_op jit(solution)/shard_map/ppermute | solution.py:18
  6.9 0.7 %copy-start.2 = (f32[128]{0:T(128)S(1)}, f32[128]{0:T(128)}, u32[]{:S(2)}) copy-start(f32[128]{0:T(128)} %param.7) | copy-start | bytes 1540
  9.1 6.0 %collective-permute-start.3 = (bf16[512,128]{1,0:T(8,128)(2,1)S(1)}, bf16[512,128]{1,0:T(8,128)(2,1)S(1)}, u32[]{:S(2)}, u32[]{:S(2)}) collective-permute-start(bf16[512,128]{1,0:T(8,128)(2,1)S(1)} %get-tuple-element.15), channel_id=1, source_target_pairs={{0,1},{1,0},{2,3},{3,2},{4,5},{5,4},{6,7},{7,6},{8,9},{9,8},{10,11... | collective-permute-start | bytes 393224 | tf_op jit(solution)/shard_map/ppermute | solution.py:18
  15.1 5.9 %collective-permute-start.4 = (bf16[128,128]{1,0:T(8,128)(2,1)S(1)}, bf16[128,128]{1,0:T(8,128)(2,1)S(1)}, u32[]{:S(2)}, u32[]{:S(2)}) collective-permute-start(bf16[128,128]{1,0:T(8,128)(2,1)S(1)} %get-tuple-element.17), channel_id=1, source_target_pairs={{0,6},{1,7},{2,4},{3,5},{4,2},{5,3},{6,0},{7,1},{8,14},{9,15},{10,... | collective-permute-start | bytes 98312 | tf_op jit(solution)/shard_map/ppermute | solution.py:18
  18.8 4.8 %collective-permute-start.5 = (bf16[128,128]{1,0:T(8,128)(2,1)S(1)}, bf16[128,128]{1,0:T(8,128)(2,1)S(1)}, u32[]{:S(2)}, u32[]{:S(2)}) collective-permute-start(bf16[128,128]{1,0:T(8,128)(2,1)S(1)} %get-tuple-element.18), channel_id=1, source_target_pairs={{0,4},{1,5},{2,6},{3,7},{4,0},{5,1},{6,2},{7,3},{8,12},{9,13},{10,... | collective-permute-start | bytes 98312 | tf_op jit(solution)/shard_map/ppermute | solution.py:18
  18.8 4.8 %collective-permute-start.6 = (bf16[128,128]{1,0:T(8,128)(2,1)S(1)}, bf16[128,128]{1,0:T(8,128)(2,1)S(1)}, u32[]{:S(2)}, u32[]{:S(2)}) collective-permute-start(bf16[128,128]{1,0:T(8,128)(2,1)S(1)} %get-tuple-element.19), channel_id=1, source_target_pairs={{0,2},{1,3},{2,0},{3,1},{4,6},{5,7},{6,4},{7,5},{8,10},{9,11},{10,... | collective-permute-start | bytes 98312 | tf_op jit(solution)/shard_map/ppermute | solution.py:18
  23.7 5.8 %collective-permute-start.9 = (bf16[144,128]{1,0:T(8,128)(2,1)S(1)}, bf16[144,128]{1,0:T(8,128)(2,1)S(1)}, u32[]{:S(2)}, u32[]{:S(2)}) collective-permute-start(bf16[144,128]{1,0:T(8,128)(2,1)S(1)} %shard_map.61.refs_0_), channel_id=1, source_target_pairs={{0,6},{1,7},{2,4},{3,5},{4,2},{5,3},{6,0},{7,1},{8,14},{9,15},{10,... | collective-permute-start | bytes 110600 | tf_op jit(solution)/shard_map/ppermute | solution.py:18
  25.2 4.9 %collective-permute-start.8 = (bf16[144,128]{1,0:T(8,128)(2,1)S(1)}, bf16[144,128]{1,0:T(8,128)(2,1)S(1)}, u32[]{:S(2)}, u32[]{:S(2)}) collective-permute-start(bf16[144,128]{1,0:T(8,128)(2,1)S(1)} %shard_map.61.refs_0_), channel_id=1, source_target_pairs={{0,4},{1,5},{2,6},{3,7},{4,0},{5,1},{6,2},{7,3},{8,12},{9,13},{10,... | collective-permute-start | bytes 110600 | tf_op jit(solution)/shard_map/ppermute | solution.py:18
  25.8 4.6 %collective-permute-start.7 = (bf16[144,128]{1,0:T(8,128)(2,1)S(1)}, bf16[144,128]{1,0:T(8,128)(2,1)S(1)}, u32[]{:S(2)}, u32[]{:S(2)}) collective-permute-start(bf16[144,128]{1,0:T(8,128)(2,1)S(1)} %shard_map.61.refs_0_), channel_id=1, source_target_pairs={{0,2},{1,3},{2,0},{3,1},{4,6},{5,7},{6,4},{7,5},{8,10},{9,11},{10,... | collective-permute-start | bytes 110600 | tf_op jit(solution)/shard_map/ppermute | solution.py:18
  30.5 5.2 %collective-permute-start.10 = (bf16[576,128]{1,0:T(8,128)(2,1)S(1)}, bf16[576,128]{1,0:T(8,128)(2,1)S(1)}, u32[]{:S(2)}, u32[]{:S(2)}) collective-permute-start(bf16[576,128]{1,0:T(8,128)(2,1)S(1)} %shard_map.62.refs_0_), channel_id=1, source_target_pairs={{0,1},{1,0},{2,3},{3,2},{4,5},{5,4},{6,7},{7,6},{8,9},{9,8},{10,11... | collective-permute-start | bytes 442376 | tf_op jit(solution)/shard_map/ppermute | solution.py:18
  37.9 3.3 %collective-permute-start.11 = (f32[24,256]{1,0:T(8,128)S(1)}, f32[24,256]{1,0:T(8,128)S(1)}, u32[]{:S(2)}, u32[]{:S(2)}) collective-permute-start(f32[24,256]{1,0:T(8,128)S(1)} %get-tuple-element.21), channel_id=1, source_target_pairs={{0,24},{8,16},{16,8},{24,0},{1,25},{9,17},{17,9},{25,1},{2,26},{10... | collective-permute-start | bytes 73736 | tf_op jit(solution)/shard_map/ppermute | solution.py:18
  38.0 4.1 %collective-permute-start.12 = (f32[24,256]{1,0:T(8,128)S(1)}, f32[24,256]{1,0:T(8,128)S(1)}, u32[]{:S(2)}, u32[]{:S(2)}) collective-permute-start(f32[24,256]{1,0:T(8,128)S(1)} %get-tuple-element.22), channel_id=1, source_target_pairs={{0,16},{8,24},{16,0},{24,8},{1,17},{9,25},{17,1},{25,9},{2,18},{10... | collective-permute-start | bytes 73736 | tf_op jit(solution)/shard_map/ppermute | solution.py:18
  38.9 3.2 %collective-permute-start.13 = (f32[24,256]{1,0:T(8,128)S(1)}, f32[24,256]{1,0:T(8,128)S(1)}, u32[]{:S(2)}, u32[]{:S(2)}) collective-permute-start(f32[24,256]{1,0:T(8,128)S(1)} %get-tuple-element.23), channel_id=1, source_target_pairs={{0,8},{8,0},{16,24},{24,16},{1,9},{9,1},{17,25},{25,17},{2,10},{10... | collective-permute-start | bytes 73736 | tf_op jit(solution)/shard_map/ppermute | solution.py:18

commit v4 on v3

v4 whole, which is shorter than its diff:
```python
import functools

import jax
import jax.numpy as jnp
from jax import lax
from jax.experimental import pallas as pl
from jax.experimental.pallas import tpu as pltpu
from jax.sharding import PartitionSpec as P

EXTRA_ROWS = 16
WEIGHT_ROWS = 8
MISFIT_ROWS = 8
VMEM_LIMIT = 24 * 1024 * 1024
SMALL_LIMIT = 4 * 1024 * 1024


def swap(value, axis, step):
    return lax.ppermute(value, axis, [(i, i ^ step) for i in range(lax.axis_size(axis))])


def levels(size, vectors):
    near = 1
    while near * near * 4 <= size and near * 2 <= vectors:
        near *= 2
    return near, size // near


def turn_body(start, kernel_ref, out_ref, rows_ref, turned_ref):
    count, points, sensors = out_ref.shape
    rows_ref[...] = kernel_ref[:, :, start : start + count].astype(jnp.float32).reshape(sensors * points, count)
    for p in range(points):
        plane = rows_ref[pl.ds(p, sensors, stride=points), :]
        turned_ref[pl.ds(p, count, stride=points), :] = plane.T
    out_ref[...] = turned_ref[...].reshape(count, points, sensors).astype(jnp.bfloat16)


def forward_body(away, near, far, lags, n_models, n_x, *refs):
    models, xs, refs = refs[:n_models], refs[n_models : n_models + n_x], refs[n_models + n_x :]
    part_steps, points, sensors = xs[0].shape
    steps = part_steps * n_x
    me, j = lax.axis_index("sens"), lax.axis_index("par")
    place, block = j // near, lax.rem(j, near) ^ away
    if away == 0:
        observed_ref, weights_ref, out_ref, all_ref, ut_ref, u_ref, acc_ref, seen_ref, scale_ref, sems = refs
    else:
        out_ref, all_ref, ut_ref, u_ref, acc_ref = refs
    vectors, of_block = all_ref.shape[0], u_ref.shape[0]
    rows = of_block * steps // far
    if away == 0:
        first = (block * far + place) * rows
        fetch_seen = pltpu.make_async_copy(observed_ref.at[me ^ (first // steps)], seen_ref, sems.at[0])
        fetch_scale = pltpu.make_async_copy(weights_ref, scale_ref, sems.at[1])
        fetch_seen.start()
        fetch_scale.start()
    lane = lax.broadcasted_iota(jnp.int32, (points, steps), 1)
    for v in range(vectors):
        ref = models[v * n_models // vectors]
        all_ref[v] = ref[v % ref.shape[0]].astype(jnp.float32)
    for v in range(of_block):
        series = all_ref[block * of_block + v]
        for kl in range(lags):
            moved = series if kl == 0 else jnp.where(lane >= kl, pltpu.roll(series, kl, 1), 0.0)
            ut_ref[v, kl * points : (kl + 1) * points, :] = moved
        u_ref[v] = ut_ref[v].T.astype(jnp.bfloat16)
    for k0 in range(0, steps, 2 * lags):
        left = steps - k0
        x_ref, at = xs[k0 // part_steps], k0 % part_steps
        pair = [x_ref[k : k + lags].reshape(lags * points, sensors) for k in (at, at + lags)]
        some = u_ref[:, :left, :].reshape(of_block * left, lags * points)
        term = jnp.dot(some, jnp.concatenate(pair, axis=1), preferred_element_type=jnp.float32)
        for v in range(of_block):
            at, end = v * steps, (v + 1) * steps
            part = term[v * left : (v + 1) * left]
            if k0 == 0:
                acc_ref[at:end, :] = part[:, :sensors]
            else:
                acc_ref[at + k0 : end, :] += part[:, :sensors]
            acc_ref[at + k0 + lags : end, :] += part[: left - lags, sensors:]
    for b in range(far):
        there = pl.multiple_of((place ^ b) * rows, rows)
        out_ref[b * rows : (b + 1) * rows, :] = acc_ref[pl.ds(there, rows), :].astype(out_ref.dtype)
    if away == 0:
        fetch_seen.wait()
        fetch_scale.wait()
        ut_ref[0, :, :sensors] = seen_ref[...].T
        out_ref[:rows, :] -= ut_ref[0, pl.ds(pl.multiple_of(first % steps, rows), rows), :sensors]
        out_ref[far * rows :, :] = jnp.broadcast_to(scale_ref[...], (WEIGHT_ROWS, sensors))


def middle_body(near, far, own_ref, *refs):
    terms, out_ref, sent = refs[: near - 1], refs[near - 1], refs[near:]
    rows = (own_ref.shape[0] - WEIGHT_ROWS) // far
    for b in range(far):
        part = own_ref[b * rows : (b + 1) * rows, :]
        for term in terms:
            part += term[b * rows : (b + 1) * rows, :].astype(jnp.float32)
        if b == 0:
            out_ref[:rows, :] = part
        else:
            sent[b - 1][...] = part.astype(jnp.bfloat16)
    out_ref[rows:, :] = own_ref[far * rows :, :]


def residual_body(own_ref, *refs):
    terms, out_ref = refs[:-1], refs[-1]
    rows, sensors = terms[0].shape
    mismatch = own_ref[:rows, :]
    for term in terms:
        mismatch += term[...].astype(jnp.float32)
    weighted = own_ref[rows : rows + 1, :] * mismatch
    out_ref[:rows, :] = weighted.astype(jnp.bfloat16)
    squared = jnp.sum(weighted * mismatch, axis=0, keepdims=True)
    high = squared.astype(jnp.bfloat16).astype(jnp.float32)
    rest = squared - high
    middle = rest.astype(jnp.bfloat16).astype(jnp.float32)
    low = rest - middle
    row = lax.broadcasted_iota(jnp.int32, (EXTRA_ROWS, sensors), 0)
    parts = jnp.where(row == 0, high, jnp.where(row == 1, middle, jnp.where(row == 2, low, 0.0)))
    out_ref[rows:, :] = parts.astype(jnp.bfloat16)


def join_body(*refs):
    parts, out_ref = refs[:-1], refs[-1]
    rows = parts[0].shape[0]
    for b, part in enumerate(parts):
        out_ref[b * rows : (b + 1) * rows] = part[...]


def adjoint_terms(block_ref, left_ref, r_ref, all_ref, far, lags, points):
    of_block, _, steps = r_ref.shape
    sensors = all_ref.shape[1]
    rows = of_block * steps // far
    place = lax.axis_index("par") // (lax.axis_size("par") // far)
    for b in range(far):
        there = pl.multiple_of((place ^ b) * rows, rows)
        at = b * (rows + EXTRA_ROWS)
        all_ref[pl.ds(there, rows), :] = block_ref[at : at + rows, :].astype(jnp.float32)
    lane = lax.broadcasted_iota(jnp.int32, (sensors, steps), 1)
    lane_p = lax.broadcasted_iota(jnp.int32, (points, steps), 1)
    for v in range(of_block):
        series = all_ref[v * steps : (v + 1) * steps, :].T
        for d in range(lags):
            moved = series
            if d > 0:
                moved = jnp.where(lane < steps - d, pltpu.roll(series, steps - d, 1), 0.0)
            r_ref[v, d * sensors : (d + 1) * sensors, :] = moved.astype(jnp.bfloat16)
        terms = jnp.dot(left_ref[...], r_ref[v], preferred_element_type=jnp.float32)
        total = terms[:points]
        for c in range(1, steps // lags):
            moved = pltpu.roll(terms[c * points : (c + 1) * points], steps - c * lags, 1)
            total += jnp.where(lane_p < steps - c * lags, moved, 0.0)
        yield v, total


def adjoint_own_body(far, lags, block_ref, *refs):
    xs, (left_ref, own_ref, r_ref, all_ref) = refs[:-4], refs[-4:]
    part_steps, points, sensors = xs[0].shape
    for d in range(lags):
        for c in range(len(xs) * part_steps // lags):
            k = c * lags + d
            left_ref[c * points : (c + 1) * points, d * sensors : (d + 1) * sensors] = xs[k // part_steps][k % part_steps]
    for v, total in adjoint_terms(block_ref, left_ref, r_ref, all_ref, far, lags, points):
        own_ref[v] = total


def adjoint_rest_body(far, lags, own_ref, left_ref, own_block_ref, *refs):
    blocks, (kept_ref, sent_ref, slots_ref, r_ref, all_ref) = refs[:-5], refs[-5:]
    of_block, points, steps = own_ref.shape
    near = len(blocks) + 1
    rows = of_block * steps // far
    block = lax.rem(lax.axis_index("par"), near)
    extra = 0.0
    for ref in (own_block_ref, *blocks):
        for b in range(far):
            at = b * (rows + EXTRA_ROWS) + rows
            extra += ref[at : at + EXTRA_ROWS, :].astype(jnp.float32)
    squared = jnp.full((MISFIT_ROWS, steps), jnp.sum(extra), jnp.float32)
    for v in range(of_block):
        slots_ref[block * of_block + v] = own_ref[v]
    for away, ref in enumerate(blocks, 1):
        for v, total in adjoint_terms(ref, left_ref, r_ref, all_ref, far, lags, points):
            slots_ref[(block ^ away) * of_block + v] = total
    for half, ref in enumerate((kept_ref, sent_ref)):
        for i in range(ref.shape[0]):
            ref[i, :points, :] = slots_ref[2 * i + half]
            ref[i, points:, :] = squared


def fold_body(first_ref, second_ref, kept_ref, sent_ref):
    for half, ref in enumerate((kept_ref, sent_ref)):
        for i in range(ref.shape[0]):
            ref[i] = first_ref[2 * i + half] + second_ref[2 * i + half]


def total_body(scale, first_ref, second_ref, gradient_ref, misfit_ref):
    points = gradient_ref.shape[1]
    total = first_ref[0] + second_ref[0]
    gradient_ref[0] = total[:points]
    misfit_ref[...] = total[points : points + 1, :1] * scale


def call(body, out_shape, operands, limit=SMALL_LIMIT, **options):
    vmem = pl.BlockSpec(memory_space=pltpu.VMEM)
    options.setdefault("in_specs", [vmem] * len(operands))
    return pl.pallas_call(
        body,
        out_shape=out_shape,
        out_specs=jax.tree.map(lambda _: vmem, out_shape),
        compiler_params=pltpu.CompilerParams(vmem_limit_bytes=limit),
        **options,
    )(*operands)


def local(model, kernel, observed, weights):
    n_sens, n_par = lax.axis_size("sens"), lax.axis_size("par")
    sensors, points, steps = kernel.shape
    vectors = n_sens * model.shape[0]
    near, far = levels(n_par, vectors)
    of_block = vectors // near
    lags = 256 // points
    rows = vectors * steps // n_par
    flops = 2 * vectors * sensors * points * steps * steps // near
    cost = pl.CostEstimate(flops=flops, bytes_accessed=2 * kernel.size, transcendentals=0)
    vmem, hbm = pl.BlockSpec(memory_space=pltpu.VMEM), pl.BlockSpec(memory_space=pltpu.HBM)

    def struct(shape, dtype):
        return jax.ShapeDtypeStruct(shape, dtype)

    n_x = max(1, n_sens.bit_length() - 1)
    part_steps = steps // n_x
    held, models, xs = model, [model], []
    for level in range(n_x):
        if level > 0:
            models[1], xs[-1] = lax.optimization_barrier((models[1], xs[-1]))
            held = call(join_body, struct((2 * held.shape[0],) + model.shape[1:], model.dtype), models)
        models = [held, swap(held, "sens", held.shape[0])]
        xs.append(
            call(
                functools.partial(turn_body, level * part_steps),
                struct((part_steps, points, sensors), kernel.dtype),
                (kernel,),
                VMEM_LIMIT,
                scratch_shapes=[
                    pltpu.VMEM((sensors * points, part_steps), jnp.float32),
                    pltpu.VMEM((part_steps * points, sensors), jnp.float32),
                ],
                cost_estimate=pl.CostEstimate(flops=0, bytes_accessed=4 * kernel.size, transcendentals=0),
            )
        )

    def forward(away):
        scratch = [
            pltpu.VMEM((vectors, points, steps), jnp.float32),
            pltpu.VMEM((of_block, lags * points, steps), jnp.float32),
            pltpu.VMEM((of_block, steps, lags * points), jnp.bfloat16),
            pltpu.VMEM((of_block * steps, sensors), jnp.float32),
        ]
        operands = [*models, *xs]
        specs = [vmem] * len(operands)
        if away == 0:
            scratch += [
                pltpu.VMEM((sensors, steps), jnp.float32),
                pltpu.VMEM((1, sensors), jnp.float32),
                pltpu.SemaphoreType.DMA((2,)),
            ]
            operands += [observed, weights[None, :]]
            specs += [hbm] * 2
            out = struct((far * rows + WEIGHT_ROWS, sensors), jnp.float32)
        else:
            out = struct((far * rows, sensors), jnp.bfloat16)
        return call(
            functools.partial(forward_body, away, near, far, lags, len(models), len(xs)),
            out,
            operands,
            VMEM_LIMIT,
            in_specs=specs,
            scratch_shapes=scratch,
            cost_estimate=cost,
        )

    terms = [swap(forward(away), "par", away) for away in range(1, near)]
    own, *sent = call(
        functools.partial(middle_body, near, far),
        [struct((rows + WEIGHT_ROWS, sensors), jnp.float32)] + [struct((rows, sensors), jnp.bfloat16)] * (far - 1),
        (forward(0), *terms),
    )
    terms = [swap(sent[b - 1], "par", b * near) for b in range(far - 1, 0, -1)]
    residual = call(residual_body, struct((rows + EXTRA_ROWS, sensors), jnp.bfloat16), (own, *terms))
    parts = [swap(residual, "par", b * near) for b in range(far - 1, 0, -1)]
    block = call(
        join_body, struct((far * (rows + EXTRA_ROWS), sensors), jnp.bfloat16), (residual, *parts[::-1])
    )
    others = [swap(block, "par", away) for away in range(1, near)]

    scratch = [
        pltpu.VMEM((of_block, lags * sensors, steps), jnp.bfloat16),
        pltpu.VMEM((of_block * steps, sensors), jnp.float32),
    ]
    left, own = call(
        functools.partial(adjoint_own_body, far, lags),
        [
            struct((steps // lags * points, lags * sensors), jnp.bfloat16),
            struct((of_block, points, steps), jnp.float32),
        ],
        (block, *xs),
        VMEM_LIMIT,
        scratch_shapes=scratch,
        cost_estimate=cost,
    )
    pair = [struct((vectors // 2, points + MISFIT_ROWS, steps), jnp.float32)] * 2
    kept, sent = call(
        functools.partial(adjoint_rest_body, far, lags),
        pair,
        (own, left, block, *others),
        VMEM_LIMIT,
        scratch_shapes=[pltpu.VMEM((vectors, points, steps), jnp.float32)] + scratch,
        cost_estimate=cost,
    )
    step = 1
    while kept.shape[0] > 1:
        pair = [struct((kept.shape[0] // 2,) + kept.shape[1:], jnp.float32)] * 2
        kept, sent = call(fold_body, pair, (kept, swap(sent, "sens", step)))
        step *= 2
    entries = vectors * sensors * n_sens * steps
    gradient, misfit = call(
        functools.partial(total_body, 0.5 / entries),
        [struct((1, points, steps), jnp.float32), struct((1, 1), jnp.float32)],
        (kept, swap(sent, "sens", step)),
    )
    return (gradient, misfit[0, 0])


def solution(mesh):
    return jax.shard_map(
        local,
        mesh=mesh,
        in_specs=(P("sens", "par", None), P("sens", "par", None), P(None, "sens", None), P("sens")),
        out_specs=(P("sens", "par", None), P()),
        check_vma=False,
    )
```

time: 42.8 us -> 41.5 us (0.970)
  local copies, waits for them, and re-layouts: 3.12 us -> 1.26 us
  Pallas kernels: 4.45 us -> 6.1 us
  waiting for transfers between devices: 17.2 us -> 15.6 us
    unnamed x7 -> x8, local copies, waits for them, and re-layouts: 3.12 us -> 1.26 us
    pallas_call x6 -> x12, Pallas kernels: 4.45 us -> 6.1 us  [call(): pl.pallas_call(body, out_shape=out_shape, out_specs=jax.tree.map(lambda _...]
    ppermute x14 -> x12, waiting for transfers between devices: 17.2 us -> 15.6 us  [swap(): lax.ppermute(value, axis, [(i, i ^ step) for i in range(lax.axis_size(axi...]
    ppermute x14 -> x12, starting transfers between devices: 17.2 us -> 17.6 us  [swap(): lax.ppermute(value, axis, [(i, i ^ step) for i in range(lax.axis_size(axi...]
  transfers between devices with their start and end apart: 14 -> 12, of which waited for: 10 -> 10; matrix products, arithmetic and copies ran while one was open for 6% -> 0% of each run, Pallas kernels for 0% -> 8%
where the time goes in v4:
time: 41.5 us; the launch traced here: 41.3 us
  starting transfers between devices  17.6 us (42%)
  waiting for transfers between devices  15.6 us (38%)
  Pallas kernels  6.1 us (15%)
  local copies, waits for them, and re-layouts  1.26 us (3%)
  between operations  0.73 us (2%)
    ppermute x12, starting transfers between devices, swap(): lax.ppermute(value, axis, [(i, i ^ step) for i in range(lax.axis_size(axi...  17.6 us
    ppermute x12, waiting for transfers between devices, swap(): lax.ppermute(value, axis, [(i, i ^ step) for i in range(lax.axis_size(axi...  15.6 us
    pallas_call x12, Pallas kernels, call(): pl.pallas_call(body, out_shape=out_shape, out_specs=jax.tree.map(lambda _...  6.1 us
    unnamed x8, local copies, waits for them, and re-layouts  1.26 us
  transfers between devices with their start and end apart: 12, of which 10 were waited for; matrix products, arithmetic and copies ran while one was open for 0% of the time, Pallas kernels for 8%

profile of v4, /device:TPU:0, one launch (start us, length us, event | category | flops | bytes accessed | tf_op | source)
XLA Modules:
  0.0 41.3 jit_solution(14615286012597281498)
XLA Ops:
  0.6 0.5 %collective-permute-start = (bf16[1,16,256]{2,1,0:T(8,128)(2,1)}, bf16[1,16,256]{2,1,0:T(8,128)(2,1)S(1)}, u32[]{:S(2)}, u32[]{:S(2)}) collective-permute-start(bf16[1,16,256]{2,1,0:T(8,128)(2,1)} %refs_0_.1), channel_id=1, source_target_pairs={{0,8},{8,0},{16,24},{24,16},{1,9},{9,1},{17,25},{25,17},{2,10},{10... | collective-permute-start | bytes 24584 | tf_op jit(solution)/shard_map/ppermute | solution.py:18
  1.1 1.2 %copy-done = bf16[128,16,256]{2,1,0:T(8,128)(2,1)S(1)} copy-done((bf16[128,16,256]{2,1,0:T(8,128)(2,1)S(1)}, bf16[128,16,256]{2,1,0:T(8,128)(2,1)}, u32[]{:S(2)}) %copy-start) | copy-done | bytes 1048600
  2.4 0.7 %shard_map.59.refs_2_.refs_0_ = bf16[128,16,128]{2,1,0:T(8,128)(2,1)S(1)} custom-call(bf16[128,16,256]{2,1,0:T(8,128)(2,1)S(1)} %copy-done), custom_call_target="tpu_custom_call" | custom-call | bytes 2097152 | tf_op jit(solution)/shard_map/pallas_call | solution.py:205
  3.0 0.0 copy-done.1
  3.1 2.6 %collective-permute-start.1 = (bf16[2,16,256]{2,1,0:T(8,128)(2,1)S(1)}, bf16[2,16,256]{2,1,0:T(8,128)(2,1)S(1)}, u32[]{:S(2)}, u32[]{:S(2)}) collective-permute-start(bf16[2,16,256]{2,1,0:T(8,128)(2,1)S(1)} %shard_map.60.refs_0_), channel_id=1, source_target_pairs={{0,16},{8,24},{16,0},{24,8},{1,17},{9,25},{17,1},{25,9},{2,18},{10... | collective-permute-start | bytes 49160 | tf_op jit(solution)/shard_map/ppermute | solution.py:18
  5.6 0.6 %shard_map.61.refs_3_.refs_1_ = bf16[128,16,128]{2,1,0:T(8,128)(2,1)S(1)} custom-call(bf16[128,16,256]{2,1,0:T(8,128)(2,1)S(1)} %copy-done), custom_call_target="tpu_custom_call" | custom-call | bytes 2097152 | tf_op jit(solution)/shard_map/pallas_call | solution.py:205
  6.3 0.0 copy-start.2
  6.3 1.0 %collective-permute-done.1.refs_1_ = bf16[2,16,256]{2,1,0:T(8,128)(2,1)S(1)} collective-permute-done((bf16[2,16,256]{2,1,0:T(8,128)(2,1)S(1)}, bf16[2,16,256]{2,1,0:T(8,128)(2,1)S(1)}, u32[]{:S(2)}, u32[]{:S(2)}) %collective-permute-start.1) | collective-permute-done | bytes 16416 | tf_op jit(solution)/shard_map/ppermute | solution.py:18
  7.4 0.7 %shard_map.63 = bf16[512,128]{1,0:T(8,128)(2,1)S(1)} custom-call(bf16[2,16,256]{2,1,0:T(8,128)(2,1)S(1)} %shard_map.60.refs_0_, bf16[2,16,256]{2,1,0:T(8,128)(2,1)S(1)} %collective-permute-done.1.refs_1_, bf16[128,16,128]{2,1,0:T(8,128)(2,1)S(1)} %shard_map.59.refs_2_.refs_0_, bf16[128,16,128]{2,1,0:T(8,128)(2,1)S(1)} %shard_map.61.refs_3_.refs_1_), custom_call_target="tpu_custom_call" | custom-call | flops 536870912 | bytes 1048576 | tf_op jit(solution)/shard_map/pallas_call | solution.py:205
  8.0 0.0 copy-start.3
  8.0 2.1 %collective-permute-start.2 = (bf16[512,128]{1,0:T(8,128)(2,1)S(1)}, bf16[512,128]{1,0:T(8,128)(2,1)S(1)}, u32[]{:S(2)}, u32[]{:S(2)}) collective-permute-start(bf16[512,128]{1,0:T(8,128)(2,1)S(1)} %shard_map.63), channel_id=1, source_target_pairs={{0,1},{1,0},{2,3},{3,2},{4,5},{5,4},{6,7},{7,6},{8,9},{9,8},{10,11... | collective-permute-start | bytes 393224 | tf_op jit(solution)/shard_map/ppermute | solution.py:18
  10.2 1.0 %shard_map.62.own_ref = f32[520,128]{1,0:T(8,128)S(1)} custom-call(bf16[2,16,256]{2,1,0:T(8,128)(2,1)S(1)} %shard_map.60.refs_0_, bf16[2,16,256]{2,1,0:T(8,128)(2,1)S(1)} %collective-permute-done.1.refs_1_, bf16[128,16,128]{2,1,0:T(8,128)(2,1)S(1)} %shard_map.59.refs_2_.refs_0_, bf16[128,16,128]{2,1,0:T(8,128)(2,1)S(1)} %shard_map.61.refs_3_.refs_1_, ...), custom_call_target="tpu_custom_call" | custom-call | flops 536870912 | bytes 1048576 | tf_op jit(solution)/shard_map/pallas_call | solution.py:205
  11.2 2.0 %collective-permute-done.2.refs_0_ = bf16[512,128]{1,0:T(8,128)(2,1)S(1)} collective-permute-done((bf16[512,128]{1,0:T(8,128)(2,1)S(1)}, bf16[512,128]{1,0:T(8,128)(2,1)S(1)}, u32[]{:S(2)}, u32[]{:S(2)}) %collective-permute-start.2) | collective-permute-done | bytes 131104 | tf_op jit(solution)/shard_map/ppermute | solution.py:18
  13.2 4.1 %collective-permute-start.3 = (bf16[128,128]{1,0:T(8,128)(2,1)S(1)}, bf16[128,128]{1,0:T(8,128)(2,1)S(1)}, u32[]{:S(2)}, u32[]{:S(2)}) collective-permute-start(bf16[128,128]{1,0:T(8,128)(2,1)S(1)} %get-tuple-element.19), channel_id=1, source_target_pairs={{0,6},{1,7},{2,4},{3,5},{4,2},{5,3},{6,0},{7,1},{8,14},{9,15},{10,... | collective-permute-start | bytes 98312 | tf_op jit(solution)/shard_map/ppermute | solution.py:18
  17.3 0.6 %collective-permute-start.5 = (bf16[128,128]{1,0:T(8,128)(2,1)S(1)}, bf16[128,128]{1,0:T(8,128)(2,1)S(1)}, u32[]{:S(2)}, u32[]{:S(2)}) collective-permute-start(bf16[128,128]{1,0:T(8,128)(2,1)S(1)} %get-tuple-element.21), channel_id=1, source_target_pairs={{0,2},{1,3},{2,0},{3,1},{4,6},{5,7},{6,4},{7,5},{8,10},{9,11},{10,... | collective-permute-start | bytes 98312 | tf_op jit(solution)/shard_map/ppermute | solution.py:18
  18.0 1.4 %collective-permute-done.3.refs_0_ = bf16[128,128]{1,0:T(8,128)(2,1)S(1)} collective-permute-done((bf16[128,128]{1,0:T(8,128)(2,1)S(1)}, bf16[128,128]{1,0:T(8,128)(2,1)S(1)}, u32[]{:S(2)}, u32[]{:S(2)}) %collective-permute-start.3) | collective-permute-done | bytes 32800 | tf_op jit(solution)/shard_map/ppermute | solution.py:18
  19.3 3.0 %collective-permute-done.4.refs_1_ = bf16[128,128]{1,0:T(8,128)(2,1)S(1)} collective-permute-done((bf16[128,128]{1,0:T(8,128)(2,1)S(1)}, bf16[128,128]{1,0:T(8,128)(2,1)S(1)}, u32[]{:S(2)}, u32[]{:S(2)}) %collective-permute-start.4) | collective-permute-done | bytes 32800 | tf_op jit(solution)/shard_map/ppermute | solution.py:18
  22.4 1.3 %collective-permute-start.8 = (bf16[144,128]{1,0:T(8,128)(2,1)S(1)}, bf16[144,128]{1,0:T(8,128)(2,1)S(1)}, u32[]{:S(2)}, u32[]{:S(2)}) collective-permute-start(bf16[144,128]{1,0:T(8,128)(2,1)S(1)} %shard_map.65.refs_0_), channel_id=1, source_target_pairs={{0,6},{1,7},{2,4},{3,5},{4,2},{5,3},{6,0},{7,1},{8,14},{9,15},{10,... | collective-permute-start | bytes 110600 | tf_op jit(solution)/shard_map/ppermute | solution.py:18
  23.7 0.6 %collective-permute-start.7 = (bf16[144,128]{1,0:T(8,128)(2,1)S(1)}, bf16[144,128]{1,0:T(8,128)(2,1)S(1)}, u32[]{:S(2)}, u32[]{:S(2)}) collective-permute-start(bf16[144,128]{1,0:T(8,128)(2,1)S(1)} %shard_map.65.refs_0_), channel_id=1, source_target_pairs={{0,4},{1,5},{2,6},{3,7},{4,0},{5,1},{6,2},{7,3},{8,12},{9,13},{10,... | collective-permute-start | bytes 110600 | tf_op jit(solution)/shard_map/ppermute | solution.py:18
  24.3 2.5 %collective-permute-start.6 = (bf16[144,128]{1,0:T(8,128)(2,1)S(1)}, bf16[144,128]{1,0:T(8,128)(2,1)S(1)}, u32[]{:S(2)}, u32[]{:S(2)}) collective-permute-start(bf16[144,128]{1,0:T(8,128)(2,1)S(1)} %shard_map.65.refs_0_), channel_id=1, source_target_pairs={{0,2},{1,3},{2,0},{3,1},{4,6},{5,7},{6,4},{7,5},{8,10},{9,11},{10,... | collective-permute-start | bytes 110600 | tf_op jit(solution)/shard_map/ppermute | solution.py:18
  26.8 1.4 %collective-permute-done.8.refs_3_ = bf16[144,128]{1,0:T(8,128)(2,1)S(1)} collective-permute-done((bf16[144,128]{1,0:T(8,128)(2,1)S(1)}, bf16[144,128]{1,0:T(8,128)(2,1)S(1)}, u32[]{:S(2)}, u32[]{:S(2)}) %collective-permute-start.8) | collective-permute-done | bytes 36896 | tf_op jit(solution)/shard_map/ppermute | solution.py:18
  28.2 0.4 %collective-permute-done.7.refs_2_ = bf16[144,128]{1,0:T(8,128)(2,1)S(1)} collective-permute-done((bf16[144,128]{1,0:T(8,128)(2,1)S(1)}, bf16[144,128]{1,0:T(8,128)(2,1)S(1)}, u32[]{:S(2)}, u32[]{:S(2)}) %collective-permute-start.7) | collective-permute-done | bytes 36896 | tf_op jit(solution)/shard_map/ppermute | solution.py:18
  28.6 0.4 collective-permute-done.6.refs_1_
  29.0 1.6 %collective-permute-start.9 = (bf16[576,128]{1,0:T(8,128)(2,1)S(1)}, bf16[576,128]{1,0:T(8,128)(2,1)S(1)}, u32[]{:S(2)}, u32[]{:S(2)}) collective-permute-start(bf16[576,128]{1,0:T(8,128)(2,1)S(1)} %shard_map.66.block_ref.own_block_ref), channel_id=1, source_target_pairs={{0,1},{1,0},{2,3},{3,2},{4,5},{5,4},{6,7},{7,6},{8,9},{9,8},{10,11... | collective-permute-start | bytes 442376 | tf_op jit(solution)/shard_map/ppermute | solution.py:18
  30.6 1.2 %shard_map.67 = (bf16[256,2048]{1,0:T(8,128)(2,1)S(1)}, f32[2,16,256]{2,1,0:T(8,128)S(1)}) custom-call(bf16[576,128]{1,0:T(8,128)(2,1)S(1)} %shard_map.66.block_ref.own_block_ref, bf16[128,16,128]{2,1,0:T(8,128)(2,1)S(1)} %shard_map.59.refs_2_.refs_0_, bf16[128,16,128]{2,1,0:T(8,128)(2,1)S(1)} %shard_map.61.refs_3_.refs_1_), custom_call_target="tpu_custom_call" | custom-call | flops 536870912 | bytes 1048576 | tf_op jit(solution)/shard_map/pallas_call | solution.py:205
  31.8 2.4 %collective-permute-done.9.refs_0_ = bf16[576,128]{1,0:T(8,128)(2,1)S(1)} collective-permute-done((bf16[576,128]{1,0:T(8,128)(2,1)S(1)}, bf16[576,128]{1,0:T(8,128)(2,1)S(1)}, u32[]{:S(2)}, u32[]{:S(2)}) %collective-permute-start.9) | collective-permute-done | bytes 147488 | tf_op jit(solution)/shard_map/ppermute | solution.py:18
  34.2 1.2 %shard_map.68 = (f32[2,24,256]{2,1,0:T(8,128)S(1)}, f32[2,24,256]{2,1,0:T(8,128)S(1)}) custom-call(f32[2,16,256]{2,1,0:T(8,128)S(1)} %get-tuple-element.22.own_ref, bf16[256,2048]{1,0:T(8,128)(2,1)S(1)} %get-tuple-element.23.left_ref, bf16[576,128]{1,0:T(8,128)(2,1)S(1)} %shard_map.66.block_ref.own_block_ref, bf16[576,128]{1,0:T(8,128)(2,1)S(1)} %collective-permute-done.9.refs_0_), custom_call_target="tpu_custom_call" | custom-call | flops 536870912 | bytes 1048576 | tf_op jit(solution)/shard_map/pallas_call | solution.py:205
  35.5 0.1 collective-permute-start.10
  35.6 1.2 %collective-permute-done.10.second_ref = f32[2,24,256]{2,1,0:T(8,128)S(1)} collective-permute-done((f32[2,24,256]{2,1,0:T(8,128)S(1)}, f32[2,24,256]{2,1,0:T(8,128)S(1)}, u32[]{:S(2)}, u32[]{:S(2)}) %collective-permute-start.10) | collective-permute-done | bytes 49184 | tf_op jit(solution)/shard_map/ppermute | solution.py:18
  36.8 1.5 %collective-permute-start.11 = (f32[1,24,256]{2,1,0:T(8,128)S(1)}, f32[1,24,256]{2,1,0:T(8,128)S(1)}, u32[]{:S(2)}, u32[]{:S(2)}) collective-permute-start(f32[1,24,256]{2,1,0:T(8,128)S(1)} %get-tuple-element.27), channel_id=1, source_target_pairs={{0,16},{8,24},{16,0},{24,8},{1,17},{9,25},{17,1},{25,9},{2,18},{10... | collective-permute-start | bytes 73736 | tf_op jit(solution)/shard_map/ppermute | solution.py:18
  38.3 2.3 %collective-permute-done.11.second_ref = f32[1,24,256]{2,1,0:T(8,128)S(1)} collective-permute-done((f32[1,24,256]{2,1,0:T(8,128)S(1)}, f32[1,24,256]{2,1,0:T(8,128)S(1)}, u32[]{:S(2)}, u32[]{:S(2)}) %collective-permute-start.11) | collective-permute-done | bytes 24608 | tf_op jit(solution)/shard_map/ppermute | solution.py:18
  40.7 0.6 %shard_map.70 = (f32[1,16,256]{2,1,0:T(8,128)}, f32[1,1]{1,0:T(1,128)}) custom-call(f32[1,24,256]{2,1,0:T(8,128)S(1)} %get-tuple-element.26.first_ref, f32[1,24,256]{2,1,0:T(8,128)S(1)} %collective-permute-done.11.second_ref), custom_call_target="tpu_custom_call" | custom-call | tf_op jit(solution)/shard_map/pallas_call | solution.py:205
  (12 shorter events, 0.1 us)
Async XLA Ops:
  0.6 2.4 %collective-permute-start = (bf16[1,16,256]{2,1,0:T(8,128)(2,1)}, bf16[1,16,256]{2,1,0:T(8,128)(2,1)S(1)}, u32[]{:S(2)}, u32[]{:S(2)}) collective-permute-start(bf16[1,16,256]{2,1,0:T(8,128)(2,1)} %refs_0_.1), channel_id=1, source_target_pairs={{0,8},{8,0},{16,24},{24,16},{1,9},{9,1},{17,25},{25,17},{2,10},{10... | collective-permute-start | bytes 24584 | tf_op jit(solution)/shard_map/ppermute | solution.py:18
  1.1 1.2 %copy-start = (bf16[128,16,256]{2,1,0:T(8,128)(2,1)S(1)}, bf16[128,16,256]{2,1,0:T(8,128)(2,1)}, u32[]{:S(2)}) copy-start(bf16[128,16,256]{2,1,0:T(8,128)(2,1)} %kernel_ref.3) | copy-start | bytes 3145732
  2.4 0.7 %copy-start.1 = (bf16[1,16,256]{2,1,0:T(8,128)(2,1)S(1)}, bf16[1,16,256]{2,1,0:T(8,128)(2,1)}, u32[]{:S(2)}) copy-start(bf16[1,16,256]{2,1,0:T(8,128)(2,1)} %refs_0_.1) | copy-start | bytes 24580
  3.1 4.3 %collective-permute-start.1 = (bf16[2,16,256]{2,1,0:T(8,128)(2,1)S(1)}, bf16[2,16,256]{2,1,0:T(8,128)(2,1)S(1)}, u32[]{:S(2)}, u32[]{:S(2)}) collective-permute-start(bf16[2,16,256]{2,1,0:T(8,128)(2,1)S(1)} %shard_map.60.refs_0_), channel_id=1, source_target_pairs={{0,16},{8,24},{16,0},{24,8},{1,17},{9,25},{17,1},{25,9},{2,18},{10... | collective-permute-start | bytes 49160 | tf_op jit(solution)/shard_map/ppermute | solution.py:18
  6.3 3.9 %copy-start.2 = (f32[4,128,256]{2,1,0:T(8,128)S(1)}, f32[4,128,256]{2,1,0:T(8,128)}, u32[]{:S(2)}) copy-start(f32[4,128,256]{2,1,0:T(8,128)} %refs_4_.1) | copy-start | bytes 1572868
  8.0 2.1 %copy-start.3 = (f32[128]{0:T(128)S(1)}, f32[128]{0:T(128)}, u32[]{:S(2)}) copy-start(f32[128]{0:T(128)} %param.7) | copy-start | bytes 1540
  8.0 5.1 %collective-permute-start.2 = (bf16[512,128]{1,0:T(8,128)(2,1)S(1)}, bf16[512,128]{1,0:T(8,128)(2,1)S(1)}, u32[]{:S(2)}, u32[]{:S(2)}) collective-permute-start(bf16[512,128]{1,0:T(8,128)(2,1)S(1)} %shard_map.63), channel_id=1, source_target_pairs={{0,1},{1,0},{2,3},{3,2},{4,5},{5,4},{6,7},{7,6},{8,9},{9,8},{10,11... | collective-permute-start | bytes 393224 | tf_op jit(solution)/shard_map/ppermute | solution.py:18
  13.2 6.1 %collective-permute-start.3 = (bf16[128,128]{1,0:T(8,128)(2,1)S(1)}, bf16[128,128]{1,0:T(8,128)(2,1)S(1)}, u32[]{:S(2)}, u32[]{:S(2)}) collective-permute-start(bf16[128,128]{1,0:T(8,128)(2,1)S(1)} %get-tuple-element.19), channel_id=1, source_target_pairs={{0,6},{1,7},{2,4},{3,5},{4,2},{5,3},{6,0},{7,1},{8,14},{9,15},{10,... | collective-permute-start | bytes 98312 | tf_op jit(solution)/shard_map/ppermute | solution.py:18
  17.3 5.0 %collective-permute-start.4 = (bf16[128,128]{1,0:T(8,128)(2,1)S(1)}, bf16[128,128]{1,0:T(8,128)(2,1)S(1)}, u32[]{:S(2)}, u32[]{:S(2)}) collective-permute-start(bf16[128,128]{1,0:T(8,128)(2,1)S(1)} %get-tuple-element.20), channel_id=1, source_target_pairs={{0,4},{1,5},{2,6},{3,7},{4,0},{5,1},{6,2},{7,3},{8,12},{9,13},{10,... | collective-permute-start | bytes 98312 | tf_op jit(solution)/shard_map/ppermute | solution.py:18
  17.3 5.0 %collective-permute-start.5 = (bf16[128,128]{1,0:T(8,128)(2,1)S(1)}, bf16[128,128]{1,0:T(8,128)(2,1)S(1)}, u32[]{:S(2)}, u32[]{:S(2)}) collective-permute-start(bf16[128,128]{1,0:T(8,128)(2,1)S(1)} %get-tuple-element.21), channel_id=1, source_target_pairs={{0,2},{1,3},{2,0},{3,1},{4,6},{5,7},{6,4},{7,5},{8,10},{9,11},{10,... | collective-permute-start | bytes 98312 | tf_op jit(solution)/shard_map/ppermute | solution.py:18
  22.4 5.8 %collective-permute-start.8 = (bf16[144,128]{1,0:T(8,128)(2,1)S(1)}, bf16[144,128]{1,0:T(8,128)(2,1)S(1)}, u32[]{:S(2)}, u32[]{:S(2)}) collective-permute-start(bf16[144,128]{1,0:T(8,128)(2,1)S(1)} %shard_map.65.refs_0_), channel_id=1, source_target_pairs={{0,6},{1,7},{2,4},{3,5},{4,2},{5,3},{6,0},{7,1},{8,14},{9,15},{10,... | collective-permute-start | bytes 110600 | tf_op jit(solution)/shard_map/ppermute | solution.py:18
  23.7 4.9 %collective-permute-start.7 = (bf16[144,128]{1,0:T(8,128)(2,1)S(1)}, bf16[144,128]{1,0:T(8,128)(2,1)S(1)}, u32[]{:S(2)}, u32[]{:S(2)}) collective-permute-start(bf16[144,128]{1,0:T(8,128)(2,1)S(1)} %shard_map.65.refs_0_), channel_id=1, source_target_pairs={{0,4},{1,5},{2,6},{3,7},{4,0},{5,1},{6,2},{7,3},{8,12},{9,13},{10,... | collective-permute-start | bytes 110600 | tf_op jit(solution)/shard_map/ppermute | solution.py:18
  24.3 4.7 %collective-permute-start.6 = (bf16[144,128]{1,0:T(8,128)(2,1)S(1)}, bf16[144,128]{1,0:T(8,128)(2,1)S(1)}, u32[]{:S(2)}, u32[]{:S(2)}) collective-permute-start(bf16[144,128]{1,0:T(8,128)(2,1)S(1)} %shard_map.65.refs_0_), channel_id=1, source_target_pairs={{0,2},{1,3},{2,0},{3,1},{4,6},{5,7},{6,4},{7,5},{8,10},{9,11},{10,... | collective-permute-start | bytes 110600 | tf_op jit(solution)/shard_map/ppermute | solution.py:18
  29.0 5.2 %collective-permute-start.9 = (bf16[576,128]{1,0:T(8,128)(2,1)S(1)}, bf16[576,128]{1,0:T(8,128)(2,1)S(1)}, u32[]{:S(2)}, u32[]{:S(2)}) collective-permute-start(bf16[576,128]{1,0:T(8,128)(2,1)S(1)} %shard_map.66.block_ref.own_block_ref), channel_id=1, source_target_pairs={{0,1},{1,0},{2,3},{3,2},{4,5},{5,4},{6,7},{7,6},{8,9},{9,8},{10,11... | collective-permute-start | bytes 442376 | tf_op jit(solution)/shard_map/ppermute | solution.py:18
  35.5 1.3 %collective-permute-start.10 = (f32[2,24,256]{2,1,0:T(8,128)S(1)}, f32[2,24,256]{2,1,0:T(8,128)S(1)}, u32[]{:S(2)}, u32[]{:S(2)}) collective-permute-start(f32[2,24,256]{2,1,0:T(8,128)S(1)} %get-tuple-element.25), channel_id=1, source_target_pairs={{0,8},{8,0},{16,24},{24,16},{1,9},{9,1},{17,25},{25,17},{2,10},{10... | collective-permute-start | bytes 147464 | tf_op jit(solution)/shard_map/ppermute | solution.py:18
  36.8 3.9 %collective-permute-start.11 = (f32[1,24,256]{2,1,0:T(8,128)S(1)}, f32[1,24,256]{2,1,0:T(8,128)S(1)}, u32[]{:S(2)}, u32[]{:S(2)}) collective-permute-start(f32[1,24,256]{2,1,0:T(8,128)S(1)} %get-tuple-element.27), channel_id=1, source_target_pairs={{0,16},{8,24},{16,0},{24,8},{1,17},{9,25},{17,1},{25,9},{2,18},{10... | collective-permute-start | bytes 73736 | tf_op jit(solution)/shard_map/ppermute | solution.py:18

commit v5 on v4

v5 whole, which is shorter than its diff:
```python
import functools

import jax
import jax.numpy as jnp
from jax import lax
from jax.experimental import pallas as pl
from jax.experimental.pallas import tpu as pltpu
from jax.sharding import PartitionSpec as P

EXTRA_ROWS = 16
WEIGHT_ROWS = 8
MISFIT_ROWS = 8
VMEM_LIMIT = 24 * 1024 * 1024
SMALL_LIMIT = 4 * 1024 * 1024


def swap(value, axis, step):
    return lax.ppermute(value, axis, [(i, i ^ step) for i in range(lax.axis_size(axis))])


def levels(size, vectors):
    near = 1
    while near * near * 4 <= size and near * 2 <= vectors:
        near *= 2
    return near, size // near


def turn_body(kernel_ref, out_ref, turned_ref, *parts):
    steps, points, sensors = out_ref.shape
    count = steps // len(parts)
    for i, rows_ref in enumerate(parts):
        lags = slice(i * count, (i + 1) * count)
        rows_ref[...] = kernel_ref[:, :, lags].astype(jnp.float32).reshape(sensors * points, count)
        for p in range(points):
            plane = rows_ref[pl.ds(p, sensors, stride=points), :]
            turned_ref[pl.ds(i * count * points + p, count, stride=points), :] = plane.T
        turned = turned_ref[i * count * points : (i + 1) * count * points, :]
        out_ref[lags] = turned.reshape(count, points, sensors).astype(jnp.bfloat16)


def forward_body(away, near, far, lags, n_models, n_x, *refs):
    models, xs, refs = refs[:n_models], refs[n_models : n_models + n_x], refs[n_models + n_x :]
    part_steps, points, sensors = xs[0].shape
    steps = part_steps * n_x
    me, j = lax.axis_index("sens"), lax.axis_index("par")
    place, block = j // near, lax.rem(j, near) ^ away
    if away == 0:
        observed_ref, weights_ref, out_ref, all_ref, ut_ref, u_ref, acc_ref, seen_ref, scale_ref, sems = refs
        outs = [out_ref]
    else:
        outs, (all_ref, ut_ref, u_ref, acc_ref) = refs[:-4], refs[-4:]
    vectors, of_block = all_ref.shape[0], u_ref.shape[0]
    rows = of_block * steps // far
    if away == 0:
        first = (block * far + place) * rows
        fetch_seen = pltpu.make_async_copy(observed_ref.at[me ^ (first // steps)], seen_ref, sems.at[0])
        fetch_scale = pltpu.make_async_copy(weights_ref, scale_ref, sems.at[1])
        fetch_seen.start()
        fetch_scale.start()
    lane = lax.broadcasted_iota(jnp.int32, (points, steps), 1)
    for v in range(vectors):
        ref = models[v * n_models // vectors]
        all_ref[v] = ref[v % ref.shape[0]].astype(jnp.float32)
    for v in range(of_block):
        series = all_ref[block * of_block + v]
        for kl in range(lags):
            moved = series if kl == 0 else jnp.where(lane >= kl, pltpu.roll(series, kl, 1), 0.0)
            ut_ref[v, kl * points : (kl + 1) * points, :] = moved
        u_ref[v] = ut_ref[v].T.astype(jnp.bfloat16)
    for k0 in range(0, steps, 2 * lags):
        left = steps - k0
        x_ref, at = xs[k0 // part_steps], k0 % part_steps
        pair = [x_ref[k : k + lags].reshape(lags * points, sensors) for k in (at, at + lags)]
        some = u_ref[:, :left, :].reshape(of_block * left, lags * points)
        term = jnp.dot(some, jnp.concatenate(pair, axis=1), preferred_element_type=jnp.float32)
        for v in range(of_block):
            at, end = v * steps, (v + 1) * steps
            part = term[v * left : (v + 1) * left]
            if k0 == 0:
                acc_ref[at:end, :] = part[:, :sensors]
            else:
                acc_ref[at + k0 : end, :] += part[:, :sensors]
            acc_ref[at + k0 + lags : end, :] += part[: left - lags, sensors:]
    for b in range(far):
        there = pl.multiple_of((place ^ b) * rows, rows)
        ref, at = outs[b * len(outs) // far], b % (far // len(outs)) * rows
        ref[at : at + rows, :] = acc_ref[pl.ds(there, rows), :].astype(ref.dtype)
    if away == 0:
        fetch_seen.wait()
        fetch_scale.wait()
        ut_ref[0, :, :sensors] = seen_ref[...].T
        out_ref[:rows, :] -= ut_ref[0, pl.ds(pl.multiple_of(first % steps, rows), rows), :sensors]
        out_ref[far * rows :, :] = jnp.broadcast_to(scale_ref[...], (WEIGHT_ROWS, sensors))


def middle_body(near, start, count, own_ref, *refs):
    terms, outs = refs[: near - 1], refs[near - 1 :]
    rows = terms[0].shape[0] // count
    for i, ref in enumerate(outs):
        part = own_ref[(start + i) * rows : (start + i + 1) * rows, :]
        for term in terms:
            part += term[i * rows : (i + 1) * rows, :].astype(jnp.float32)
        ref[:rows, :] = part.astype(ref.dtype)
    if start == 0:
        outs[0][rows:, :] = own_ref[own_ref.shape[0] - WEIGHT_ROWS :, :]


def three_parts(value):
    high = value.astype(jnp.bfloat16).astype(jnp.float32)
    rest = value - high
    middle = rest.astype(jnp.bfloat16).astype(jnp.float32)
    low = rest - middle
    row = lax.broadcasted_iota(jnp.int32, (EXTRA_ROWS, value.shape[1]), 0)
    parts = jnp.where(row == 0, high, jnp.where(row == 1, middle, jnp.where(row == 2, low, 0.0)))
    return parts.astype(jnp.bfloat16)


def residual_body(own_ref, *refs):
    terms, out_ref = refs[:-1], refs[-1]
    rows, sensors = terms[0].shape
    mismatch = own_ref[:rows, :]
    for term in terms:
        mismatch += term[...].astype(jnp.float32)
    weighted = own_ref[rows : rows + 1, :] * mismatch
    out_ref[:rows, :] = weighted.astype(jnp.bfloat16)
    squared = jnp.sum(weighted * mismatch, axis=0, keepdims=True)
    out_ref[rows:, :] = three_parts(squared)


def join_body(*refs):
    parts, out_ref = refs[:-1], refs[-1]
    rows = parts[0].shape[0] - EXTRA_ROWS
    extra = 0.0
    for i, part in enumerate(parts):
        out_ref[i * rows : (i + 1) * rows, :] = part[:rows, :]
        extra += part[rows:, :].astype(jnp.float32)
    out_ref[len(parts) * rows :, :] = three_parts(jnp.sum(extra, axis=0, keepdims=True))


def adjoint_terms(groups, left_ref, r_ref, all_ref, far, lags, points):
    of_block, _, steps = r_ref.shape
    sensors = all_ref.shape[1]
    rows = of_block * steps // far
    place = lax.axis_index("par") // (lax.axis_size("par") // far)
    for b in range(far):
        there = pl.multiple_of((place ^ b) * rows, rows)
        ref, at = groups[b * len(groups) // far], b % (far // len(groups)) * rows
        all_ref[pl.ds(there, rows), :] = ref[at : at + rows, :].astype(jnp.float32)
    lane = lax.broadcasted_iota(jnp.int32, (sensors, steps), 1)
    lane_p = lax.broadcasted_iota(jnp.int32, (points, steps), 1)
    for v in range(of_block):
        series = all_ref[v * steps : (v + 1) * steps, :].T
        for d in range(lags):
            moved = series
            if d > 0:
                moved = jnp.where(lane < steps - d, pltpu.roll(series, steps - d, 1), 0.0)
            r_ref[v, d * sensors : (d + 1) * sensors, :] = moved.astype(jnp.bfloat16)
        terms = jnp.dot(left_ref[...], r_ref[v], preferred_element_type=jnp.float32)
        total = terms[:points]
        for c in range(1, steps // lags):
            moved = pltpu.roll(terms[c * points : (c + 1) * points], steps - c * lags, 1)
            total += jnp.where(lane_p < steps - c * lags, moved, 0.0)
        yield v, total


def adjoint_own_body(far, lags, n_groups, *refs):
    groups, xs, (left_ref, own_ref, r_ref, all_ref) = refs[:n_groups], refs[n_groups:-4], refs[-4:]
    part_steps, points, sensors = xs[0].shape
    for d in range(lags):
        for c in range(len(xs) * part_steps // lags):
            k = c * lags + d
            left_ref[c * points : (c + 1) * points, d * sensors : (d + 1) * sensors] = xs[k // part_steps][k % part_steps]
    for v, total in adjoint_terms(groups, left_ref, r_ref, all_ref, far, lags, points):
        own_ref[v] = total


def adjoint_rest_body(near, far, lags, n_groups, own_ref, left_ref, *refs):
    groups, outs, (slots_ref, r_ref, all_ref) = refs[: near * n_groups], refs[near * n_groups : -3], refs[-3:]
    of_block, points, steps = own_ref.shape
    lanes = outs[0].shape[1]
    block = lax.rem(lax.axis_index("par"), near)
    extra = 0.0
    for ref in groups:
        extra += ref[ref.shape[0] - EXTRA_ROWS :, :].astype(jnp.float32)
    squared = jnp.full((MISFIT_ROWS, lanes), jnp.sum(extra), jnp.float32)
    for v in range(of_block):
        slots_ref[block * of_block + v] = own_ref[v]
    for away in range(1, near):
        some = groups[away * n_groups : (away + 1) * n_groups]
        for v, total in adjoint_terms(some, left_ref, r_ref, all_ref, far, lags, points):
            slots_ref[(block ^ away) * of_block + v] = total
    for v, ref in enumerate(outs):
        for i in range(steps // lanes):
            ref[i * points : (i + 1) * points, :] = slots_ref[v, :, i * lanes : (i + 1) * lanes]
        ref[steps // lanes * points :, :] = squared


def total_body(scale, *refs):
    terms, (gradient_ref, misfit_ref) = refs[:-2], refs[-2:]
    _, points, steps = gradient_ref.shape
    lanes = terms[0].shape[1]
    total = terms[0][...]
    for term in terms[1:]:
        total += term[...]
    for i in range(steps // lanes):
        gradient_ref[0, :, i * lanes : (i + 1) * lanes] = total[i * points : (i + 1) * points]
    at = steps // lanes * points
    misfit_ref[...] = total[at : at + 1, :1] * scale


def call(body, out_shape, operands, limit=SMALL_LIMIT, **options):
    vmem = pl.BlockSpec(memory_space=pltpu.VMEM)
    options.setdefault("in_specs", [vmem] * len(operands))
    return pl.pallas_call(
        body,
        out_shape=out_shape,
        out_specs=jax.tree.map(lambda _: vmem, out_shape),
        compiler_params=pltpu.CompilerParams(vmem_limit_bytes=limit),
        **options,
    )(*operands)


def local(model, kernel, observed, weights):
    n_sens, n_par = lax.axis_size("sens"), lax.axis_size("par")
    sensors, points, steps = kernel.shape
    vectors = n_sens * model.shape[0]
    near, far = levels(n_par, vectors)
    of_block = vectors // near
    n_groups = min(2, far)
    slots = far // n_groups
    lags = 256 // points
    rows = vectors * steps // n_par
    lanes = min(128, steps)
    flops = 2 * vectors * sensors * points * steps * steps // near
    cost = pl.CostEstimate(flops=flops, bytes_accessed=2 * kernel.size, transcendentals=0)
    vmem, hbm = pl.BlockSpec(memory_space=pltpu.VMEM), pl.BlockSpec(memory_space=pltpu.HBM)

    def struct(shape, dtype):
        return jax.ShapeDtypeStruct(shape, dtype)

    models = [model] + [swap(model, "sens", step) for step in range(1, n_sens)]
    xs = [
        call(
            turn_body,
            struct((steps, points, sensors), kernel.dtype),
            (kernel,),
            VMEM_LIMIT,
            scratch_shapes=[
                pltpu.VMEM((steps * points, sensors), jnp.float32),
            ]
            + [pltpu.VMEM((sensors * points, lanes), jnp.float32)] * (steps // lanes),
            cost_estimate=pl.CostEstimate(flops=0, bytes_accessed=6 * kernel.size, transcendentals=0),
        )
    ]

    def forward(away):
        scratch = [
            pltpu.VMEM((vectors, points, steps), jnp.float32),
            pltpu.VMEM((of_block, lags * points, steps), jnp.float32),
            pltpu.VMEM((of_block, steps, lags * points), jnp.bfloat16),
            pltpu.VMEM((of_block * steps, sensors), jnp.float32),
        ]
        operands = [*models, *xs]
        specs = [vmem] * len(operands)
        if away == 0:
            scratch += [
                pltpu.VMEM((sensors, steps), jnp.float32),
                pltpu.VMEM((1, sensors), jnp.float32),
                pltpu.SemaphoreType.DMA((2,)),
            ]
            operands += [observed, weights[None, :]]
            specs += [hbm] * 2
            out = struct((far * rows + WEIGHT_ROWS, sensors), jnp.float32)
        else:
            out = [struct((slots * rows, sensors), jnp.bfloat16)] * n_groups
        return call(
            functools.partial(forward_body, away, near, far, lags, len(models), len(xs)),
            out,
            operands,
            VMEM_LIMIT,
            in_specs=specs,
            scratch_shapes=scratch,
            cost_estimate=cost,
        )

    sent = [forward(away) for away in range(1, near)]
    crossed = [[swap(some[g], "par", away) for away, some in enumerate(sent, 1)] for g in range(n_groups - 1, -1, -1)]
    sums = forward(0)
    terms = []
    for g, some in zip(range(n_groups - 1, -1, -1), crossed):
        outs = [struct((rows, sensors), jnp.bfloat16)] * slots
        if g == 0:
            outs[0] = struct((rows + WEIGHT_ROWS, sensors), jnp.float32)
        outs = call(functools.partial(middle_body, near, g * slots, slots), outs, (sums, *some))
        if g == 0:
            own, *outs = outs
        first = far - len(terms) - 1
        terms += [swap(out, "par", b * near) for b, out in zip(range(first, 0, -1), outs[::-1])]
    residual = call(residual_body, struct((rows + EXTRA_ROWS, sensors), jnp.bfloat16), (own, *terms))
    parts = [residual] + [swap(residual, "par", b * near) for b in range(1, far)]
    joined = struct((slots * rows + EXTRA_ROWS, sensors), jnp.bfloat16)
    groups = [call(join_body, joined, parts[g * slots : (g + 1) * slots]) for g in range(n_groups)]
    others = [[swap(group, "par", away) for group in groups] for away in range(1, near)]

    scratch = [
        pltpu.VMEM((of_block, lags * sensors, steps), jnp.bfloat16),
        pltpu.VMEM((of_block * steps, sensors), jnp.float32),
    ]
    left, own = call(
        functools.partial(adjoint_own_body, far, lags, n_groups),
        [
            struct((steps // lags * points, lags * sensors), jnp.bfloat16),
            struct((of_block, points, steps), jnp.float32),
        ],
        (*groups, *xs),
        VMEM_LIMIT,
        scratch_shapes=scratch,
        cost_estimate=cost,
    )
    partials = call(
        functools.partial(adjoint_rest_body, near, far, lags, n_groups),
        [struct((steps // lanes * points + MISFIT_ROWS, lanes), jnp.float32)] * vectors,
        (own, left, *groups, *[group for some in others for group in some]),
        VMEM_LIMIT,
        scratch_shapes=[pltpu.VMEM((vectors, points, steps), jnp.float32)] + scratch,
        cost_estimate=cost,
    )
    received = [swap(partials[step], "sens", step) for step in range(n_sens - 1, 0, -1)]
    entries = vectors * sensors * n_sens * steps
    gradient, misfit = call(
        functools.partial(total_body, 0.5 / entries),
        [struct((1, points, steps), jnp.float32), struct((1, 1), jnp.float32)],
        (partials[0], *received),
    )
    return (gradient, misfit[0, 0])


def solution(mesh):
    return jax.shard_map(
        local,
        mesh=mesh,
        in_specs=(P("sens", "par", None), P("sens", "par", None), P(None, "sens", None), P("sens")),
        out_specs=(P("sens", "par", None), P()),
        check_vma=False,
    )
```

time: 41.5 us -> 40 us (0.964)
  waiting for transfers between devices: 15.6 us -> 13.4 us
  starting transfers between devices: 17.6 us -> 18.1 us
    ppermute x12 -> x16, waiting for transfers between devices: 15.6 us -> 13.4 us  [swap(): lax.ppermute(value, axis, [(i, i ^ step) for i in range(lax.axis_size(axi...]
    ppermute x12 -> x16, starting transfers between devices: 17.6 us -> 18.1 us  [swap(): lax.ppermute(value, axis, [(i, i ^ step) for i in range(lax.axis_size(axi...]
    pallas_call x12 -> x11, Pallas kernels: 6.1 us -> 6.2 us  [call(): pl.pallas_call(body, out_shape=out_shape, out_specs=jax.tree.map(lambda _...]
  transfers between devices with their start and end apart: 12 -> 16, of which waited for: 10 -> 10; matrix products, arithmetic and copies ran while one was open for 0% -> 0% of each run, Pallas kernels for 8% -> 9%
where the time goes in v5:
time: 40 us; the launch traced here: 39.8 us
  starting transfers between devices  18.1 us (45%)
  waiting for transfers between devices  13.4 us (34%)
  Pallas kernels  6.2 us (16%)
  local copies, waits for them, and re-layouts  1.38 us (3%)
  between operations  0.73 us (2%)
    ppermute x16, starting transfers between devices, swap(): lax.ppermute(value, axis, [(i, i ^ step) for i in range(lax.axis_size(axi...  18.1 us
    ppermute x16, waiting for transfers between devices, swap(): lax.ppermute(value, axis, [(i, i ^ step) for i in range(lax.axis_size(axi...  13.4 us
    pallas_call x11, Pallas kernels, call(): pl.pallas_call(body, out_shape=out_shape, out_specs=jax.tree.map(lambda _...  6.2 us
    unnamed x8, local copies, waits for them, and re-layouts  1.38 us
  transfers between devices with their start and end apart: 16, of which 10 were waited for; matrix products, arithmetic and copies ran while one was open for 0% of the time, Pallas kernels for 9%

profile of v5, /device:TPU:0, one launch (start us, length us, event | category | flops | bytes accessed | tf_op | source)
XLA Modules:
  0.0 39.8 jit_solution(14753215041319221314)
XLA Ops:
  0.6 2.4 %collective-permute-start.2 = (bf16[1,16,256]{2,1,0:T(8,128)(2,1)}, bf16[1,16,256]{2,1,0:T(8,128)(2,1)S(1)}, u32[]{:S(2)}, u32[]{:S(2)}) collective-permute-start(bf16[1,16,256]{2,1,0:T(8,128)(2,1)} %refs_0_.3), channel_id=1, source_target_pairs={{0,24},{8,16},{16,8},{24,0},{1,25},{9,17},{17,9},{25,1},{2,26},{10... | collective-permute-start | bytes 24584 | tf_op jit(solution)/shard_map/ppermute | solution.py:18
  3.1 0.6 %collective-permute-start.1 = (bf16[1,16,256]{2,1,0:T(8,128)(2,1)}, bf16[1,16,256]{2,1,0:T(8,128)(2,1)S(1)}, u32[]{:S(2)}, u32[]{:S(2)}) collective-permute-start(bf16[1,16,256]{2,1,0:T(8,128)(2,1)} %refs_0_.3), channel_id=1, source_target_pairs={{0,16},{8,24},{16,0},{24,8},{1,17},{9,25},{17,1},{25,9},{2,18},{10... | collective-permute-start | bytes 24584 | tf_op jit(solution)/shard_map/ppermute | solution.py:18
  3.7 0.0 collective-permute-start
  3.8 1.2 %copy-done = bf16[128,16,256]{2,1,0:T(8,128)(2,1)S(1)} copy-done((bf16[128,16,256]{2,1,0:T(8,128)(2,1)S(1)}, bf16[128,16,256]{2,1,0:T(8,128)(2,1)}, u32[]{:S(2)}) %copy-start) | copy-done | bytes 1048600
  5.0 1.3 %shard_map.59.refs_4_.refs_2_ = bf16[256,16,128]{2,1,0:T(8,128)(2,1)S(1)} custom-call(bf16[128,16,256]{2,1,0:T(8,128)(2,1)S(1)} %copy-done), custom_call_target="tpu_custom_call" | custom-call | bytes 3145728 | tf_op jit(solution)/shard_map/pallas_call | solution.py:214
  6.3 0.6 %collective-permute-done.1.refs_2_ = bf16[1,16,256]{2,1,0:T(8,128)(2,1)S(1)} collective-permute-done((bf16[1,16,256]{2,1,0:T(8,128)(2,1)}, bf16[1,16,256]{2,1,0:T(8,128)(2,1)S(1)}, u32[]{:S(2)}, u32[]{:S(2)}) %collective-permute-start.1) | collective-permute-done | bytes 8224 | tf_op jit(solution)/shard_map/ppermute | solution.py:18
  6.9 0.7 %shard_map.61 = (bf16[256,128]{1,0:T(8,128)(2,1)S(1)}, bf16[256,128]{1,0:T(8,128)(2,1)S(1)}) custom-call(bf16[1,16,256]{2,1,0:T(8,128)(2,1)S(1)} %copy-done.2, bf16[1,16,256]{2,1,0:T(8,128)(2,1)S(1)} %collective-permute-done.refs_1_, bf16[1,16,256]{2,1,0:T(8,128)(2,1)S(1)} %collective-permute-done.1.refs_2_, ...), custom_call_target="tpu_custom_call" | custom-call | flops 536870912 | bytes 1048576 | tf_op jit(solution)/shard_map/pallas_call | solution.py:214
  7.6 1.6 %collective-permute-start.4 = (bf16[256,128]{1,0:T(8,128)(2,1)S(1)}, bf16[256,128]{1,0:T(8,128)(2,1)S(1)}, u32[]{:S(2)}, u32[]{:S(2)}) collective-permute-start(bf16[256,128]{1,0:T(8,128)(2,1)S(1)} %get-tuple-element.18), channel_id=1, source_target_pairs={{0,1},{1,0},{2,3},{3,2},{4,5},{5,4},{6,7},{7,6},{8,9},{9,8},{10,11... | collective-permute-start | bytes 196616 | tf_op jit(solution)/shard_map/ppermute | solution.py:18
  9.2 0.5 %collective-permute-start.3 = (bf16[256,128]{1,0:T(8,128)(2,1)S(1)}, bf16[256,128]{1,0:T(8,128)(2,1)S(1)}, u32[]{:S(2)}, u32[]{:S(2)}) collective-permute-start(bf16[256,128]{1,0:T(8,128)(2,1)S(1)} %get-tuple-element.16), channel_id=1, source_target_pairs={{0,1},{1,0},{2,3},{3,2},{4,5},{5,4},{6,7},{7,6},{8,9},{9,8},{10,11... | collective-permute-start | bytes 196616 | tf_op jit(solution)/shard_map/ppermute | solution.py:18
  9.7 0.1 copy-done.3
  9.9 1.0 %shard_map.60.own_ref = f32[520,128]{1,0:T(8,128)S(1)} custom-call(bf16[1,16,256]{2,1,0:T(8,128)(2,1)S(1)} %copy-done.2, bf16[1,16,256]{2,1,0:T(8,128)(2,1)S(1)} %collective-permute-done.refs_1_, bf16[1,16,256]{2,1,0:T(8,128)(2,1)S(1)} %collective-permute-done.1.refs_2_, bf16[1,16,256]{2,1,0:T(8,128)(2,1)S(1)} %collective-permute-done.2.refs_3_, ...), custom_call_target="tpu_custom_call" | custom-call | flops 536870912 | bytes 1048576 | tf_op jit(solution)/shard_map/pallas_call | solution.py:214
  10.8 1.7 %collective-permute-done.4.refs_0_ = bf16[256,128]{1,0:T(8,128)(2,1)S(1)} collective-permute-done((bf16[256,128]{1,0:T(8,128)(2,1)S(1)}, bf16[256,128]{1,0:T(8,128)(2,1)S(1)}, u32[]{:S(2)}, u32[]{:S(2)}) %collective-permute-start.4) | collective-permute-done | bytes 65568 | tf_op jit(solution)/shard_map/ppermute | solution.py:18
  12.5 3.7 %collective-permute-start.5 = (bf16[128,128]{1,0:T(8,128)(2,1)S(1)}, bf16[128,128]{1,0:T(8,128)(2,1)S(1)}, u32[]{:S(2)}, u32[]{:S(2)}) collective-permute-start(bf16[128,128]{1,0:T(8,128)(2,1)S(1)} %get-tuple-element.19), channel_id=1, source_target_pairs={{0,6},{1,7},{2,4},{3,5},{4,2},{5,3},{6,0},{7,1},{8,14},{9,15},{10,... | collective-permute-start | bytes 98312 | tf_op jit(solution)/shard_map/ppermute | solution.py:18
  16.2 0.8 %collective-permute-start.7 = (bf16[128,128]{1,0:T(8,128)(2,1)S(1)}, bf16[128,128]{1,0:T(8,128)(2,1)S(1)}, u32[]{:S(2)}, u32[]{:S(2)}) collective-permute-start(bf16[128,128]{1,0:T(8,128)(2,1)S(1)} %get-tuple-element.21), channel_id=1, source_target_pairs={{0,2},{1,3},{2,0},{3,1},{4,6},{5,7},{6,4},{7,5},{8,10},{9,11},{10,... | collective-permute-start | bytes 98312 | tf_op jit(solution)/shard_map/ppermute | solution.py:18
  17.1 1.2 %collective-permute-done.5.refs_0_ = bf16[128,128]{1,0:T(8,128)(2,1)S(1)} collective-permute-done((bf16[128,128]{1,0:T(8,128)(2,1)S(1)}, bf16[128,128]{1,0:T(8,128)(2,1)S(1)}, u32[]{:S(2)}, u32[]{:S(2)}) %collective-permute-start.5) | collective-permute-done | bytes 32800 | tf_op jit(solution)/shard_map/ppermute | solution.py:18
  18.3 2.7 %collective-permute-done.6.refs_1_ = bf16[128,128]{1,0:T(8,128)(2,1)S(1)} collective-permute-done((bf16[128,128]{1,0:T(8,128)(2,1)S(1)}, bf16[128,128]{1,0:T(8,128)(2,1)S(1)}, u32[]{:S(2)}, u32[]{:S(2)}) %collective-permute-start.6) | collective-permute-done | bytes 32800 | tf_op jit(solution)/shard_map/ppermute | solution.py:18
  21.1 0.1 collective-permute-start.8
  21.2 3.5 %collective-permute-start.10 = (bf16[144,128]{1,0:T(8,128)(2,1)S(1)}, bf16[144,128]{1,0:T(8,128)(2,1)S(1)}, u32[]{:S(2)}, u32[]{:S(2)}) collective-permute-start(bf16[144,128]{1,0:T(8,128)(2,1)S(1)} %shard_map.64.refs_0_), channel_id=1, source_target_pairs={{0,6},{1,7},{2,4},{3,5},{4,2},{5,3},{6,0},{7,1},{8,14},{9,15},{10,... | collective-permute-start | bytes 110600 | tf_op jit(solution)/shard_map/ppermute | solution.py:18
  24.7 0.4 %collective-permute-done.8.refs_1_ = bf16[144,128]{1,0:T(8,128)(2,1)S(1)} collective-permute-done((bf16[144,128]{1,0:T(8,128)(2,1)S(1)}, bf16[144,128]{1,0:T(8,128)(2,1)S(1)}, u32[]{:S(2)}, u32[]{:S(2)}) %collective-permute-start.8) | collective-permute-done | bytes 36896 | tf_op jit(solution)/shard_map/ppermute | solution.py:18
  25.1 1.3 %collective-permute-start.11 = (bf16[272,128]{1,0:T(8,128)(2,1)S(1)}, bf16[272,128]{1,0:T(8,128)(2,1)S(1)}, u32[]{:S(2)}, u32[]{:S(2)}) collective-permute-start(bf16[272,128]{1,0:T(8,128)(2,1)S(1)} %shard_map.65.refs_0_), channel_id=1, source_target_pairs={{0,1},{1,0},{2,3},{3,2},{4,5},{5,4},{6,7},{7,6},{8,9},{9,8},{10,11... | collective-permute-start | bytes 208904 | tf_op jit(solution)/shard_map/ppermute | solution.py:18
  26.5 0.5 %collective-permute-done.10.refs_1_ = bf16[144,128]{1,0:T(8,128)(2,1)S(1)} collective-permute-done((bf16[144,128]{1,0:T(8,128)(2,1)S(1)}, bf16[144,128]{1,0:T(8,128)(2,1)S(1)}, u32[]{:S(2)}, u32[]{:S(2)}) %collective-permute-start.10) | collective-permute-done | bytes 36896 | tf_op jit(solution)/shard_map/ppermute | solution.py:18
  27.0 2.5 %collective-permute-done.9.refs_0_ = bf16[144,128]{1,0:T(8,128)(2,1)S(1)} collective-permute-done((bf16[144,128]{1,0:T(8,128)(2,1)S(1)}, bf16[144,128]{1,0:T(8,128)(2,1)S(1)}, u32[]{:S(2)}, u32[]{:S(2)}) %collective-permute-start.9) | collective-permute-done | bytes 36896 | tf_op jit(solution)/shard_map/ppermute | solution.py:18
  29.6 1.5 %collective-permute-start.12 = (bf16[272,128]{1,0:T(8,128)(2,1)S(1)}, bf16[272,128]{1,0:T(8,128)(2,1)S(1)}, u32[]{:S(2)}, u32[]{:S(2)}) collective-permute-start(bf16[272,128]{1,0:T(8,128)(2,1)S(1)} %shard_map.66.refs_1_), channel_id=1, source_target_pairs={{0,1},{1,0},{2,3},{3,2},{4,5},{5,4},{6,7},{7,6},{8,9},{9,8},{10,11... | collective-permute-start | bytes 208904 | tf_op jit(solution)/shard_map/ppermute | solution.py:18
  31.1 1.2 %shard_map.67 = (bf16[256,2048]{1,0:T(8,128)(2,1)S(1)}, f32[2,16,256]{2,1,0:T(8,128)S(1)}) custom-call(bf16[272,128]{1,0:T(8,128)(2,1)S(1)} %shard_map.65.refs_0_, bf16[272,128]{1,0:T(8,128)(2,1)S(1)} %shard_map.66.refs_1_, bf16[256,16,128]{2,1,0:T(8,128)(2,1)S(1)} %shard_map.59.refs_4_.refs_2_), custom_call_target="tpu_custom_call" | custom-call | flops 536870912 | bytes 1048576 | tf_op jit(solution)/shard_map/pallas_call | solution.py:214
  32.3 1.6 %collective-permute-done.12.refs_3_ = bf16[272,128]{1,0:T(8,128)(2,1)S(1)} collective-permute-done((bf16[272,128]{1,0:T(8,128)(2,1)S(1)}, bf16[272,128]{1,0:T(8,128)(2,1)S(1)}, u32[]{:S(2)}, u32[]{:S(2)}) %collective-permute-start.12) | collective-permute-done | bytes 69664 | tf_op jit(solution)/shard_map/ppermute | solution.py:18
  34.0 1.3 %shard_map.68 = (f32[40,128]{1,0:T(8,128)S(1)}, f32[40,128]{1,0:T(8,128)S(1)}, f32[40,128]{1,0:T(8,128)S(1)}, f32[40,128]{1,0:T(8,128)S(1)}) custom-call(f32[2,16,256]{2,1,0:T(8,128)S(1)} %get-tuple-element.22.own_ref, bf16[256,2048]{1,0:T(8,128)(2,1)S(1)} %get-tuple-element.23.left_ref, bf16[272,128]{1,0:T(8,128)(2,1)S(1)} %shard_map.65.refs_0_, ...), custom_call_target="tpu_custom_call" | custom-call | flops 536870912 | bytes 1048576 | tf_op jit(solution)/shard_map/pallas_call | solution.py:214
  35.2 0.1 collective-permute-start.13
  35.3 1.3 %collective-permute-start.14 = (f32[40,128]{1,0:T(8,128)S(1)}, f32[40,128]{1,0:T(8,128)S(1)}, u32[]{:S(2)}, u32[]{:S(2)}) collective-permute-start(f32[40,128]{1,0:T(8,128)S(1)} %get-tuple-element.26), channel_id=1, source_target_pairs={{0,16},{8,24},{16,0},{24,8},{1,17},{9,25},{17,1},{25,9},{2,18},{10... | collective-permute-start | bytes 61448 | tf_op jit(solution)/shard_map/ppermute | solution.py:18
  36.7 0.5 %collective-permute-start.15 = (f32[40,128]{1,0:T(8,128)S(1)}, f32[40,128]{1,0:T(8,128)S(1)}, u32[]{:S(2)}, u32[]{:S(2)}) collective-permute-start(f32[40,128]{1,0:T(8,128)S(1)} %get-tuple-element.27), channel_id=1, source_target_pairs={{0,8},{8,0},{16,24},{24,16},{1,9},{9,1},{17,25},{25,17},{2,10},{10... | collective-permute-start | bytes 61448 | tf_op jit(solution)/shard_map/ppermute | solution.py:18
  37.2 1.4 %collective-permute-done.13.refs_1_ = f32[40,128]{1,0:T(8,128)S(1)} collective-permute-done((f32[40,128]{1,0:T(8,128)S(1)}, f32[40,128]{1,0:T(8,128)S(1)}, u32[]{:S(2)}, u32[]{:S(2)}) %collective-permute-start.13) | collective-permute-done | bytes 20512 | tf_op jit(solution)/shard_map/ppermute | solution.py:18
  38.6 0.6 %collective-permute-done.14.refs_2_ = f32[40,128]{1,0:T(8,128)S(1)} collective-permute-done((f32[40,128]{1,0:T(8,128)S(1)}, f32[40,128]{1,0:T(8,128)S(1)}, u32[]{:S(2)}, u32[]{:S(2)}) %collective-permute-start.14) | collective-permute-done | bytes 20512 | tf_op jit(solution)/shard_map/ppermute | solution.py:18
  39.2 0.6 %shard_map.69 = (f32[1,16,256]{2,1,0:T(8,128)}, f32[1,1]{1,0:T(1,128)}) custom-call(f32[40,128]{1,0:T(8,128)S(1)} %get-tuple-element.24.refs_0_, f32[40,128]{1,0:T(8,128)S(1)} %collective-permute-done.13.refs_1_, f32[40,128]{1,0:T(8,128)S(1)} %collective-permute-done.14.refs_2_, f32[40,128]{1,0:T(8,128)S(1)} %collective-permute-done.15.refs_3_), custom_call_target="tpu_custom_call" | custom-call | tf_op jit(solution)/shard_map/pallas_call | solution.py:214
  (19 shorter events, 0.2 us)
Async XLA Ops:
  0.6 5.7 %collective-permute-start.2 = (bf16[1,16,256]{2,1,0:T(8,128)(2,1)}, bf16[1,16,256]{2,1,0:T(8,128)(2,1)S(1)}, u32[]{:S(2)}, u32[]{:S(2)}) collective-permute-start(bf16[1,16,256]{2,1,0:T(8,128)(2,1)} %refs_0_.3), channel_id=1, source_target_pairs={{0,24},{8,16},{16,8},{24,0},{1,25},{9,17},{17,9},{25,1},{2,26},{10... | collective-permute-start | bytes 24584 | tf_op jit(solution)/shard_map/ppermute | solution.py:18
  3.1 3.9 %collective-permute-start.1 = (bf16[1,16,256]{2,1,0:T(8,128)(2,1)}, bf16[1,16,256]{2,1,0:T(8,128)(2,1)S(1)}, u32[]{:S(2)}, u32[]{:S(2)}) collective-permute-start(bf16[1,16,256]{2,1,0:T(8,128)(2,1)} %refs_0_.3), channel_id=1, source_target_pairs={{0,16},{8,24},{16,0},{24,8},{1,17},{9,25},{17,1},{25,9},{2,18},{10... | collective-permute-start | bytes 24584 | tf_op jit(solution)/shard_map/ppermute | solution.py:18
  3.7 3.2 %collective-permute-start = (bf16[1,16,256]{2,1,0:T(8,128)(2,1)}, bf16[1,16,256]{2,1,0:T(8,128)(2,1)S(1)}, u32[]{:S(2)}, u32[]{:S(2)}) collective-permute-start(bf16[1,16,256]{2,1,0:T(8,128)(2,1)} %refs_0_.3), channel_id=1, source_target_pairs={{0,8},{8,0},{16,24},{24,16},{1,9},{9,1},{17,25},{25,17},{2,10},{10... | collective-permute-start | bytes 24584 | tf_op jit(solution)/shard_map/ppermute | solution.py:18
  3.8 1.2 %copy-start = (bf16[128,16,256]{2,1,0:T(8,128)(2,1)S(1)}, bf16[128,16,256]{2,1,0:T(8,128)(2,1)}, u32[]{:S(2)}) copy-start(bf16[128,16,256]{2,1,0:T(8,128)(2,1)} %kernel_ref.1) | copy-start | bytes 3145732
  5.0 2.0 %copy-start.2 = (bf16[1,16,256]{2,1,0:T(8,128)(2,1)S(1)}, bf16[1,16,256]{2,1,0:T(8,128)(2,1)}, u32[]{:S(2)}) copy-start(bf16[1,16,256]{2,1,0:T(8,128)(2,1)} %refs_0_.3) | copy-start | bytes 24580
  6.3 3.4 %copy-start.1 = (f32[4,128,256]{2,1,0:T(8,128)S(1)}, f32[4,128,256]{2,1,0:T(8,128)}, u32[]{:S(2)}) copy-start(f32[4,128,256]{2,1,0:T(8,128)} %refs_5_.1) | copy-start | bytes 1572868
  7.6 4.9 %collective-permute-start.4 = (bf16[256,128]{1,0:T(8,128)(2,1)S(1)}, bf16[256,128]{1,0:T(8,128)(2,1)S(1)}, u32[]{:S(2)}, u32[]{:S(2)}) collective-permute-start(bf16[256,128]{1,0:T(8,128)(2,1)S(1)} %get-tuple-element.18), channel_id=1, source_target_pairs={{0,1},{1,0},{2,3},{3,2},{4,5},{5,4},{6,7},{7,6},{8,9},{9,8},{10,11... | collective-permute-start | bytes 196616 | tf_op jit(solution)/shard_map/ppermute | solution.py:18
  9.2 0.7 %copy-start.3 = (f32[128]{0:T(128)S(1)}, f32[128]{0:T(128)}, u32[]{:S(2)}) copy-start(f32[128]{0:T(128)} %param.7) | copy-start | bytes 1540
  9.2 7.0 %collective-permute-start.3 = (bf16[256,128]{1,0:T(8,128)(2,1)S(1)}, bf16[256,128]{1,0:T(8,128)(2,1)S(1)}, u32[]{:S(2)}, u32[]{:S(2)}) collective-permute-start(bf16[256,128]{1,0:T(8,128)(2,1)S(1)} %get-tuple-element.16), channel_id=1, source_target_pairs={{0,1},{1,0},{2,3},{3,2},{4,5},{5,4},{6,7},{7,6},{8,9},{9,8},{10,11... | collective-permute-start | bytes 196616 | tf_op jit(solution)/shard_map/ppermute | solution.py:18
  12.5 5.8 %collective-permute-start.5 = (bf16[128,128]{1,0:T(8,128)(2,1)S(1)}, bf16[128,128]{1,0:T(8,128)(2,1)S(1)}, u32[]{:S(2)}, u32[]{:S(2)}) collective-permute-start(bf16[128,128]{1,0:T(8,128)(2,1)S(1)} %get-tuple-element.19), channel_id=1, source_target_pairs={{0,6},{1,7},{2,4},{3,5},{4,2},{5,3},{6,0},{7,1},{8,14},{9,15},{10,... | collective-permute-start | bytes 98312 | tf_op jit(solution)/shard_map/ppermute | solution.py:18
  16.2 4.8 %collective-permute-start.6 = (bf16[128,128]{1,0:T(8,128)(2,1)S(1)}, bf16[128,128]{1,0:T(8,128)(2,1)S(1)}, u32[]{:S(2)}, u32[]{:S(2)}) collective-permute-start(bf16[128,128]{1,0:T(8,128)(2,1)S(1)} %get-tuple-element.20), channel_id=1, source_target_pairs={{0,4},{1,5},{2,6},{3,7},{4,0},{5,1},{6,2},{7,3},{8,12},{9,13},{10,... | collective-permute-start | bytes 98312 | tf_op jit(solution)/shard_map/ppermute | solution.py:18
  16.2 4.8 %collective-permute-start.7 = (bf16[128,128]{1,0:T(8,128)(2,1)S(1)}, bf16[128,128]{1,0:T(8,128)(2,1)S(1)}, u32[]{:S(2)}, u32[]{:S(2)}) collective-permute-start(bf16[128,128]{1,0:T(8,128)(2,1)S(1)} %get-tuple-element.21), channel_id=1, source_target_pairs={{0,2},{1,3},{2,0},{3,1},{4,6},{5,7},{6,4},{7,5},{8,10},{9,11},{10,... | collective-permute-start | bytes 98312 | tf_op jit(solution)/shard_map/ppermute | solution.py:18
  21.1 4.0 %collective-permute-start.8 = (bf16[144,128]{1,0:T(8,128)(2,1)S(1)}, bf16[144,128]{1,0:T(8,128)(2,1)S(1)}, u32[]{:S(2)}, u32[]{:S(2)}) collective-permute-start(bf16[144,128]{1,0:T(8,128)(2,1)S(1)} %shard_map.64.refs_0_), channel_id=1, source_target_pairs={{0,2},{1,3},{2,0},{3,1},{4,6},{5,7},{6,4},{7,5},{8,10},{9,11},{10,... | collective-permute-start | bytes 110600 | tf_op jit(solution)/shard_map/ppermute | solution.py:18
  21.2 5.9 %collective-permute-start.10 = (bf16[144,128]{1,0:T(8,128)(2,1)S(1)}, bf16[144,128]{1,0:T(8,128)(2,1)S(1)}, u32[]{:S(2)}, u32[]{:S(2)}) collective-permute-start(bf16[144,128]{1,0:T(8,128)(2,1)S(1)} %shard_map.64.refs_0_), channel_id=1, source_target_pairs={{0,6},{1,7},{2,4},{3,5},{4,2},{5,3},{6,0},{7,1},{8,14},{9,15},{10,... | collective-permute-start | bytes 110600 | tf_op jit(solution)/shard_map/ppermute | solution.py:18
  24.7 4.9 %collective-permute-start.9 = (bf16[144,128]{1,0:T(8,128)(2,1)S(1)}, bf16[144,128]{1,0:T(8,128)(2,1)S(1)}, u32[]{:S(2)}, u32[]{:S(2)}) collective-permute-start(bf16[144,128]{1,0:T(8,128)(2,1)S(1)} %shard_map.64.refs_0_), channel_id=1, source_target_pairs={{0,4},{1,5},{2,6},{3,7},{4,0},{5,1},{6,2},{7,3},{8,12},{9,13},{10,... | collective-permute-start | bytes 110600 | tf_op jit(solution)/shard_map/ppermute | solution.py:18
  25.1 7.2 %collective-permute-start.11 = (bf16[272,128]{1,0:T(8,128)(2,1)S(1)}, bf16[272,128]{1,0:T(8,128)(2,1)S(1)}, u32[]{:S(2)}, u32[]{:S(2)}) collective-permute-start(bf16[272,128]{1,0:T(8,128)(2,1)S(1)} %shard_map.65.refs_0_), channel_id=1, source_target_pairs={{0,1},{1,0},{2,3},{3,2},{4,5},{5,4},{6,7},{7,6},{8,9},{9,8},{10,11... | collective-permute-start | bytes 208904 | tf_op jit(solution)/shard_map/ppermute | solution.py:18
  29.6 4.4 %collective-permute-start.12 = (bf16[272,128]{1,0:T(8,128)(2,1)S(1)}, bf16[272,128]{1,0:T(8,128)(2,1)S(1)}, u32[]{:S(2)}, u32[]{:S(2)}) collective-permute-start(bf16[272,128]{1,0:T(8,128)(2,1)S(1)} %shard_map.66.refs_1_), channel_id=1, source_target_pairs={{0,1},{1,0},{2,3},{3,2},{4,5},{5,4},{6,7},{7,6},{8,9},{9,8},{10,11... | collective-permute-start | bytes 208904 | tf_op jit(solution)/shard_map/ppermute | solution.py:18
  35.2 3.3 %collective-permute-start.13 = (f32[40,128]{1,0:T(8,128)S(1)}, f32[40,128]{1,0:T(8,128)S(1)}, u32[]{:S(2)}, u32[]{:S(2)}) collective-permute-start(f32[40,128]{1,0:T(8,128)S(1)} %get-tuple-element.25), channel_id=1, source_target_pairs={{0,24},{8,16},{16,8},{24,0},{1,25},{9,17},{17,9},{25,1},{2,26},{10... | collective-permute-start | bytes 61448 | tf_op jit(solution)/shard_map/ppermute | solution.py:18
  35.3 3.8 %collective-permute-start.14 = (f32[40,128]{1,0:T(8,128)S(1)}, f32[40,128]{1,0:T(8,128)S(1)}, u32[]{:S(2)}, u32[]{:S(2)}) collective-permute-start(f32[40,128]{1,0:T(8,128)S(1)} %get-tuple-element.26), channel_id=1, source_target_pairs={{0,16},{8,24},{16,0},{24,8},{1,17},{9,25},{17,1},{25,9},{2,18},{10... | collective-permute-start | bytes 61448 | tf_op jit(solution)/shard_map/ppermute | solution.py:18
  36.7 2.5 %collective-permute-start.15 = (f32[40,128]{1,0:T(8,128)S(1)}, f32[40,128]{1,0:T(8,128)S(1)}, u32[]{:S(2)}, u32[]{:S(2)}) collective-permute-start(f32[40,128]{1,0:T(8,128)S(1)} %get-tuple-element.27), channel_id=1, source_target_pairs={{0,8},{8,0},{16,24},{24,16},{1,9},{9,1},{17,25},{25,17},{2,10},{10... | collective-permute-start | bytes 61448 | tf_op jit(solution)/shard_map/ppermute | solution.py:18

commit v6 on v5

--- a/solution.py
+++ b/solution.py
@@ -28,9 +28,11 @@
 def turn_body(kernel_ref, out_ref, turned_ref, *parts):
     steps, points, sensors = out_ref.shape
     count = steps // len(parts)
+    first = kernel_ref.shape[2] - steps
     for i, rows_ref in enumerate(parts):
         lags = slice(i * count, (i + 1) * count)
-        rows_ref[...] = kernel_ref[:, :, lags].astype(jnp.float32).reshape(sensors * points, count)
+        some = kernel_ref[:, :, first + i * count : first + (i + 1) * count]
+        rows_ref[...] = some.astype(jnp.float32).reshape(sensors * points, count)
         for p in range(points):
             plane = rows_ref[pl.ds(p, sensors, stride=points), :]
             turned_ref[pl.ds(i * count * points + p, count, stride=points), :] = plane.T
@@ -40,8 +42,9 @@
 
 def forward_body(away, near, far, lags, n_models, n_x, *refs):
     models, xs, refs = refs[:n_models], refs[n_models : n_models + n_x], refs[n_models + n_x :]
-    part_steps, points, sensors = xs[0].shape
-    steps = part_steps * n_x
+    points, sensors = xs[0].shape[1:]
+    ks = [(x_ref, k) for x_ref in xs for k in range(x_ref.shape[0])]
+    steps = len(ks)
     me, j = lax.axis_index("sens"), lax.axis_index("par")
     place, block = j // near, lax.rem(j, near) ^ away
     if away == 0:
@@ -69,7 +72,7 @@
         u_ref[v] = ut_ref[v].T.astype(jnp.bfloat16)
     for k0 in range(0, steps, 2 * lags):
         left = steps - k0
-        x_ref, at = xs[k0 // part_steps], k0 % part_steps
+        x_ref, at = ks[k0]
         pair = [x_ref[k : k + lags].reshape(lags * points, sensors) for k in (at, at + lags)]
         some = u_ref[:, :left, :].reshape(of_block * left, lags * points)
         term = jnp.dot(some, jnp.concatenate(pair, axis=1), preferred_element_type=jnp.float32)
@@ -137,18 +140,19 @@
     out_ref[len(parts) * rows :, :] = three_parts(jnp.sum(extra, axis=0, keepdims=True))
 
 
-def adjoint_terms(groups, left_ref, r_ref, all_ref, far, lags, points):
-    of_block, _, steps = r_ref.shape
+def adjoint_terms(group_ref, start, left_ref, r_ref, all_ref, slots, lags, points):
+    of_group, _, steps = r_ref.shape
     sensors = all_ref.shape[1]
-    rows = of_block * steps // far
-    place = lax.axis_index("par") // (lax.axis_size("par") // far)
-    for b in range(far):
-        there = pl.multiple_of((place ^ b) * rows, rows)
-        ref, at = groups[b * len(groups) // far], b % (far // len(groups)) * rows
-        all_ref[pl.ds(there, rows), :] = ref[at : at + rows, :].astype(jnp.float32)
+    rows = of_group * steps // slots
+    near, _ = levels(lax.axis_size("par"), lax.axis_size("sens"))
+    place = lax.axis_index("par") // near
+    group = (place ^ start) // slots
+    for b in range(slots):
+        there = pl.multiple_of(((place ^ (start + b)) - group * slots) * rows, rows)
+        all_ref[pl.ds(there, rows), :] = group_ref[b * rows : (b + 1) * rows, :].astype(jnp.float32)
     lane = lax.broadcasted_iota(jnp.int32, (sensors, steps), 1)
     lane_p = lax.broadcasted_iota(jnp.int32, (points, steps), 1)
-    for v in range(of_block):
+    for v in range(of_group):
         series = all_ref[v * steps : (v + 1) * steps, :].T
         for d in range(lags):
             moved = series
@@ -160,35 +164,43 @@
         for c in range(1, steps // lags):
             moved = pltpu.roll(terms[c * points : (c + 1) * points], steps - c * lags, 1)
             total += jnp.where(lane_p < steps - c * lags, moved, 0.0)
-        yield v, total
-
-
-def adjoint_own_body(far, lags, n_groups, *refs):
-    groups, xs, (left_ref, own_ref, r_ref, all_ref) = refs[:n_groups], refs[n_groups:-4], refs[-4:]
-    part_steps, points, sensors = xs[0].shape
-    for d in range(lags):
-        for c in range(len(xs) * part_steps // lags):
-            k = c * lags + d
-            left_ref[c * points : (c + 1) * points, d * sensors : (d + 1) * sensors] = xs[k // part_steps][k % part_steps]
-    for v, total in adjoint_terms(groups, left_ref, r_ref, all_ref, far, lags, points):
-        own_ref[v] = total
-
-
-def adjoint_rest_body(near, far, lags, n_groups, own_ref, left_ref, *refs):
-    groups, outs, (slots_ref, r_ref, all_ref) = refs[: near * n_groups], refs[near * n_groups : -3], refs[-3:]
-    of_block, points, steps = own_ref.shape
-    lanes = outs[0].shape[1]
-    block = lax.rem(lax.axis_index("par"), near)
+        yield group * of_group + v, total
+
+
+def left_body(lags, *refs):
+    xs, left_ref = refs[:-1], refs[-1]
+    points, sensors = xs[0].shape[1:]
+    ks = [(x_ref, k) for x_ref in xs for k in range(x_ref.shape[0])]
+    for k, (x_ref, at) in enumerate(ks):
+        c, d = divmod(k, lags)
+        left_ref[c * points : (c + 1) * points, d * sensors : (d + 1) * sensors] = x_ref[at]
+
+
+def adjoint_piece_body(start, slots, lags, group_ref, left_ref, out_ref, r_ref, all_ref):
+    points = out_ref.shape[1]
+    for v, (_, total) in enumerate(adjoint_terms(group_ref, start, left_ref, r_ref, all_ref, slots, lags, points)):
+        out_ref[v] = total
+
+
+def adjoint_last_body(near, slots, lags, n_groups, *refs):
+    done, refs = refs[: near * n_groups - 1], refs[near * n_groups - 1 :]
+    left_ref, groups, refs = refs[0], refs[1 : 1 + near * n_groups], refs[1 + near * n_groups :]
+    outs, (slots_ref, r_ref, all_ref) = refs[:-3], refs[-3:]
+    of_group, points, steps = done[0].shape
+    of_block, lanes = of_group * n_groups, outs[0].shape[1]
+    j = lax.axis_index("par")
+    place, block = j // near, lax.rem(j, near)
     extra = 0.0
     for ref in groups:
         extra += ref[ref.shape[0] - EXTRA_ROWS :, :].astype(jnp.float32)
     squared = jnp.full((MISFIT_ROWS, lanes), jnp.sum(extra), jnp.float32)
-    for v in range(of_block):
-        slots_ref[block * of_block + v] = own_ref[v]
-    for away in range(1, near):
-        some = groups[away * n_groups : (away + 1) * n_groups]
-        for v, total in adjoint_terms(some, left_ref, r_ref, all_ref, far, lags, points):
-            slots_ref[(block ^ away) * of_block + v] = total
+    for i, ref in enumerate(done):
+        away, group = i // n_groups, (place ^ (i % n_groups * slots)) // slots
+        for v in range(of_group):
+            slots_ref[(block ^ away) * of_block + group * of_group + v] = ref[v]
+    start = (n_groups - 1) * slots
+    for v, total in adjoint_terms(groups[-1], start, left_ref, r_ref, all_ref, slots, lags, points):
+        slots_ref[(block ^ (near - 1)) * of_block + v] = total
     for v, ref in enumerate(outs):
         for i in range(steps // lanes):
             ref[i * points : (i + 1) * points, :] = slots_ref[v, :, i * lanes : (i + 1) * lanes]
@@ -226,31 +238,33 @@
     vectors = n_sens * model.shape[0]
     near, far = levels(n_par, vectors)
     of_block = vectors // near
-    n_groups = min(2, far)
+    n_groups = 2 if of_block % 2 == 0 and far % 2 == 0 else 1
     slots = far // n_groups
     lags = 256 // points
     rows = vectors * steps // n_par
     lanes = min(128, steps)
     flops = 2 * vectors * sensors * points * steps * steps // near
     cost = pl.CostEstimate(flops=flops, bytes_accessed=2 * kernel.size, transcendentals=0)
+    piece_cost = pl.CostEstimate(flops=flops // n_groups, bytes_accessed=2 * kernel.size, transcendentals=0)
     vmem, hbm = pl.BlockSpec(memory_space=pltpu.VMEM), pl.BlockSpec(memory_space=pltpu.HBM)
 
     def struct(shape, dtype):
         return jax.ShapeDtypeStruct(shape, dtype)
 
     models = [model] + [swap(model, "sens", step) for step in range(1, n_sens)]
+    half = steps - steps // lanes // 2 * lanes
     xs = [
         call(
             turn_body,
-            struct((steps, points, sensors), kernel.dtype),
-            (kernel,),
+            struct((count, points, sensors), kernel.dtype),
+            (some,),
             VMEM_LIMIT,
-            scratch_shapes=[
-                pltpu.VMEM((steps * points, sensors), jnp.float32),
-            ]
-            + [pltpu.VMEM((sensors * points, lanes), jnp.float32)] * (steps // lanes),
-            cost_estimate=pl.CostEstimate(flops=0, bytes_accessed=6 * kernel.size, transcendentals=0),
+            scratch_shapes=[pltpu.VMEM((count * points, sensors), jnp.float32)]
+            + [pltpu.VMEM((sensors * points, lanes), jnp.float32)] * (count // lanes),
+            cost_estimate=pl.CostEstimate(flops=0, bytes_accessed=3 * kernel.size, transcendentals=0),
         )
+        for count, some in ((half, kernel[:, :, :half]), (steps - half, kernel))
+        if count > 0
     ]
 
     def forward(away):
@@ -302,28 +316,37 @@
     groups = [call(join_body, joined, parts[g * slots : (g + 1) * slots]) for g in range(n_groups)]
     others = [[swap(group, "par", away) for group in groups] for away in range(1, near)]
 
+    of_group = of_block // n_groups
     scratch = [
-        pltpu.VMEM((of_block, lags * sensors, steps), jnp.bfloat16),
-        pltpu.VMEM((of_block * steps, sensors), jnp.float32),
+        pltpu.VMEM((of_group, lags * sensors, steps), jnp.bfloat16),
+        pltpu.VMEM((of_group * steps, sensors), jnp.float32),
     ]
-    left, own = call(
-        functools.partial(adjoint_own_body, far, lags, n_groups),
-        [
-            struct((steps // lags * points, lags * sensors), jnp.bfloat16),
-            struct((of_block, points, steps), jnp.float32),
-        ],
-        (*groups, *xs),
+    left = call(
+        functools.partial(left_body, lags),
+        struct((steps // lags * points, lags * sensors), jnp.bfloat16),
+        xs,
         VMEM_LIMIT,
-        scratch_shapes=scratch,
-        cost_estimate=cost,
+        cost_estimate=pl.CostEstimate(flops=0, bytes_accessed=kernel.size, transcendentals=0),
     )
+    every = groups + [group for some in others for group in some]
+    done = [
+        call(
+            functools.partial(adjoint_piece_body, i % n_groups * slots, slots, lags),
+            struct((of_group, points, steps), jnp.float32),
+            (group, left),
+            VMEM_LIMIT,
+            scratch_shapes=scratch,
+            cost_estimate=piece_cost,
+        )
+        for i, group in enumerate(every[:-1])
+    ]
     partials = call(
-        functools.partial(adjoint_rest_body, near, far, lags, n_groups),
+        functools.partial(adjoint_last_body, near, slots, lags, n_groups),
         [struct((steps // lanes * points + MISFIT_ROWS, lanes), jnp.float32)] * vectors,
-        (own, left, *groups, *[group for some in others for group in some]),
+        (*done, left, *every),
         VMEM_LIMIT,
         scratch_shapes=[pltpu.VMEM((vectors, points, steps), jnp.float32)] + scratch,
-        cost_estimate=cost,
+        cost_estimate=piece_cost,
     )
     received = [swap(partials[step], "sens", step) for step in range(n_sens - 1, 0, -1)]
     entries = vectors * sensors * n_sens * steps

time: 40 us -> 39.1 us (0.978)
  waiting for transfers between devices: 13.4 us -> 10.3 us
  starting transfers between devices: 18.1 us -> 19.7 us
  Pallas kernels: 6.2 us -> 6.85 us
    ppermute x16, waiting for transfers between devices: 13.4 us -> 10.3 us  [swap(): lax.ppermute(value, axis, [(i, i ^ step) for i in range(lax.axis_size(axi...]
    ppermute x16, starting transfers between devices: 18.1 us -> 19.7 us  [swap(): lax.ppermute(value, axis, [(i, i ^ step) for i in range(lax.axis_size(axi...]
    unnamed x8, local copies, waits for them, and re-layouts: 1.38 us -> 0.16 us
    slice x0 -> x1, local copies, waits for them, and re-layouts: none -> 1.08 us  [local(): kernel[:, :, :half]]
    pallas_call x11 -> x15, Pallas kernels: 6.2 us -> 6.85 us  [call(): pl.pallas_call(body, out_shape=out_shape, out_specs=jax.tree.map(lambda _...]
  transfers between devices with their start and end apart: 16 -> 16, of which waited for: 10 -> 8; matrix products, arithmetic and copies ran while one was open for 0% -> 3% of each run, Pallas kernels for 9% -> 12%
where the time goes in v6:
time: 39.1 us; the launch traced here: 38.9 us
  starting transfers between devices  19.7 us (50%)
  waiting for transfers between devices  10.3 us (26%)
  Pallas kernels  6.85 us (18%)
  local copies, waits for them, and re-layouts  1.24 us (3%)
  between operations  0.8 us (2%)
    ppermute x16, starting transfers between devices, swap(): lax.ppermute(value, axis, [(i, i ^ step) for i in range(lax.axis_size(axi...  19.7 us
    ppermute x16, waiting for transfers between devices, swap(): lax.ppermute(value, axis, [(i, i ^ step) for i in range(lax.axis_size(axi...  10.3 us
    pallas_call x15, Pallas kernels, call(): pl.pallas_call(body, out_shape=out_shape, out_specs=jax.tree.map(lambda _...  6.85 us
    slice x1, local copies, waits for them, and re-layouts, local(): kernel[:, :, :half]  1.08 us
  transfers between devices with their start and end apart: 16, of which 8 were waited for; matrix products, arithmetic and copies ran while one was open for 3% of the time, Pallas kernels for 12%

profile of v6, /device:TPU:0, one launch (start us, length us, event | category | flops | bytes accessed | tf_op | source)
XLA Modules:
  0.0 38.9 jit_solution(351108930375268535)
XLA Ops:
  0.6 0.5 %collective-permute-start = (bf16[1,16,256]{2,1,0:T(8,128)(2,1)}, bf16[1,16,256]{2,1,0:T(8,128)(2,1)S(1)}, u32[]{:S(2)}, u32[]{:S(2)}) collective-permute-start(bf16[1,16,256]{2,1,0:T(8,128)(2,1)} %refs_0_.3), channel_id=1, source_target_pairs={{0,8},{8,0},{16,24},{24,16},{1,9},{9,1},{17,25},{25,17},{2,10},{10... | collective-permute-start | bytes 24584 | tf_op jit(solution)/shard_map/ppermute | solution.py:18
  1.2 2.6 %collective-permute-start.1 = (bf16[1,16,256]{2,1,0:T(8,128)(2,1)}, bf16[1,16,256]{2,1,0:T(8,128)(2,1)S(1)}, u32[]{:S(2)}, u32[]{:S(2)}) collective-permute-start(bf16[1,16,256]{2,1,0:T(8,128)(2,1)} %refs_0_.3), channel_id=1, source_target_pairs={{0,16},{8,24},{16,0},{24,8},{1,17},{9,25},{17,1},{25,9},{2,18},{10... | collective-permute-start | bytes 24584 | tf_op jit(solution)/shard_map/ppermute | solution.py:18
  3.8 1.1 %slice.3.kernel_ref = bf16[128,16,128]{2,1,0:T(8,128)(2,1)S(1)} slice(bf16[128,16,256]{2,1,0:T(8,128)(2,1)} %kernel_ref.1), slice={[0:128], [0:16], [0:128]} | slice | bytes 1048576 | tf_op jit(solution)/shard_map/slice | solution.py:266
  4.9 0.7 %shard_map.60.refs_5_.refs_1_ = bf16[128,16,128]{2,1,0:T(8,128)(2,1)S(1)} custom-call(bf16[128,16,256]{2,1,0:T(8,128)(2,1)S(1)} %copy-done), custom_call_target="tpu_custom_call" | custom-call | bytes 1572864 | tf_op jit(solution)/shard_map/pallas_call | solution.py:226
  5.6 0.7 %shard_map.59.refs_4_.refs_0_ = bf16[128,16,128]{2,1,0:T(8,128)(2,1)S(1)} custom-call(bf16[128,16,128]{2,1,0:T(8,128)(2,1)S(1)} %slice.3.kernel_ref), custom_call_target="tpu_custom_call" | custom-call | bytes 1572864 | tf_op jit(solution)/shard_map/pallas_call | solution.py:226
  6.2 0.8 %collective-permute-done.2.refs_3_ = bf16[1,16,256]{2,1,0:T(8,128)(2,1)S(1)} collective-permute-done((bf16[1,16,256]{2,1,0:T(8,128)(2,1)}, bf16[1,16,256]{2,1,0:T(8,128)(2,1)S(1)}, u32[]{:S(2)}, u32[]{:S(2)}) %collective-permute-start.2) | collective-permute-done | bytes 8224 | tf_op jit(solution)/shard_map/ppermute | solution.py:18
  7.0 0.7 %shard_map.62 = (bf16[256,128]{1,0:T(8,128)(2,1)S(1)}, bf16[256,128]{1,0:T(8,128)(2,1)S(1)}) custom-call(bf16[1,16,256]{2,1,0:T(8,128)(2,1)S(1)} %copy-done.2, bf16[1,16,256]{2,1,0:T(8,128)(2,1)S(1)} %collective-permute-done.refs_1_, bf16[1,16,256]{2,1,0:T(8,128)(2,1)S(1)} %collective-permute-done.1.refs_2_, ...), custom_call_target="tpu_custom_call" | custom-call | flops 536870912 | bytes 1048576 | tf_op jit(solution)/shard_map/pallas_call | solution.py:226
  7.7 1.6 %collective-permute-start.4 = (bf16[256,128]{1,0:T(8,128)(2,1)S(1)}, bf16[256,128]{1,0:T(8,128)(2,1)S(1)}, u32[]{:S(2)}, u32[]{:S(2)}) collective-permute-start(bf16[256,128]{1,0:T(8,128)(2,1)S(1)} %get-tuple-element.16), channel_id=1, source_target_pairs={{0,1},{1,0},{2,3},{3,2},{4,5},{5,4},{6,7},{7,6},{8,9},{9,8},{10,11... | collective-permute-start | bytes 196616 | tf_op jit(solution)/shard_map/ppermute | solution.py:18
  9.3 0.5 %collective-permute-start.3 = (bf16[256,128]{1,0:T(8,128)(2,1)S(1)}, bf16[256,128]{1,0:T(8,128)(2,1)S(1)}, u32[]{:S(2)}, u32[]{:S(2)}) collective-permute-start(bf16[256,128]{1,0:T(8,128)(2,1)S(1)} %get-tuple-element.14), channel_id=1, source_target_pairs={{0,1},{1,0},{2,3},{3,2},{4,5},{5,4},{6,7},{7,6},{8,9},{9,8},{10,11... | collective-permute-start | bytes 196616 | tf_op jit(solution)/shard_map/ppermute | solution.py:18
  9.8 0.1 copy-done.3
  9.9 1.0 %shard_map.61.own_ref = f32[520,128]{1,0:T(8,128)S(1)} custom-call(bf16[1,16,256]{2,1,0:T(8,128)(2,1)S(1)} %copy-done.2, bf16[1,16,256]{2,1,0:T(8,128)(2,1)S(1)} %collective-permute-done.refs_1_, bf16[1,16,256]{2,1,0:T(8,128)(2,1)S(1)} %collective-permute-done.1.refs_2_, bf16[1,16,256]{2,1,0:T(8,128)(2,1)S(1)} %collective-permute-done.2.refs_3_, ...), custom_call_target="tpu_custom_call" | custom-call | flops 536870912 | bytes 1048576 | tf_op jit(solution)/shard_map/pallas_call | solution.py:226
  10.9 1.5 %collective-permute-done.4.refs_0_ = bf16[256,128]{1,0:T(8,128)(2,1)S(1)} collective-permute-done((bf16[256,128]{1,0:T(8,128)(2,1)S(1)}, bf16[256,128]{1,0:T(8,128)(2,1)S(1)}, u32[]{:S(2)}, u32[]{:S(2)}) %collective-permute-start.4) | collective-permute-done | bytes 65568 | tf_op jit(solution)/shard_map/ppermute | solution.py:18
  12.4 3.7 %collective-permute-start.5 = (bf16[128,128]{1,0:T(8,128)(2,1)S(1)}, bf16[128,128]{1,0:T(8,128)(2,1)S(1)}, u32[]{:S(2)}, u32[]{:S(2)}) collective-permute-start(bf16[128,128]{1,0:T(8,128)(2,1)S(1)} %get-tuple-element.17), channel_id=1, source_target_pairs={{0,6},{1,7},{2,4},{3,5},{4,2},{5,3},{6,0},{7,1},{8,14},{9,15},{10,... | collective-permute-start | bytes 98312 | tf_op jit(solution)/shard_map/ppermute | solution.py:18
  16.1 0.8 %collective-permute-start.7 = (bf16[128,128]{1,0:T(8,128)(2,1)S(1)}, bf16[128,128]{1,0:T(8,128)(2,1)S(1)}, u32[]{:S(2)}, u32[]{:S(2)}) collective-permute-start(bf16[128,128]{1,0:T(8,128)(2,1)S(1)} %get-tuple-element.19), channel_id=1, source_target_pairs={{0,2},{1,3},{2,0},{3,1},{4,6},{5,7},{6,4},{7,5},{8,10},{9,11},{10,... | collective-permute-start | bytes 98312 | tf_op jit(solution)/shard_map/ppermute | solution.py:18
  16.9 1.3 %collective-permute-done.5.refs_0_ = bf16[128,128]{1,0:T(8,128)(2,1)S(1)} collective-permute-done((bf16[128,128]{1,0:T(8,128)(2,1)S(1)}, bf16[128,128]{1,0:T(8,128)(2,1)S(1)}, u32[]{:S(2)}, u32[]{:S(2)}) %collective-permute-start.5) | collective-permute-done | bytes 32800 | tf_op jit(solution)/shard_map/ppermute | solution.py:18
  18.2 2.7 %collective-permute-done.6.refs_1_ = bf16[128,128]{1,0:T(8,128)(2,1)S(1)} collective-permute-done((bf16[128,128]{1,0:T(8,128)(2,1)S(1)}, bf16[128,128]{1,0:T(8,128)(2,1)S(1)}, u32[]{:S(2)}, u32[]{:S(2)}) %collective-permute-start.6) | collective-permute-done | bytes 32800 | tf_op jit(solution)/shard_map/ppermute | solution.py:18
  21.0 2.5 %collective-permute-start.9 = (bf16[144,128]{1,0:T(8,128)(2,1)S(1)}, bf16[144,128]{1,0:T(8,128)(2,1)S(1)}, u32[]{:S(2)}, u32[]{:S(2)}) collective-permute-start(bf16[144,128]{1,0:T(8,128)(2,1)S(1)} %shard_map.65.refs_0_), channel_id=1, source_target_pairs={{0,4},{1,5},{2,6},{3,7},{4,0},{5,1},{6,2},{7,3},{8,12},{9,13},{10,... | collective-permute-start | bytes 110600 | tf_op jit(solution)/shard_map/ppermute | solution.py:18
  23.5 1.9 %collective-permute-start.10 = (bf16[144,128]{1,0:T(8,128)(2,1)S(1)}, bf16[144,128]{1,0:T(8,128)(2,1)S(1)}, u32[]{:S(2)}, u32[]{:S(2)}) collective-permute-start(bf16[144,128]{1,0:T(8,128)(2,1)S(1)} %shard_map.65.refs_0_), channel_id=1, source_target_pairs={{0,6},{1,7},{2,4},{3,5},{4,2},{5,3},{6,0},{7,1},{8,14},{9,15},{10,... | collective-permute-start | bytes 110600 | tf_op jit(solution)/shard_map/ppermute | solution.py:18
  25.4 1.8 %collective-permute-start.11 = (bf16[272,128]{1,0:T(8,128)(2,1)S(1)}, bf16[272,128]{1,0:T(8,128)(2,1)S(1)}, u32[]{:S(2)}, u32[]{:S(2)}) collective-permute-start(bf16[272,128]{1,0:T(8,128)(2,1)S(1)} %shard_map.66.group_ref.refs_4_), channel_id=1, source_target_pairs={{0,1},{1,0},{2,3},{3,2},{4,5},{5,4},{6,7},{7,6},{8,9},{9,8},{10,11... | collective-permute-start | bytes 208904 | tf_op jit(solution)/shard_map/ppermute | solution.py:18
  27.2 0.2 shard_map.67.left_ref.refs_3_
  27.4 1.8 %collective-permute-done.10.refs_1_ = bf16[144,128]{1,0:T(8,128)(2,1)S(1)} collective-permute-done((bf16[144,128]{1,0:T(8,128)(2,1)S(1)}, bf16[144,128]{1,0:T(8,128)(2,1)S(1)}, u32[]{:S(2)}, u32[]{:S(2)}) %collective-permute-start.10) | collective-permute-done | bytes 36896 | tf_op jit(solution)/shard_map/ppermute | solution.py:18
  29.2 1.8 %collective-permute-start.12 = (bf16[272,128]{1,0:T(8,128)(2,1)S(1)}, bf16[272,128]{1,0:T(8,128)(2,1)S(1)}, u32[]{:S(2)}, u32[]{:S(2)}) collective-permute-start(bf16[272,128]{1,0:T(8,128)(2,1)S(1)} %shard_map.69.group_ref.refs_5_), channel_id=1, source_target_pairs={{0,1},{1,0},{2,3},{3,2},{4,5},{5,4},{6,7},{7,6},{8,9},{9,8},{10,11... | collective-permute-start | bytes 208904 | tf_op jit(solution)/shard_map/ppermute | solution.py:18
  31.0 0.7 %shard_map.68.refs_0_ = f32[1,16,256]{2,1,0:T(8,128)S(1)} custom-call(bf16[272,128]{1,0:T(8,128)(2,1)S(1)} %shard_map.66.group_ref.refs_4_, bf16[256,2048]{1,0:T(8,128)(2,1)S(1)} %shard_map.67.left_ref.refs_3_), custom_call_target="tpu_custom_call" | custom-call | flops 268435456 | bytes 1048576 | tf_op jit(solution)/shard_map/pallas_call | solution.py:226
  31.8 0.7 %shard_map.70.refs_1_ = f32[1,16,256]{2,1,0:T(8,128)S(1)} custom-call(bf16[272,128]{1,0:T(8,128)(2,1)S(1)} %shard_map.69.group_ref.refs_5_, bf16[256,2048]{1,0:T(8,128)(2,1)S(1)} %shard_map.67.left_ref.refs_3_), custom_call_target="tpu_custom_call" | custom-call | flops 268435456 | bytes 1048576 | tf_op jit(solution)/shard_map/pallas_call | solution.py:226
  32.5 0.7 %shard_map.71.refs_2_ = f32[1,16,256]{2,1,0:T(8,128)S(1)} custom-call(bf16[272,128]{1,0:T(8,128)(2,1)S(1)} %collective-permute-done.11.group_ref.refs_6_, bf16[256,2048]{1,0:T(8,128)(2,1)S(1)} %shard_map.67.left_ref.refs_3_), custom_call_target="tpu_custom_call" | custom-call | flops 268435456 | bytes 1048576 | tf_op jit(solution)/shard_map/pallas_call | solution.py:226
  33.3 0.3 collective-permute-done.12.refs_7_
  33.6 0.8 %shard_map.72 = (f32[40,128]{1,0:T(8,128)S(1)}, f32[40,128]{1,0:T(8,128)S(1)}, f32[40,128]{1,0:T(8,128)S(1)}, f32[40,128]{1,0:T(8,128)S(1)}) custom-call(f32[1,16,256]{2,1,0:T(8,128)S(1)} %shard_map.68.refs_0_, f32[1,16,256]{2,1,0:T(8,128)S(1)} %shard_map.70.refs_1_, f32[1,16,256]{2,1,0:T(8,128)S(1)} %shard_map.71.refs_2_, ...), custom_call_target="tpu_custom_call" | custom-call | flops 268435456 | bytes 1048576 | tf_op jit(solution)/shard_map/pallas_call | solution.py:226
  34.5 0.7 %collective-permute-start.14 = (f32[40,128]{1,0:T(8,128)S(1)}, f32[40,128]{1,0:T(8,128)S(1)}, u32[]{:S(2)}, u32[]{:S(2)}) collective-permute-start(f32[40,128]{1,0:T(8,128)S(1)} %get-tuple-element.22), channel_id=1, source_target_pairs={{0,16},{8,24},{16,0},{24,8},{1,17},{9,25},{17,1},{25,9},{2,18},{10... | collective-permute-start | bytes 61448 | tf_op jit(solution)/shard_map/ppermute | solution.py:18
  35.2 1.1 %collective-permute-start.15 = (f32[40,128]{1,0:T(8,128)S(1)}, f32[40,128]{1,0:T(8,128)S(1)}, u32[]{:S(2)}, u32[]{:S(2)}) collective-permute-start(f32[40,128]{1,0:T(8,128)S(1)} %get-tuple-element.23), channel_id=1, source_target_pairs={{0,8},{8,0},{16,24},{24,16},{1,9},{9,1},{17,25},{25,17},{2,10},{10... | collective-permute-start | bytes 61448 | tf_op jit(solution)/shard_map/ppermute | solution.py:18
  36.3 1.3 %collective-permute-done.13.refs_1_ = f32[40,128]{1,0:T(8,128)S(1)} collective-permute-done((f32[40,128]{1,0:T(8,128)S(1)}, f32[40,128]{1,0:T(8,128)S(1)}, u32[]{:S(2)}, u32[]{:S(2)}) %collective-permute-start.13) | collective-permute-done | bytes 20512 | tf_op jit(solution)/shard_map/ppermute | solution.py:18
  37.7 0.7 %collective-permute-done.14.refs_2_ = f32[40,128]{1,0:T(8,128)S(1)} collective-permute-done((f32[40,128]{1,0:T(8,128)S(1)}, f32[40,128]{1,0:T(8,128)S(1)}, u32[]{:S(2)}, u32[]{:S(2)}) %collective-permute-start.14) | collective-permute-done | bytes 20512 | tf_op jit(solution)/shard_map/ppermute | solution.py:18
  38.3 0.6 %shard_map.73 = (f32[1,16,256]{2,1,0:T(8,128)}, f32[1,1]{1,0:T(1,128)}) custom-call(f32[40,128]{1,0:T(8,128)S(1)} %get-tuple-element.20.refs_0_, f32[40,128]{1,0:T(8,128)S(1)} %collective-permute-done.13.refs_1_, f32[40,128]{1,0:T(8,128)S(1)} %collective-permute-done.14.refs_2_, f32[40,128]{1,0:T(8,128)S(1)} %collective-permute-done.15.refs_3_), custom_call_target="tpu_custom_call" | custom-call | tf_op jit(solution)/shard_map/pallas_call | solution.py:226
  (24 shorter events, 0.4 us)
Async XLA Ops:
  0.6 4.2 %copy-start = (bf16[128,16,256]{2,1,0:T(8,128)(2,1)S(1)}, bf16[128,16,256]{2,1,0:T(8,128)(2,1)}, u32[]{:S(2)}) copy-start(bf16[128,16,256]{2,1,0:T(8,128)(2,1)} %kernel_ref.1) | copy-start | bytes 3145732
  0.6 5.6 %collective-permute-start = (bf16[1,16,256]{2,1,0:T(8,128)(2,1)}, bf16[1,16,256]{2,1,0:T(8,128)(2,1)S(1)}, u32[]{:S(2)}, u32[]{:S(2)}) collective-permute-start(bf16[1,16,256]{2,1,0:T(8,128)(2,1)} %refs_0_.3), channel_id=1, source_target_pairs={{0,8},{8,0},{16,24},{24,16},{1,9},{9,1},{17,25},{25,17},{2,10},{10... | collective-permute-start | bytes 24584 | tf_op jit(solution)/shard_map/ppermute | solution.py:18
  1.2 5.1 %collective-permute-start.1 = (bf16[1,16,256]{2,1,0:T(8,128)(2,1)}, bf16[1,16,256]{2,1,0:T(8,128)(2,1)S(1)}, u32[]{:S(2)}, u32[]{:S(2)}) collective-permute-start(bf16[1,16,256]{2,1,0:T(8,128)(2,1)} %refs_0_.3), channel_id=1, source_target_pairs={{0,16},{8,24},{16,0},{24,8},{1,17},{9,25},{17,1},{25,9},{2,18},{10... | collective-permute-start | bytes 24584 | tf_op jit(solution)/shard_map/ppermute | solution.py:18
  3.7 3.3 %collective-permute-start.2 = (bf16[1,16,256]{2,1,0:T(8,128)(2,1)}, bf16[1,16,256]{2,1,0:T(8,128)(2,1)S(1)}, u32[]{:S(2)}, u32[]{:S(2)}) collective-permute-start(bf16[1,16,256]{2,1,0:T(8,128)(2,1)} %refs_0_.3), channel_id=1, source_target_pairs={{0,24},{8,16},{16,8},{24,0},{1,25},{9,17},{17,9},{25,1},{2,26},{10... | collective-permute-start | bytes 24584 | tf_op jit(solution)/shard_map/ppermute | solution.py:18
  5.5 1.5 %copy-start.2 = (bf16[1,16,256]{2,1,0:T(8,128)(2,1)S(1)}, bf16[1,16,256]{2,1,0:T(8,128)(2,1)}, u32[]{:S(2)}) copy-start(bf16[1,16,256]{2,1,0:T(8,128)(2,1)} %refs_0_.3) | copy-start | bytes 24580
  6.2 3.6 %copy-start.1 = (f32[4,128,256]{2,1,0:T(8,128)S(1)}, f32[4,128,256]{2,1,0:T(8,128)}, u32[]{:S(2)}) copy-start(f32[4,128,256]{2,1,0:T(8,128)} %refs_6_.1) | copy-start | bytes 1572868
  7.7 4.7 %collective-permute-start.4 = (bf16[256,128]{1,0:T(8,128)(2,1)S(1)}, bf16[256,128]{1,0:T(8,128)(2,1)S(1)}, u32[]{:S(2)}, u32[]{:S(2)}) collective-permute-start(bf16[256,128]{1,0:T(8,128)(2,1)S(1)} %get-tuple-element.16), channel_id=1, source_target_pairs={{0,1},{1,0},{2,3},{3,2},{4,5},{5,4},{6,7},{7,6},{8,9},{9,8},{10,11... | collective-permute-start | bytes 196616 | tf_op jit(solution)/shard_map/ppermute | solution.py:18
  9.3 0.7 %copy-start.3 = (f32[128]{0:T(128)S(1)}, f32[128]{0:T(128)}, u32[]{:S(2)}) copy-start(f32[128]{0:T(128)} %param.7) | copy-start | bytes 1540
  9.3 6.8 %collective-permute-start.3 = (bf16[256,128]{1,0:T(8,128)(2,1)S(1)}, bf16[256,128]{1,0:T(8,128)(2,1)S(1)}, u32[]{:S(2)}, u32[]{:S(2)}) collective-permute-start(bf16[256,128]{1,0:T(8,128)(2,1)S(1)} %get-tuple-element.14), channel_id=1, source_target_pairs={{0,1},{1,0},{2,3},{3,2},{4,5},{5,4},{6,7},{7,6},{8,9},{9,8},{10,11... | collective-permute-start | bytes 196616 | tf_op jit(solution)/shard_map/ppermute | solution.py:18
  12.4 5.8 %collective-permute-start.5 = (bf16[128,128]{1,0:T(8,128)(2,1)S(1)}, bf16[128,128]{1,0:T(8,128)(2,1)S(1)}, u32[]{:S(2)}, u32[]{:S(2)}) collective-permute-start(bf16[128,128]{1,0:T(8,128)(2,1)S(1)} %get-tuple-element.17), channel_id=1, source_target_pairs={{0,6},{1,7},{2,4},{3,5},{4,2},{5,3},{6,0},{7,1},{8,14},{9,15},{10,... | collective-permute-start | bytes 98312 | tf_op jit(solution)/shard_map/ppermute | solution.py:18
  16.1 4.8 %collective-permute-start.6 = (bf16[128,128]{1,0:T(8,128)(2,1)S(1)}, bf16[128,128]{1,0:T(8,128)(2,1)S(1)}, u32[]{:S(2)}, u32[]{:S(2)}) collective-permute-start(bf16[128,128]{1,0:T(8,128)(2,1)S(1)} %get-tuple-element.18), channel_id=1, source_target_pairs={{0,4},{1,5},{2,6},{3,7},{4,0},{5,1},{6,2},{7,3},{8,12},{9,13},{10,... | collective-permute-start | bytes 98312 | tf_op jit(solution)/shard_map/ppermute | solution.py:18
  16.1 4.8 %collective-permute-start.7 = (bf16[128,128]{1,0:T(8,128)(2,1)S(1)}, bf16[128,128]{1,0:T(8,128)(2,1)S(1)}, u32[]{:S(2)}, u32[]{:S(2)}) collective-permute-start(bf16[128,128]{1,0:T(8,128)(2,1)S(1)} %get-tuple-element.19), channel_id=1, source_target_pairs={{0,2},{1,3},{2,0},{3,1},{4,6},{5,7},{6,4},{7,5},{8,10},{9,11},{10,... | collective-permute-start | bytes 98312 | tf_op jit(solution)/shard_map/ppermute | solution.py:18
  20.9 4.5 %collective-permute-start.8 = (bf16[144,128]{1,0:T(8,128)(2,1)S(1)}, bf16[144,128]{1,0:T(8,128)(2,1)S(1)}, u32[]{:S(2)}, u32[]{:S(2)}) collective-permute-start(bf16[144,128]{1,0:T(8,128)(2,1)S(1)} %shard_map.65.refs_0_), channel_id=1, source_target_pairs={{0,2},{1,3},{2,0},{3,1},{4,6},{5,7},{6,4},{7,5},{8,10},{9,11},{10,... | collective-permute-start | bytes 110600 | tf_op jit(solution)/shard_map/ppermute | solution.py:18
  21.0 6.4 %collective-permute-start.9 = (bf16[144,128]{1,0:T(8,128)(2,1)S(1)}, bf16[144,128]{1,0:T(8,128)(2,1)S(1)}, u32[]{:S(2)}, u32[]{:S(2)}) collective-permute-start(bf16[144,128]{1,0:T(8,128)(2,1)S(1)} %shard_map.65.refs_0_), channel_id=1, source_target_pairs={{0,4},{1,5},{2,6},{3,7},{4,0},{5,1},{6,2},{7,3},{8,12},{9,13},{10,... | collective-permute-start | bytes 110600 | tf_op jit(solution)/shard_map/ppermute | solution.py:18
  23.5 5.8 %collective-permute-start.10 = (bf16[144,128]{1,0:T(8,128)(2,1)S(1)}, bf16[144,128]{1,0:T(8,128)(2,1)S(1)}, u32[]{:S(2)}, u32[]{:S(2)}) collective-permute-start(bf16[144,128]{1,0:T(8,128)(2,1)S(1)} %shard_map.65.refs_0_), channel_id=1, source_target_pairs={{0,6},{1,7},{2,4},{3,5},{4,2},{5,3},{6,0},{7,1},{8,14},{9,15},{10,... | collective-permute-start | bytes 110600 | tf_op jit(solution)/shard_map/ppermute | solution.py:18
  25.4 7.1 %collective-permute-start.11 = (bf16[272,128]{1,0:T(8,128)(2,1)S(1)}, bf16[272,128]{1,0:T(8,128)(2,1)S(1)}, u32[]{:S(2)}, u32[]{:S(2)}) collective-permute-start(bf16[272,128]{1,0:T(8,128)(2,1)S(1)} %shard_map.66.group_ref.refs_4_), channel_id=1, source_target_pairs={{0,1},{1,0},{2,3},{3,2},{4,5},{5,4},{6,7},{7,6},{8,9},{9,8},{10,11... | collective-permute-start | bytes 208904 | tf_op jit(solution)/shard_map/ppermute | solution.py:18
  29.2 4.4 %collective-permute-start.12 = (bf16[272,128]{1,0:T(8,128)(2,1)S(1)}, bf16[272,128]{1,0:T(8,128)(2,1)S(1)}, u32[]{:S(2)}, u32[]{:S(2)}) collective-permute-start(bf16[272,128]{1,0:T(8,128)(2,1)S(1)} %shard_map.69.group_ref.refs_5_), channel_id=1, source_target_pairs={{0,1},{1,0},{2,3},{3,2},{4,5},{5,4},{6,7},{7,6},{8,9},{9,8},{10,11... | collective-permute-start | bytes 208904 | tf_op jit(solution)/shard_map/ppermute | solution.py:18
  34.4 3.3 %collective-permute-start.13 = (f32[40,128]{1,0:T(8,128)S(1)}, f32[40,128]{1,0:T(8,128)S(1)}, u32[]{:S(2)}, u32[]{:S(2)}) collective-permute-start(f32[40,128]{1,0:T(8,128)S(1)} %get-tuple-element.21), channel_id=1, source_target_pairs={{0,24},{8,16},{16,8},{24,0},{1,25},{9,17},{17,9},{25,1},{2,26},{10... | collective-permute-start | bytes 61448 | tf_op jit(solution)/shard_map/ppermute | solution.py:18
  34.5 3.8 %collective-permute-start.14 = (f32[40,128]{1,0:T(8,128)S(1)}, f32[40,128]{1,0:T(8,128)S(1)}, u32[]{:S(2)}, u32[]{:S(2)}) collective-permute-start(f32[40,128]{1,0:T(8,128)S(1)} %get-tuple-element.22), channel_id=1, source_target_pairs={{0,16},{8,24},{16,0},{24,8},{1,17},{9,25},{17,1},{25,9},{2,18},{10... | collective-permute-start | bytes 61448 | tf_op jit(solution)/shard_map/ppermute | solution.py:18
  35.2 3.1 %collective-permute-start.15 = (f32[40,128]{1,0:T(8,128)S(1)}, f32[40,128]{1,0:T(8,128)S(1)}, u32[]{:S(2)}, u32[]{:S(2)}) collective-permute-start(f32[40,128]{1,0:T(8,128)S(1)} %get-tuple-element.23), channel_id=1, source_target_pairs={{0,8},{8,0},{16,24},{24,16},{1,9},{9,1},{17,25},{25,17},{2,10},{10... | collective-permute-start | bytes 61448 | tf_op jit(solution)/shard_map/ppermute | solution.py:18

commit v7 on v6

--- a/solution.py
+++ b/solution.py
@@ -40,7 +40,7 @@
         out_ref[lags] = turned.reshape(count, points, sensors).astype(jnp.bfloat16)
 
 
-def forward_body(away, near, far, lags, n_models, n_x, *refs):
+def forward_body(away, start, slots, near, lags, n_models, n_x, *refs):
     models, xs, refs = refs[:n_models], refs[n_models : n_models + n_x], refs[n_models + n_x :]
     points, sensors = xs[0].shape[1:]
     ks = [(x_ref, k) for x_ref in xs for k in range(x_ref.shape[0])]
@@ -49,13 +49,13 @@
     place, block = j // near, lax.rem(j, near) ^ away
     if away == 0:
         observed_ref, weights_ref, out_ref, all_ref, ut_ref, u_ref, acc_ref, seen_ref, scale_ref, sems = refs
-        outs = [out_ref]
     else:
-        outs, (all_ref, ut_ref, u_ref, acc_ref) = refs[:-4], refs[-4:]
-    vectors, of_block = all_ref.shape[0], u_ref.shape[0]
-    rows = of_block * steps // far
+        out_ref, all_ref, ut_ref, u_ref, acc_ref = refs
+    vectors, of_group = all_ref.shape[0], u_ref.shape[0]
+    rows = of_group * steps // slots
+    group = (place ^ start) // slots
     if away == 0:
-        first = (block * far + place) * rows
+        first = (block * slots + place) * rows
         fetch_seen = pltpu.make_async_copy(observed_ref.at[me ^ (first // steps)], seen_ref, sems.at[0])
         fetch_scale = pltpu.make_async_copy(weights_ref, scale_ref, sems.at[1])
         fetch_seen.start()
@@ -64,8 +64,8 @@
     for v in range(vectors):
         ref = models[v * n_models // vectors]
         all_ref[v] = ref[v % ref.shape[0]].astype(jnp.float32)
-    for v in range(of_block):
-        series = all_ref[block * of_block + v]
+    for v in range(of_group):
+        series = all_ref[block * (vectors // near) + group * of_group + v]
         for kl in range(lags):
             moved = series if kl == 0 else jnp.where(lane >= kl, pltpu.roll(series, kl, 1), 0.0)
             ut_ref[v, kl * points : (kl + 1) * points, :] = moved
@@ -74,9 +74,9 @@
         left = steps - k0
         x_ref, at = ks[k0]
         pair = [x_ref[k : k + lags].reshape(lags * points, sensors) for k in (at, at + lags)]
-        some = u_ref[:, :left, :].reshape(of_block * left, lags * points)
+        some = u_ref[:, :left, :].reshape(of_group * left, lags * points)
         term = jnp.dot(some, jnp.concatenate(pair, axis=1), preferred_element_type=jnp.float32)
-        for v in range(of_block):
+        for v in range(of_group):
             at, end = v * steps, (v + 1) * steps
             part = term[v * left : (v + 1) * left]
             if k0 == 0:
@@ -84,16 +84,15 @@
             else:
                 acc_ref[at + k0 : end, :] += part[:, :sensors]
             acc_ref[at + k0 + lags : end, :] += part[: left - lags, sensors:]
-    for b in range(far):
-        there = pl.multiple_of((place ^ b) * rows, rows)
-        ref, at = outs[b * len(outs) // far], b % (far // len(outs)) * rows
-        ref[at : at + rows, :] = acc_ref[pl.ds(there, rows), :].astype(ref.dtype)
+    for b in range(slots):
+        there = pl.multiple_of(((place ^ (start + b)) - group * slots) * rows, rows)
+        out_ref[b * rows : (b + 1) * rows, :] = acc_ref[pl.ds(there, rows), :].astype(out_ref.dtype)
     if away == 0:
         fetch_seen.wait()
         fetch_scale.wait()
         ut_ref[0, :, :sensors] = seen_ref[...].T
         out_ref[:rows, :] -= ut_ref[0, pl.ds(pl.multiple_of(first % steps, rows), rows), :sensors]
-        out_ref[far * rows :, :] = jnp.broadcast_to(scale_ref[...], (WEIGHT_ROWS, sensors))
+        out_ref[slots * rows :, :] = jnp.broadcast_to(scale_ref[...], (WEIGHT_ROWS, sensors))
 
 
 def middle_body(near, start, count, own_ref, *refs):
@@ -253,26 +252,27 @@
 
     models = [model] + [swap(model, "sens", step) for step in range(1, n_sens)]
     half = steps - steps // lanes // 2 * lanes
-    xs = [
-        call(
-            turn_body,
-            struct((count, points, sensors), kernel.dtype),
-            (some,),
-            VMEM_LIMIT,
-            scratch_shapes=[pltpu.VMEM((count * points, sensors), jnp.float32)]
-            + [pltpu.VMEM((sensors * points, lanes), jnp.float32)] * (count // lanes),
-            cost_estimate=pl.CostEstimate(flops=0, bytes_accessed=3 * kernel.size, transcendentals=0),
+    xs = [jnp.transpose(kernel[:, :, :half], (2, 1, 0))]
+    if half < steps:
+        xs.append(
+            call(
+                turn_body,
+                struct((steps - half, points, sensors), kernel.dtype),
+                (kernel,),
+                VMEM_LIMIT,
+                scratch_shapes=[pltpu.VMEM(((steps - half) * points, sensors), jnp.float32)]
+                + [pltpu.VMEM((sensors * points, lanes), jnp.float32)] * ((steps - half) // lanes),
+                cost_estimate=pl.CostEstimate(flops=0, bytes_accessed=3 * kernel.size, transcendentals=0),
+            )
         )
-        for count, some in ((half, kernel[:, :, :half]), (steps - half, kernel))
-        if count > 0
-    ]
-
-    def forward(away):
+
+    def forward(away, start, count):
+        of_part = of_block * count // far
         scratch = [
             pltpu.VMEM((vectors, points, steps), jnp.float32),
-            pltpu.VMEM((of_block, lags * points, steps), jnp.float32),
-            pltpu.VMEM((of_block, steps, lags * points), jnp.bfloat16),
-            pltpu.VMEM((of_block * steps, sensors), jnp.float32),
+            pltpu.VMEM((of_part, lags * points, steps), jnp.float32),
+            pltpu.VMEM((of_part, steps, lags * points), jnp.bfloat16),
+            pltpu.VMEM((of_part * steps, sensors), jnp.float32),
         ]
         operands = [*models, *xs]
         specs = [vmem] * len(operands)
@@ -284,22 +284,24 @@
             ]
             operands += [observed, weights[None, :]]
             specs += [hbm] * 2
-            out = struct((far * rows + WEIGHT_ROWS, sensors), jnp.float32)
+            out = struct((count * rows + WEIGHT_ROWS, sensors), jnp.float32)
         else:
-            out = [struct((slots * rows, sensors), jnp.bfloat16)] * n_groups
+            out = struct((count * rows, sensors), jnp.bfloat16)
         return call(
-            functools.partial(forward_body, away, near, far, lags, len(models), len(xs)),
+            functools.partial(forward_body, away, start, count, near, lags, len(models), len(xs)),
             out,
             operands,
             VMEM_LIMIT,
             in_specs=specs,
             scratch_shapes=scratch,
-            cost_estimate=cost,
+            cost_estimate=cost if away == 0 else piece_cost,
         )
 
-    sent = [forward(away) for away in range(1, near)]
-    crossed = [[swap(some[g], "par", away) for away, some in enumerate(sent, 1)] for g in range(n_groups - 1, -1, -1)]
-    sums = forward(0)
+    crossed = [
+        [swap(forward(away, g * slots, slots), "par", away) for away in range(1, near)]
+        for g in range(n_groups - 1, -1, -1)
+    ]
+    sums = forward(0, 0, far)
     terms = []
     for g, some in zip(range(n_groups - 1, -1, -1), crossed):
         outs = [struct((rows, sensors), jnp.bfloat16)] * slots

time: 39.1 us -> 38.7 us (0.990)
  starting transfers between devices: 19.7 us -> 21 us
  waiting for transfers between devices: 10.3 us -> 9.13 us
    ppermute x16, starting transfers between devices: 19.7 us -> 21 us  [swap(): lax.ppermute(value, axis, [(i, i ^ step) for i in range(lax.axis_size(axi...]
    ppermute x16, waiting for transfers between devices: 10.3 us -> 9.13 us  [swap(): lax.ppermute(value, axis, [(i, i ^ step) for i in range(lax.axis_size(axi...]
    slice x1 -> x2, local copies, waits for them, and re-layouts: 1.08 us -> 0.38 us  [local(): xs = [jnp.transpose(kernel[:, :, :half], (2, 1, 0))]]
    unnamed x8 -> x9, local copies, waits for them, and re-layouts: 0.16 us -> 0.83 us
    pallas_call x15, Pallas kernels: 6.85 us -> 6.46 us  [call(): pl.pallas_call(body, out_shape=out_shape, out_specs=jax.tree.map(lambda _...]
  transfers between devices with their start and end apart: 16 -> 16, of which waited for: 8 -> 7; matrix products, arithmetic and copies ran while one was open for 3% -> 2% of each run, Pallas kernels for 12% -> 12%
where the time goes in v7:
time: 38.7 us; the launch traced here: 38.6 us
  starting transfers between devices  21 us (54%)
  waiting for transfers between devices  9.13 us (24%)
  Pallas kernels  6.46 us (17%)
  local copies, waits for them, and re-layouts  1.21 us (3%)
  between operations  0.79 us (2%)
    ppermute x16, starting transfers between devices, swap(): lax.ppermute(value, axis, [(i, i ^ step) for i in range(lax.axis_size(axi...  21 us
    ppermute x16, waiting for transfers between devices, swap(): lax.ppermute(value, axis, [(i, i ^ step) for i in range(lax.axis_size(axi...  9.13 us
    pallas_call x15, Pallas kernels, call(): pl.pallas_call(body, out_shape=out_shape, out_specs=jax.tree.map(lambda _...  6.46 us
    unnamed x9, local copies, waits for them, and re-layouts  0.83 us
  transfers between devices with their start and end apart: 16, of which 7 were waited for; matrix products, arithmetic and copies ran while one was open for 2% of the time, Pallas kernels for 12%

profile of v7, /device:TPU:0, one launch (start us, length us, event | category | flops | bytes accessed | tf_op | source)
XLA Modules:
  0.0 38.6 jit_solution(5298159895540739203)
XLA Ops:
  0.6 0.5 %collective-permute-start = (bf16[1,16,256]{2,1,0:T(8,128)(2,1)}, bf16[1,16,256]{2,1,0:T(8,128)(2,1)S(1)}, u32[]{:S(2)}, u32[]{:S(2)}) collective-permute-start(bf16[1,16,256]{2,1,0:T(8,128)(2,1)} %refs_0_.5), channel_id=1, source_target_pairs={{0,8},{8,0},{16,24},{24,16},{1,9},{9,1},{17,25},{25,17},{2,10},{10... | collective-permute-start | bytes 24584 | tf_op jit(solution)/shard_map/ppermute | solution.py:18
  1.2 2.6 %collective-permute-start.1 = (bf16[1,16,256]{2,1,0:T(8,128)(2,1)}, bf16[1,16,256]{2,1,0:T(8,128)(2,1)S(1)}, u32[]{:S(2)}, u32[]{:S(2)}) collective-permute-start(bf16[1,16,256]{2,1,0:T(8,128)(2,1)} %refs_0_.5), channel_id=1, source_target_pairs={{0,16},{8,24},{16,0},{24,8},{1,17},{9,25},{17,1},{25,9},{2,18},{10... | collective-permute-start | bytes 24584 | tf_op jit(solution)/shard_map/ppermute | solution.py:18
  3.8 0.6 %shard_map.59.refs_5_.refs_1_ = bf16[128,16,128]{2,1,0:T(8,128)(2,1)S(1)} custom-call(bf16[128,16,256]{2,1,0:T(8,128)(2,1)S(1)} %copy-done), custom_call_target="tpu_custom_call" | custom-call | bytes 1572864 | tf_op jit(solution)/shard_map/pallas_call | solution.py:225
  4.5 0.4 slice-done
  4.8 0.7 %copy.7 = bf16[128,16,128]{0,1,2:T(8,128)(2,1)S(1)} copy(bf16[128,16,128]{2,1,0:T(8,128)(2,1)S(1)} %slice-done) | data formatting | bytes 1048576
  5.6 1.4 %collective-permute-done.2.refs_3_ = bf16[1,16,256]{2,1,0:T(8,128)(2,1)S(1)} collective-permute-done((bf16[1,16,256]{2,1,0:T(8,128)(2,1)}, bf16[1,16,256]{2,1,0:T(8,128)(2,1)S(1)}, u32[]{:S(2)}, u32[]{:S(2)}) %collective-permute-start.2) | collective-permute-done | bytes 8224 | tf_op jit(solution)/shard_map/ppermute | solution.py:18
  7.0 0.5 %shard_map.63 = bf16[256,128]{1,0:T(8,128)(2,1)S(1)} custom-call(bf16[1,16,256]{2,1,0:T(8,128)(2,1)S(1)} %copy-done.1, bf16[1,16,256]{2,1,0:T(8,128)(2,1)S(1)} %collective-permute-done.refs_1_, bf16[1,16,256]{2,1,0:T(8,128)(2,1)S(1)} %collective-permute-done.1.refs_2_, bf16[1,16,256]{2,1,0:T(8,128)(2,1)S(1)} %collective-permute-done.2.refs_3_, ...), custom_call_target="tpu_custom_call" | custom-call | flops 268435456 | bytes 1048576 | tf_op jit(solution)/shard_map/pallas_call | solution.py:225
  7.5 1.6 %collective-permute-start.4 = (bf16[256,128]{1,0:T(8,128)(2,1)S(1)}, bf16[256,128]{1,0:T(8,128)(2,1)S(1)}, u32[]{:S(2)}, u32[]{:S(2)}) collective-permute-start(bf16[256,128]{1,0:T(8,128)(2,1)S(1)} %shard_map.63), channel_id=1, source_target_pairs={{0,1},{1,0},{2,3},{3,2},{4,5},{5,4},{6,7},{7,6},{8,9},{9,8},{10,11... | collective-permute-start | bytes 196616 | tf_op jit(solution)/shard_map/ppermute | solution.py:18
  9.1 0.5 %shard_map.61 = bf16[256,128]{1,0:T(8,128)(2,1)S(1)} custom-call(bf16[1,16,256]{2,1,0:T(8,128)(2,1)S(1)} %copy-done.1, bf16[1,16,256]{2,1,0:T(8,128)(2,1)S(1)} %collective-permute-done.refs_1_, bf16[1,16,256]{2,1,0:T(8,128)(2,1)S(1)} %collective-permute-done.1.refs_2_, bf16[1,16,256]{2,1,0:T(8,128)(2,1)S(1)} %collective-permute-done.2.refs_3_, ...), custom_call_target="tpu_custom_call" | custom-call | flops 268435456 | bytes 1048576 | tf_op jit(solution)/shard_map/pallas_call | solution.py:225
  9.6 0.6 %collective-permute-start.3 = (bf16[256,128]{1,0:T(8,128)(2,1)S(1)}, bf16[256,128]{1,0:T(8,128)(2,1)S(1)}, u32[]{:S(2)}, u32[]{:S(2)}) collective-permute-start(bf16[256,128]{1,0:T(8,128)(2,1)S(1)} %shard_map.61), channel_id=1, source_target_pairs={{0,1},{1,0},{2,3},{3,2},{4,5},{5,4},{6,7},{7,6},{8,9},{9,8},{10,11... | collective-permute-start | bytes 196616 | tf_op jit(solution)/shard_map/ppermute | solution.py:18
  10.1 0.1 copy-done.3
  10.2 1.0 %shard_map.60.own_ref = f32[520,128]{1,0:T(8,128)S(1)} custom-call(bf16[1,16,256]{2,1,0:T(8,128)(2,1)S(1)} %copy-done.1, bf16[1,16,256]{2,1,0:T(8,128)(2,1)S(1)} %collective-permute-done.refs_1_, bf16[1,16,256]{2,1,0:T(8,128)(2,1)S(1)} %collective-permute-done.1.refs_2_, bf16[1,16,256]{2,1,0:T(8,128)(2,1)S(1)} %collective-permute-done.2.refs_3_, ...), custom_call_target="tpu_custom_call" | custom-call | flops 536870912 | bytes 1048576 | tf_op jit(solution)/shard_map/pallas_call | solution.py:225
  11.2 0.6 %collective-permute-done.4.refs_0_ = bf16[256,128]{1,0:T(8,128)(2,1)S(1)} collective-permute-done((bf16[256,128]{1,0:T(8,128)(2,1)S(1)}, bf16[256,128]{1,0:T(8,128)(2,1)S(1)}, u32[]{:S(2)}, u32[]{:S(2)}) %collective-permute-start.4) | collective-permute-done | bytes 65568 | tf_op jit(solution)/shard_map/ppermute | solution.py:18
  11.9 3.7 %collective-permute-start.5 = (bf16[128,128]{1,0:T(8,128)(2,1)S(1)}, bf16[128,128]{1,0:T(8,128)(2,1)S(1)}, u32[]{:S(2)}, u32[]{:S(2)}) collective-permute-start(bf16[128,128]{1,0:T(8,128)(2,1)S(1)} %get-tuple-element.13), channel_id=1, source_target_pairs={{0,6},{1,7},{2,4},{3,5},{4,2},{5,3},{6,0},{7,1},{8,14},{9,15},{10,... | collective-permute-start | bytes 98312 | tf_op jit(solution)/shard_map/ppermute | solution.py:18
  15.5 0.8 %collective-permute-start.7 = (bf16[128,128]{1,0:T(8,128)(2,1)S(1)}, bf16[128,128]{1,0:T(8,128)(2,1)S(1)}, u32[]{:S(2)}, u32[]{:S(2)}) collective-permute-start(bf16[128,128]{1,0:T(8,128)(2,1)S(1)} %get-tuple-element.15), channel_id=1, source_target_pairs={{0,2},{1,3},{2,0},{3,1},{4,6},{5,7},{6,4},{7,5},{8,10},{9,11},{10,... | collective-permute-start | bytes 98312 | tf_op jit(solution)/shard_map/ppermute | solution.py:18
  16.4 1.4 %collective-permute-done.5.refs_0_ = bf16[128,128]{1,0:T(8,128)(2,1)S(1)} collective-permute-done((bf16[128,128]{1,0:T(8,128)(2,1)S(1)}, bf16[128,128]{1,0:T(8,128)(2,1)S(1)}, u32[]{:S(2)}, u32[]{:S(2)}) %collective-permute-start.5) | collective-permute-done | bytes 32800 | tf_op jit(solution)/shard_map/ppermute | solution.py:18
  17.8 2.5 %collective-permute-done.6.refs_1_ = bf16[128,128]{1,0:T(8,128)(2,1)S(1)} collective-permute-done((bf16[128,128]{1,0:T(8,128)(2,1)S(1)}, bf16[128,128]{1,0:T(8,128)(2,1)S(1)}, u32[]{:S(2)}, u32[]{:S(2)}) %collective-permute-start.6) | collective-permute-done | bytes 32800 | tf_op jit(solution)/shard_map/ppermute | solution.py:18
  20.5 2.2 %collective-permute-start.9 = (bf16[144,128]{1,0:T(8,128)(2,1)S(1)}, bf16[144,128]{1,0:T(8,128)(2,1)S(1)}, u32[]{:S(2)}, u32[]{:S(2)}) collective-permute-start(bf16[144,128]{1,0:T(8,128)(2,1)S(1)} %shard_map.65.refs_0_), channel_id=1, source_target_pairs={{0,4},{1,5},{2,6},{3,7},{4,0},{5,1},{6,2},{7,3},{8,12},{9,13},{10,... | collective-permute-start | bytes 110600 | tf_op jit(solution)/shard_map/ppermute | solution.py:18
  22.6 2.2 %collective-permute-start.10 = (bf16[144,128]{1,0:T(8,128)(2,1)S(1)}, bf16[144,128]{1,0:T(8,128)(2,1)S(1)}, u32[]{:S(2)}, u32[]{:S(2)}) collective-permute-start(bf16[144,128]{1,0:T(8,128)(2,1)S(1)} %shard_map.65.refs_0_), channel_id=1, source_target_pairs={{0,6},{1,7},{2,4},{3,5},{4,2},{5,3},{6,0},{7,1},{8,14},{9,15},{10,... | collective-permute-start | bytes 110600 | tf_op jit(solution)/shard_map/ppermute | solution.py:18
  24.9 2.3 %collective-permute-start.11 = (bf16[272,128]{1,0:T(8,128)(2,1)S(1)}, bf16[272,128]{1,0:T(8,128)(2,1)S(1)}, u32[]{:S(2)}, u32[]{:S(2)}) collective-permute-start(bf16[272,128]{1,0:T(8,128)(2,1)S(1)} %shard_map.66.group_ref.refs_4_), channel_id=1, source_target_pairs={{0,1},{1,0},{2,3},{3,2},{4,5},{5,4},{6,7},{7,6},{8,9},{9,8},{10,11... | collective-permute-start | bytes 208904 | tf_op jit(solution)/shard_map/ppermute | solution.py:18
  27.1 0.2 shard_map.67.left_ref.refs_3_
  27.3 1.1 %collective-permute-done.10.refs_1_ = bf16[144,128]{1,0:T(8,128)(2,1)S(1)} collective-permute-done((bf16[144,128]{1,0:T(8,128)(2,1)S(1)}, bf16[144,128]{1,0:T(8,128)(2,1)S(1)}, u32[]{:S(2)}, u32[]{:S(2)}) %collective-permute-start.10) | collective-permute-done | bytes 36896 | tf_op jit(solution)/shard_map/ppermute | solution.py:18
  28.4 2.5 %collective-permute-start.12 = (bf16[272,128]{1,0:T(8,128)(2,1)S(1)}, bf16[272,128]{1,0:T(8,128)(2,1)S(1)}, u32[]{:S(2)}, u32[]{:S(2)}) collective-permute-start(bf16[272,128]{1,0:T(8,128)(2,1)S(1)} %shard_map.69.group_ref.refs_5_), channel_id=1, source_target_pairs={{0,1},{1,0},{2,3},{3,2},{4,5},{5,4},{6,7},{7,6},{8,9},{9,8},{10,11... | collective-permute-start | bytes 208904 | tf_op jit(solution)/shard_map/ppermute | solution.py:18
  30.9 0.7 %shard_map.68.refs_0_ = f32[1,16,256]{2,1,0:T(8,128)S(1)} custom-call(bf16[272,128]{1,0:T(8,128)(2,1)S(1)} %shard_map.66.group_ref.refs_4_, bf16[256,2048]{1,0:T(8,128)(2,1)S(1)} %shard_map.67.left_ref.refs_3_), custom_call_target="tpu_custom_call" | custom-call | flops 268435456 | bytes 1048576 | tf_op jit(solution)/shard_map/pallas_call | solution.py:225
  31.7 0.7 %shard_map.70.refs_1_ = f32[1,16,256]{2,1,0:T(8,128)S(1)} custom-call(bf16[272,128]{1,0:T(8,128)(2,1)S(1)} %shard_map.69.group_ref.refs_5_, bf16[256,2048]{1,0:T(8,128)(2,1)S(1)} %shard_map.67.left_ref.refs_3_), custom_call_target="tpu_custom_call" | custom-call | flops 268435456 | bytes 1048576 | tf_op jit(solution)/shard_map/pallas_call | solution.py:225
  32.4 0.7 %shard_map.71.refs_2_ = f32[1,16,256]{2,1,0:T(8,128)S(1)} custom-call(bf16[272,128]{1,0:T(8,128)(2,1)S(1)} %collective-permute-done.11.group_ref.refs_6_, bf16[256,2048]{1,0:T(8,128)(2,1)S(1)} %shard_map.67.left_ref.refs_3_), custom_call_target="tpu_custom_call" | custom-call | flops 268435456 | bytes 1048576 | tf_op jit(solution)/shard_map/pallas_call | solution.py:225
  33.2 0.8 %shard_map.72 = (f32[40,128]{1,0:T(8,128)S(1)}, f32[40,128]{1,0:T(8,128)S(1)}, f32[40,128]{1,0:T(8,128)S(1)}, f32[40,128]{1,0:T(8,128)S(1)}) custom-call(f32[1,16,256]{2,1,0:T(8,128)S(1)} %shard_map.68.refs_0_, f32[1,16,256]{2,1,0:T(8,128)S(1)} %shard_map.70.refs_1_, f32[1,16,256]{2,1,0:T(8,128)S(1)} %shard_map.71.refs_2_, ...), custom_call_target="tpu_custom_call" | custom-call | flops 268435456 | bytes 1048576 | tf_op jit(solution)/shard_map/pallas_call | solution.py:225
  34.1 0.6 %collective-permute-start.14 = (f32[40,128]{1,0:T(8,128)S(1)}, f32[40,128]{1,0:T(8,128)S(1)}, u32[]{:S(2)}, u32[]{:S(2)}) collective-permute-start(f32[40,128]{1,0:T(8,128)S(1)} %get-tuple-element.18), channel_id=1, source_target_pairs={{0,16},{8,24},{16,0},{24,8},{1,17},{9,25},{17,1},{25,9},{2,18},{10... | collective-permute-start | bytes 61448 | tf_op jit(solution)/shard_map/ppermute | solution.py:18
  34.7 1.2 %collective-permute-start.15 = (f32[40,128]{1,0:T(8,128)S(1)}, f32[40,128]{1,0:T(8,128)S(1)}, u32[]{:S(2)}, u32[]{:S(2)}) collective-permute-start(f32[40,128]{1,0:T(8,128)S(1)} %get-tuple-element.19), channel_id=1, source_target_pairs={{0,8},{8,0},{16,24},{24,16},{1,9},{9,1},{17,25},{25,17},{2,10},{10... | collective-permute-start | bytes 61448 | tf_op jit(solution)/shard_map/ppermute | solution.py:18
  35.9 1.3 %collective-permute-done.13.refs_1_ = f32[40,128]{1,0:T(8,128)S(1)} collective-permute-done((f32[40,128]{1,0:T(8,128)S(1)}, f32[40,128]{1,0:T(8,128)S(1)}, u32[]{:S(2)}, u32[]{:S(2)}) %collective-permute-start.13) | collective-permute-done | bytes 20512 | tf_op jit(solution)/shard_map/ppermute | solution.py:18
  37.3 0.7 %collective-permute-done.14.refs_2_ = f32[40,128]{1,0:T(8,128)S(1)} collective-permute-done((f32[40,128]{1,0:T(8,128)S(1)}, f32[40,128]{1,0:T(8,128)S(1)}, u32[]{:S(2)}, u32[]{:S(2)}) %collective-permute-start.14) | collective-permute-done | bytes 20512 | tf_op jit(solution)/shard_map/ppermute | solution.py:18
  37.9 0.6 %shard_map.73 = (f32[1,16,256]{2,1,0:T(8,128)}, f32[1,1]{1,0:T(1,128)}) custom-call(f32[40,128]{1,0:T(8,128)S(1)} %get-tuple-element.16.refs_0_, f32[40,128]{1,0:T(8,128)S(1)} %collective-permute-done.13.refs_1_, f32[40,128]{1,0:T(8,128)S(1)} %collective-permute-done.14.refs_2_, f32[40,128]{1,0:T(8,128)S(1)} %collective-permute-done.15.refs_3_), custom_call_target="tpu_custom_call" | custom-call | tf_op jit(solution)/shard_map/pallas_call | solution.py:225
  (26 shorter events, 0.4 us)
Async XLA Ops:
  0.6 3.2 %copy-start = (bf16[128,16,256]{2,1,0:T(8,128)(2,1)S(1)}, bf16[128,16,256]{2,1,0:T(8,128)(2,1)}, u32[]{:S(2)}) copy-start(bf16[128,16,256]{2,1,0:T(8,128)(2,1)} %kernel_ref.1) | copy-start | bytes 3145732
  0.6 4.9 %collective-permute-start = (bf16[1,16,256]{2,1,0:T(8,128)(2,1)}, bf16[1,16,256]{2,1,0:T(8,128)(2,1)S(1)}, u32[]{:S(2)}, u32[]{:S(2)}) collective-permute-start(bf16[1,16,256]{2,1,0:T(8,128)(2,1)} %refs_0_.5), channel_id=1, source_target_pairs={{0,8},{8,0},{16,24},{24,16},{1,9},{9,1},{17,25},{25,17},{2,10},{10... | collective-permute-start | bytes 24584 | tf_op jit(solution)/shard_map/ppermute | solution.py:18
  1.2 4.4 %collective-permute-start.1 = (bf16[1,16,256]{2,1,0:T(8,128)(2,1)}, bf16[1,16,256]{2,1,0:T(8,128)(2,1)S(1)}, u32[]{:S(2)}, u32[]{:S(2)}) collective-permute-start(bf16[1,16,256]{2,1,0:T(8,128)(2,1)} %refs_0_.5), channel_id=1, source_target_pairs={{0,16},{8,24},{16,0},{24,8},{1,17},{9,25},{17,1},{25,9},{2,18},{10... | collective-permute-start | bytes 24584 | tf_op jit(solution)/shard_map/ppermute | solution.py:18
  3.7 3.3 %collective-permute-start.2 = (bf16[1,16,256]{2,1,0:T(8,128)(2,1)}, bf16[1,16,256]{2,1,0:T(8,128)(2,1)S(1)}, u32[]{:S(2)}, u32[]{:S(2)}) collective-permute-start(bf16[1,16,256]{2,1,0:T(8,128)(2,1)} %refs_0_.5), channel_id=1, source_target_pairs={{0,24},{8,16},{16,8},{24,0},{1,25},{9,17},{17,9},{25,1},{2,26},{10... | collective-permute-start | bytes 24584 | tf_op jit(solution)/shard_map/ppermute | solution.py:18
  3.8 1.0 %slice-start = ((bf16[128,16,256]{2,1,0:T(8,128)(2,1)}), bf16[128,16,128]{2,1,0:T(8,128)(2,1)S(1)}, s32[]{:S(2)}) async-start(bf16[128,16,256]{2,1,0:T(8,128)(2,1)} %kernel_ref.1), calls=%async_computation | async-start | bytes 1048576 | tf_op jit(solution)/shard_map/slice | solution.py:255
  4.8 2.2 %copy-start.1 = (bf16[1,16,256]{2,1,0:T(8,128)(2,1)S(1)}, bf16[1,16,256]{2,1,0:T(8,128)(2,1)}, u32[]{:S(2)}) copy-start(bf16[1,16,256]{2,1,0:T(8,128)(2,1)} %refs_0_.5) | copy-start | bytes 24580
  7.5 2.7 %copy-start.2 = (f32[4,128,256]{2,1,0:T(8,128)S(1)}, f32[4,128,256]{2,1,0:T(8,128)}, u32[]{:S(2)}) copy-start(f32[4,128,256]{2,1,0:T(8,128)} %refs_6_.1) | copy-start | bytes 1572868
  7.5 4.3 %collective-permute-start.4 = (bf16[256,128]{1,0:T(8,128)(2,1)S(1)}, bf16[256,128]{1,0:T(8,128)(2,1)S(1)}, u32[]{:S(2)}, u32[]{:S(2)}) collective-permute-start(bf16[256,128]{1,0:T(8,128)(2,1)S(1)} %shard_map.63), channel_id=1, source_target_pairs={{0,1},{1,0},{2,3},{3,2},{4,5},{5,4},{6,7},{7,6},{8,9},{9,8},{10,11... | collective-permute-start | bytes 196616 | tf_op jit(solution)/shard_map/ppermute | solution.py:18
  9.6 0.7 %copy-start.3 = (f32[128]{0:T(128)S(1)}, f32[128]{0:T(128)}, u32[]{:S(2)}) copy-start(f32[128]{0:T(128)} %param.7) | copy-start | bytes 1540
  9.6 6.0 %collective-permute-start.3 = (bf16[256,128]{1,0:T(8,128)(2,1)S(1)}, bf16[256,128]{1,0:T(8,128)(2,1)S(1)}, u32[]{:S(2)}, u32[]{:S(2)}) collective-permute-start(bf16[256,128]{1,0:T(8,128)(2,1)S(1)} %shard_map.61), channel_id=1, source_target_pairs={{0,1},{1,0},{2,3},{3,2},{4,5},{5,4},{6,7},{7,6},{8,9},{9,8},{10,11... | collective-permute-start | bytes 196616 | tf_op jit(solution)/shard_map/ppermute | solution.py:18
  11.9 5.9 %collective-permute-start.5 = (bf16[128,128]{1,0:T(8,128)(2,1)S(1)}, bf16[128,128]{1,0:T(8,128)(2,1)S(1)}, u32[]{:S(2)}, u32[]{:S(2)}) collective-permute-start(bf16[128,128]{1,0:T(8,128)(2,1)S(1)} %get-tuple-element.13), channel_id=1, source_target_pairs={{0,6},{1,7},{2,4},{3,5},{4,2},{5,3},{6,0},{7,1},{8,14},{9,15},{10,... | collective-permute-start | bytes 98312 | tf_op jit(solution)/shard_map/ppermute | solution.py:18
  15.5 4.8 %collective-permute-start.6 = (bf16[128,128]{1,0:T(8,128)(2,1)S(1)}, bf16[128,128]{1,0:T(8,128)(2,1)S(1)}, u32[]{:S(2)}, u32[]{:S(2)}) collective-permute-start(bf16[128,128]{1,0:T(8,128)(2,1)S(1)} %get-tuple-element.14), channel_id=1, source_target_pairs={{0,4},{1,5},{2,6},{3,7},{4,0},{5,1},{6,2},{7,3},{8,12},{9,13},{10,... | collective-permute-start | bytes 98312 | tf_op jit(solution)/shard_map/ppermute | solution.py:18
  15.5 4.8 %collective-permute-start.7 = (bf16[128,128]{1,0:T(8,128)(2,1)S(1)}, bf16[128,128]{1,0:T(8,128)(2,1)S(1)}, u32[]{:S(2)}, u32[]{:S(2)}) collective-permute-start(bf16[128,128]{1,0:T(8,128)(2,1)S(1)} %get-tuple-element.15), channel_id=1, source_target_pairs={{0,2},{1,3},{2,0},{3,1},{4,6},{5,7},{6,4},{7,5},{8,10},{9,11},{10,... | collective-permute-start | bytes 98312 | tf_op jit(solution)/shard_map/ppermute | solution.py:18
  20.4 4.5 %collective-permute-start.8 = (bf16[144,128]{1,0:T(8,128)(2,1)S(1)}, bf16[144,128]{1,0:T(8,128)(2,1)S(1)}, u32[]{:S(2)}, u32[]{:S(2)}) collective-permute-start(bf16[144,128]{1,0:T(8,128)(2,1)S(1)} %shard_map.65.refs_0_), channel_id=1, source_target_pairs={{0,2},{1,3},{2,0},{3,1},{4,6},{5,7},{6,4},{7,5},{8,10},{9,11},{10,... | collective-permute-start | bytes 110600 | tf_op jit(solution)/shard_map/ppermute | solution.py:18
  20.5 6.8 %collective-permute-start.9 = (bf16[144,128]{1,0:T(8,128)(2,1)S(1)}, bf16[144,128]{1,0:T(8,128)(2,1)S(1)}, u32[]{:S(2)}, u32[]{:S(2)}) collective-permute-start(bf16[144,128]{1,0:T(8,128)(2,1)S(1)} %shard_map.65.refs_0_), channel_id=1, source_target_pairs={{0,4},{1,5},{2,6},{3,7},{4,0},{5,1},{6,2},{7,3},{8,12},{9,13},{10,... | collective-permute-start | bytes 110600 | tf_op jit(solution)/shard_map/ppermute | solution.py:18
  22.6 5.8 %collective-permute-start.10 = (bf16[144,128]{1,0:T(8,128)(2,1)S(1)}, bf16[144,128]{1,0:T(8,128)(2,1)S(1)}, u32[]{:S(2)}, u32[]{:S(2)}) collective-permute-start(bf16[144,128]{1,0:T(8,128)(2,1)S(1)} %shard_map.65.refs_0_), channel_id=1, source_target_pairs={{0,6},{1,7},{2,4},{3,5},{4,2},{5,3},{6,0},{7,1},{8,14},{9,15},{10,... | collective-permute-start | bytes 110600 | tf_op jit(solution)/shard_map/ppermute | solution.py:18
  24.9 7.6 %collective-permute-start.11 = (bf16[272,128]{1,0:T(8,128)(2,1)S(1)}, bf16[272,128]{1,0:T(8,128)(2,1)S(1)}, u32[]{:S(2)}, u32[]{:S(2)}) collective-permute-start(bf16[272,128]{1,0:T(8,128)(2,1)S(1)} %shard_map.66.group_ref.refs_4_), channel_id=1, source_target_pairs={{0,1},{1,0},{2,3},{3,2},{4,5},{5,4},{6,7},{7,6},{8,9},{9,8},{10,11... | collective-permute-start | bytes 208904 | tf_op jit(solution)/shard_map/ppermute | solution.py:18
  28.4 4.8 %collective-permute-start.12 = (bf16[272,128]{1,0:T(8,128)(2,1)S(1)}, bf16[272,128]{1,0:T(8,128)(2,1)S(1)}, u32[]{:S(2)}, u32[]{:S(2)}) collective-permute-start(bf16[272,128]{1,0:T(8,128)(2,1)S(1)} %shard_map.69.group_ref.refs_5_), channel_id=1, source_target_pairs={{0,1},{1,0},{2,3},{3,2},{4,5},{5,4},{6,7},{7,6},{8,9},{9,8},{10,11... | collective-permute-start | bytes 208904 | tf_op jit(solution)/shard_map/ppermute | solution.py:18
  34.0 3.3 %collective-permute-start.13 = (f32[40,128]{1,0:T(8,128)S(1)}, f32[40,128]{1,0:T(8,128)S(1)}, u32[]{:S(2)}, u32[]{:S(2)}) collective-permute-start(f32[40,128]{1,0:T(8,128)S(1)} %get-tuple-element.17), channel_id=1, source_target_pairs={{0,24},{8,16},{16,8},{24,0},{1,25},{9,17},{17,9},{25,1},{2,26},{10... | collective-permute-start | bytes 61448 | tf_op jit(solution)/shard_map/ppermute | solution.py:18
  34.1 3.8 %collective-permute-start.14 = (f32[40,128]{1,0:T(8,128)S(1)}, f32[40,128]{1,0:T(8,128)S(1)}, u32[]{:S(2)}, u32[]{:S(2)}) collective-permute-start(f32[40,128]{1,0:T(8,128)S(1)} %get-tuple-element.18), channel_id=1, source_target_pairs={{0,16},{8,24},{16,0},{24,8},{1,17},{9,25},{17,1},{25,9},{2,18},{10... | collective-permute-start | bytes 61448 | tf_op jit(solution)/shard_map/ppermute | solution.py:18
  34.7 3.2 %collective-permute-start.15 = (f32[40,128]{1,0:T(8,128)S(1)}, f32[40,128]{1,0:T(8,128)S(1)}, u32[]{:S(2)}, u32[]{:S(2)}) collective-permute-start(f32[40,128]{1,0:T(8,128)S(1)} %get-tuple-element.19), channel_id=1, source_target_pairs={{0,8},{8,0},{16,24},{24,16},{1,9},{9,1},{17,25},{25,17},{2,10},{10... | collective-permute-start | bytes 61448 | tf_op jit(solution)/shard_map/ppermute | solution.py:18

commit v8 on v7

--- a/solution.py
+++ b/solution.py
@@ -139,16 +139,18 @@
     out_ref[len(parts) * rows :, :] = three_parts(jnp.sum(extra, axis=0, keepdims=True))
 
 
-def adjoint_terms(group_ref, start, left_ref, r_ref, all_ref, slots, lags, points):
+def adjoint_terms(group, start, left_ref, r_ref, all_ref, slots, lags, points):
     of_group, _, steps = r_ref.shape
     sensors = all_ref.shape[1]
     rows = of_group * steps // slots
     near, _ = levels(lax.axis_size("par"), lax.axis_size("sens"))
     place = lax.axis_index("par") // near
-    group = (place ^ start) // slots
+    index = (place ^ start) // slots
+    per = slots // len(group)
     for b in range(slots):
-        there = pl.multiple_of(((place ^ (start + b)) - group * slots) * rows, rows)
-        all_ref[pl.ds(there, rows), :] = group_ref[b * rows : (b + 1) * rows, :].astype(jnp.float32)
+        there = pl.multiple_of(((place ^ (start + b)) - index * slots) * rows, rows)
+        at = b % per * rows
+        all_ref[pl.ds(there, rows), :] = group[b // per][at : at + rows, :].astype(jnp.float32)
     lane = lax.broadcasted_iota(jnp.int32, (sensors, steps), 1)
     lane_p = lax.broadcasted_iota(jnp.int32, (points, steps), 1)
     for v in range(of_group):
@@ -163,7 +165,7 @@
         for c in range(1, steps // lags):
             moved = pltpu.roll(terms[c * points : (c + 1) * points], steps - c * lags, 1)
             total += jnp.where(lane_p < steps - c * lags, moved, 0.0)
-        yield group * of_group + v, total
+        yield index * of_group + v, total
 
 
 def left_body(lags, *refs):
@@ -175,16 +177,18 @@
         left_ref[c * points : (c + 1) * points, d * sensors : (d + 1) * sensors] = x_ref[at]
 
 
-def adjoint_piece_body(start, slots, lags, group_ref, left_ref, out_ref, r_ref, all_ref):
+def adjoint_piece_body(start, slots, lags, *refs):
+    group, (left_ref, out_ref, r_ref, all_ref) = refs[:-4], refs[-4:]
     points = out_ref.shape[1]
-    for v, (_, total) in enumerate(adjoint_terms(group_ref, start, left_ref, r_ref, all_ref, slots, lags, points)):
+    for v, (_, total) in enumerate(adjoint_terms(group, start, left_ref, r_ref, all_ref, slots, lags, points)):
         out_ref[v] = total
 
 
-def adjoint_last_body(near, slots, lags, n_groups, *refs):
+def adjoint_last_body(near, slots, lags, n_groups, n_last, *refs):
     done, refs = refs[: near * n_groups - 1], refs[near * n_groups - 1 :]
-    left_ref, groups, refs = refs[0], refs[1 : 1 + near * n_groups], refs[1 + near * n_groups :]
-    outs, (slots_ref, r_ref, all_ref) = refs[:-3], refs[-3:]
+    slots_ref, r_ref, all_ref = refs[-3:]
+    vectors = slots_ref.shape[0]
+    left_ref, groups, outs = refs[0], refs[1 : -3 - vectors], refs[-3 - vectors : -3]
     of_group, points, steps = done[0].shape
     of_block, lanes = of_group * n_groups, outs[0].shape[1]
     j = lax.axis_index("par")
@@ -198,7 +202,7 @@
         for v in range(of_group):
             slots_ref[(block ^ away) * of_block + group * of_group + v] = ref[v]
     start = (n_groups - 1) * slots
-    for v, total in adjoint_terms(groups[-1], start, left_ref, r_ref, all_ref, slots, lags, points):
+    for v, total in adjoint_terms(groups[-n_last:], start, left_ref, r_ref, all_ref, slots, lags, points):
         slots_ref[(block ^ (near - 1)) * of_block + v] = total
     for v, ref in enumerate(outs):
         for i in range(steps // lanes):
@@ -314,9 +318,14 @@
         terms += [swap(out, "par", b * near) for b, out in zip(range(first, 0, -1), outs[::-1])]
     residual = call(residual_body, struct((rows + EXTRA_ROWS, sensors), jnp.bfloat16), (own, *terms))
     parts = [residual] + [swap(residual, "par", b * near) for b in range(1, far)]
-    joined = struct((slots * rows + EXTRA_ROWS, sensors), jnp.bfloat16)
-    groups = [call(join_body, joined, parts[g * slots : (g + 1) * slots]) for g in range(n_groups)]
-    others = [[swap(group, "par", away) for group in groups] for away in range(1, near)]
+    n_last = 2 if slots % 2 == 0 else 1
+    starts = [*range(0, far - slots, slots), *range(far - slots, far, slots // n_last), far]
+    pieces = []
+    for start, end in zip(starts, starts[1:]):
+        joined = struct(((end - start) * rows + EXTRA_ROWS, sensors), jnp.bfloat16)
+        pieces.append(parts[start] if end - start == 1 else call(join_body, joined, parts[start:end]))
+    groups = [[piece] for piece in pieces[:-n_last]] + [pieces[-n_last:]]
+    others = [[[swap(piece, "par", away) for piece in group] for group in groups] for away in range(1, near)]
 
     of_group = of_block // n_groups
     scratch = [
@@ -335,7 +344,7 @@
         call(
             functools.partial(adjoint_piece_body, i % n_groups * slots, slots, lags),
             struct((of_group, points, steps), jnp.float32),
-            (group, left),
+            (*group, left),
             VMEM_LIMIT,
             scratch_shapes=scratch,
             cost_estimate=piece_cost,
@@ -343,9 +352,9 @@
         for i, group in enumerate(every[:-1])
     ]
     partials = call(
-        functools.partial(adjoint_last_body, near, slots, lags, n_groups),
+        functools.partial(adjoint_last_body, near, slots, lags, n_groups, n_last),
         [struct((steps // lanes * points + MISFIT_ROWS, lanes), jnp.float32)] * vectors,
-        (*done, left, *every),
+        (*done, left, *[piece for group in every for piece in group]),
         VMEM_LIMIT,
         scratch_shapes=[pltpu.VMEM((vectors, points, steps), jnp.float32)] + scratch,
         cost_estimate=piece_cost,

time: 38.7 us -> 38.6 us (level)
    ppermute x16 -> x17, waiting for transfers between devices: 9.13 us -> 8.82 us  [swap(): lax.ppermute(value, axis, [(i, i ^ step) for i in range(lax.axis_size(axi...]
    ppermute x16 -> x17, starting transfers between devices: 21 us -> 21.2 us  [swap(): lax.ppermute(value, axis, [(i, i ^ step) for i in range(lax.axis_size(axi...]
    pallas_call x15 -> x14, Pallas kernels: 6.46 us -> 6.43 us  [call(): pl.pallas_call(body, out_shape=out_shape, out_specs=jax.tree.map(lambda _...]
  transfers between devices with their start and end apart: 16 -> 17, of which waited for: 7 -> 7; matrix products, arithmetic and copies ran while one was open for 2% -> 2% of each run, Pallas kernels for 12% -> 12%
where the time goes in v8:
time: 38.6 us; the launch traced here: 38.5 us
  starting transfers between devices  21.2 us (55%)
  waiting for transfers between devices  8.82 us (23%)
  Pallas kernels  6.43 us (17%)
  local copies, waits for them, and re-layouts  1.21 us (3%)
  between operations  0.81 us (2%)
    ppermute x17, starting transfers between devices, swap(): lax.ppermute(value, axis, [(i, i ^ step) for i in range(lax.axis_size(axi...  21.2 us
    ppermute x17, waiting for transfers between devices, swap(): lax.ppermute(value, axis, [(i, i ^ step) for i in range(lax.axis_size(axi...  8.82 us
    pallas_call x14, Pallas kernels, call(): pl.pallas_call(body, out_shape=out_shape, out_specs=jax.tree.map(lambda _...  6.43 us
    unnamed x9, local copies, waits for them, and re-layouts  0.83 us
  transfers between devices with their start and end apart: 17, of which 7 were waited for; matrix products, arithmetic and copies ran while one was open for 2% of the time, Pallas kernels for 12%

profile of v8, /device:TPU:0, one launch (start us, length us, event | category | flops | bytes accessed | tf_op | source)
XLA Modules:
  0.0 38.5 jit_solution(7456670205623141618)
XLA Ops:
  0.6 0.5 %collective-permute-start = (bf16[1,16,256]{2,1,0:T(8,128)(2,1)}, bf16[1,16,256]{2,1,0:T(8,128)(2,1)S(1)}, u32[]{:S(2)}, u32[]{:S(2)}) collective-permute-start(bf16[1,16,256]{2,1,0:T(8,128)(2,1)} %refs_0_.5), channel_id=1, source_target_pairs={{0,8},{8,0},{16,24},{24,16},{1,9},{9,1},{17,25},{25,17},{2,10},{10... | collective-permute-start | bytes 24584 | tf_op jit(solution)/shard_map/ppermute | solution.py:18
  1.2 2.6 %collective-permute-start.1 = (bf16[1,16,256]{2,1,0:T(8,128)(2,1)}, bf16[1,16,256]{2,1,0:T(8,128)(2,1)S(1)}, u32[]{:S(2)}, u32[]{:S(2)}) collective-permute-start(bf16[1,16,256]{2,1,0:T(8,128)(2,1)} %refs_0_.5), channel_id=1, source_target_pairs={{0,16},{8,24},{16,0},{24,8},{1,17},{9,25},{17,1},{25,9},{2,18},{10... | collective-permute-start | bytes 24584 | tf_op jit(solution)/shard_map/ppermute | solution.py:18
  3.8 0.6 %shard_map.59.refs_5_.refs_1_ = bf16[128,16,128]{2,1,0:T(8,128)(2,1)S(1)} custom-call(bf16[128,16,256]{2,1,0:T(8,128)(2,1)S(1)} %copy-done), custom_call_target="tpu_custom_call" | custom-call | bytes 1572864 | tf_op jit(solution)/shard_map/pallas_call | solution.py:229
  4.5 0.4 slice-done
  4.8 0.7 %copy.7 = bf16[128,16,128]{0,1,2:T(8,128)(2,1)S(1)} copy(bf16[128,16,128]{2,1,0:T(8,128)(2,1)S(1)} %slice-done) | data formatting | bytes 1048576
  5.6 1.4 %collective-permute-done.2.refs_3_ = bf16[1,16,256]{2,1,0:T(8,128)(2,1)S(1)} collective-permute-done((bf16[1,16,256]{2,1,0:T(8,128)(2,1)}, bf16[1,16,256]{2,1,0:T(8,128)(2,1)S(1)}, u32[]{:S(2)}, u32[]{:S(2)}) %collective-permute-start.2) | collective-permute-done | bytes 8224 | tf_op jit(solution)/shard_map/ppermute | solution.py:18
  7.0 0.5 %shard_map.63 = bf16[256,128]{1,0:T(8,128)(2,1)S(1)} custom-call(bf16[1,16,256]{2,1,0:T(8,128)(2,1)S(1)} %copy-done.1, bf16[1,16,256]{2,1,0:T(8,128)(2,1)S(1)} %collective-permute-done.refs_1_, bf16[1,16,256]{2,1,0:T(8,128)(2,1)S(1)} %collective-permute-done.1.refs_2_, bf16[1,16,256]{2,1,0:T(8,128)(2,1)S(1)} %collective-permute-done.2.refs_3_, ...), custom_call_target="tpu_custom_call" | custom-call | flops 268435456 | bytes 1048576 | tf_op jit(solution)/shard_map/pallas_call | solution.py:229
  7.5 1.6 %collective-permute-start.4 = (bf16[256,128]{1,0:T(8,128)(2,1)S(1)}, bf16[256,128]{1,0:T(8,128)(2,1)S(1)}, u32[]{:S(2)}, u32[]{:S(2)}) collective-permute-start(bf16[256,128]{1,0:T(8,128)(2,1)S(1)} %shard_map.63), channel_id=1, source_target_pairs={{0,1},{1,0},{2,3},{3,2},{4,5},{5,4},{6,7},{7,6},{8,9},{9,8},{10,11... | collective-permute-start | bytes 196616 | tf_op jit(solution)/shard_map/ppermute | solution.py:18
  9.1 0.5 %shard_map.61 = bf16[256,128]{1,0:T(8,128)(2,1)S(1)} custom-call(bf16[1,16,256]{2,1,0:T(8,128)(2,1)S(1)} %copy-done.1, bf16[1,16,256]{2,1,0:T(8,128)(2,1)S(1)} %collective-permute-done.refs_1_, bf16[1,16,256]{2,1,0:T(8,128)(2,1)S(1)} %collective-permute-done.1.refs_2_, bf16[1,16,256]{2,1,0:T(8,128)(2,1)S(1)} %collective-permute-done.2.refs_3_, ...), custom_call_target="tpu_custom_call" | custom-call | flops 268435456 | bytes 1048576 | tf_op jit(solution)/shard_map/pallas_call | solution.py:229
  9.6 0.6 %collective-permute-start.3 = (bf16[256,128]{1,0:T(8,128)(2,1)S(1)}, bf16[256,128]{1,0:T(8,128)(2,1)S(1)}, u32[]{:S(2)}, u32[]{:S(2)}) collective-permute-start(bf16[256,128]{1,0:T(8,128)(2,1)S(1)} %shard_map.61), channel_id=1, source_target_pairs={{0,1},{1,0},{2,3},{3,2},{4,5},{5,4},{6,7},{7,6},{8,9},{9,8},{10,11... | collective-permute-start | bytes 196616 | tf_op jit(solution)/shard_map/ppermute | solution.py:18
  10.2 1.0 %shard_map.60.own_ref = f32[520,128]{1,0:T(8,128)S(1)} custom-call(bf16[1,16,256]{2,1,0:T(8,128)(2,1)S(1)} %copy-done.1, bf16[1,16,256]{2,1,0:T(8,128)(2,1)S(1)} %collective-permute-done.refs_1_, bf16[1,16,256]{2,1,0:T(8,128)(2,1)S(1)} %collective-permute-done.1.refs_2_, bf16[1,16,256]{2,1,0:T(8,128)(2,1)S(1)} %collective-permute-done.2.refs_3_, ...), custom_call_target="tpu_custom_call" | custom-call | flops 536870912 | bytes 1048576 | tf_op jit(solution)/shard_map/pallas_call | solution.py:229
  11.2 0.6 %collective-permute-done.4.refs_0_ = bf16[256,128]{1,0:T(8,128)(2,1)S(1)} collective-permute-done((bf16[256,128]{1,0:T(8,128)(2,1)S(1)}, bf16[256,128]{1,0:T(8,128)(2,1)S(1)}, u32[]{:S(2)}, u32[]{:S(2)}) %collective-permute-start.4) | collective-permute-done | bytes 65568 | tf_op jit(solution)/shard_map/ppermute | solution.py:18
  11.9 3.7 %collective-permute-start.5 = (bf16[128,128]{1,0:T(8,128)(2,1)S(1)}, bf16[128,128]{1,0:T(8,128)(2,1)S(1)}, u32[]{:S(2)}, u32[]{:S(2)}) collective-permute-start(bf16[128,128]{1,0:T(8,128)(2,1)S(1)} %get-tuple-element.13), channel_id=1, source_target_pairs={{0,6},{1,7},{2,4},{3,5},{4,2},{5,3},{6,0},{7,1},{8,14},{9,15},{10,... | collective-permute-start | bytes 98312 | tf_op jit(solution)/shard_map/ppermute | solution.py:18
  15.5 0.8 %collective-permute-start.7 = (bf16[128,128]{1,0:T(8,128)(2,1)S(1)}, bf16[128,128]{1,0:T(8,128)(2,1)S(1)}, u32[]{:S(2)}, u32[]{:S(2)}) collective-permute-start(bf16[128,128]{1,0:T(8,128)(2,1)S(1)} %get-tuple-element.15), channel_id=1, source_target_pairs={{0,2},{1,3},{2,0},{3,1},{4,6},{5,7},{6,4},{7,5},{8,10},{9,11},{10,... | collective-permute-start | bytes 98312 | tf_op jit(solution)/shard_map/ppermute | solution.py:18
  16.4 1.4 %collective-permute-done.5.refs_0_ = bf16[128,128]{1,0:T(8,128)(2,1)S(1)} collective-permute-done((bf16[128,128]{1,0:T(8,128)(2,1)S(1)}, bf16[128,128]{1,0:T(8,128)(2,1)S(1)}, u32[]{:S(2)}, u32[]{:S(2)}) %collective-permute-start.5) | collective-permute-done | bytes 32800 | tf_op jit(solution)/shard_map/ppermute | solution.py:18
  17.8 2.5 %collective-permute-done.6.refs_1_ = bf16[128,128]{1,0:T(8,128)(2,1)S(1)} collective-permute-done((bf16[128,128]{1,0:T(8,128)(2,1)S(1)}, bf16[128,128]{1,0:T(8,128)(2,1)S(1)}, u32[]{:S(2)}, u32[]{:S(2)}) %collective-permute-start.6) | collective-permute-done | bytes 32800 | tf_op jit(solution)/shard_map/ppermute | solution.py:18
  20.5 2.2 %collective-permute-start.9 = (bf16[144,128]{1,0:T(8,128)(2,1)S(1)}, bf16[144,128]{1,0:T(8,128)(2,1)S(1)}, u32[]{:S(2)}, u32[]{:S(2)}) collective-permute-start(bf16[144,128]{1,0:T(8,128)(2,1)S(1)} %shard_map.65.refs_0_), channel_id=1, source_target_pairs={{0,4},{1,5},{2,6},{3,7},{4,0},{5,1},{6,2},{7,3},{8,12},{9,13},{10,... | collective-permute-start | bytes 110600 | tf_op jit(solution)/shard_map/ppermute | solution.py:18
  22.6 2.2 %collective-permute-start.10 = (bf16[144,128]{1,0:T(8,128)(2,1)S(1)}, bf16[144,128]{1,0:T(8,128)(2,1)S(1)}, u32[]{:S(2)}, u32[]{:S(2)}) collective-permute-start(bf16[144,128]{1,0:T(8,128)(2,1)S(1)} %shard_map.65.refs_0_), channel_id=1, source_target_pairs={{0,6},{1,7},{2,4},{3,5},{4,2},{5,3},{6,0},{7,1},{8,14},{9,15},{10,... | collective-permute-start | bytes 110600 | tf_op jit(solution)/shard_map/ppermute | solution.py:18
  24.9 2.3 %collective-permute-start.11 = (bf16[272,128]{1,0:T(8,128)(2,1)S(1)}, bf16[272,128]{1,0:T(8,128)(2,1)S(1)}, u32[]{:S(2)}, u32[]{:S(2)}) collective-permute-start(bf16[272,128]{1,0:T(8,128)(2,1)S(1)} %shard_map.66.refs_0_.refs_4_), channel_id=1, source_target_pairs={{0,1},{1,0},{2,3},{3,2},{4,5},{5,4},{6,7},{7,6},{8,9},{9,8},{10,11... | collective-permute-start | bytes 208904 | tf_op jit(solution)/shard_map/ppermute | solution.py:18
  27.1 0.2 shard_map.67.refs_1_.refs_2_.refs_3_
  27.3 0.3 collective-permute-start.12
  27.6 0.8 %collective-permute-done.10.refs_1_.refs_6_ = bf16[144,128]{1,0:T(8,128)(2,1)S(1)} collective-permute-done((bf16[144,128]{1,0:T(8,128)(2,1)S(1)}, bf16[144,128]{1,0:T(8,128)(2,1)S(1)}, u32[]{:S(2)}, u32[]{:S(2)}) %collective-permute-start.10) | collective-permute-done | bytes 36896 | tf_op jit(solution)/shard_map/ppermute | solution.py:18
  28.4 2.5 %collective-permute-start.13 = (bf16[144,128]{1,0:T(8,128)(2,1)S(1)}, bf16[144,128]{1,0:T(8,128)(2,1)S(1)}, u32[]{:S(2)}, u32[]{:S(2)}) collective-permute-start(bf16[144,128]{1,0:T(8,128)(2,1)S(1)} %collective-permute-done.10.refs_1_.refs_6_), channel_id=1, source_target_pairs={{0,1},{1,0},{2,3},{3,2},{4,5},{5,4},{6,7},{7,6},{8,9},{9,8},{10,11... | collective-permute-start | bytes 110600 | tf_op jit(solution)/shard_map/ppermute | solution.py:18
  30.9 0.7 %shard_map.68.refs_0_ = f32[1,16,256]{2,1,0:T(8,128)S(1)} custom-call(bf16[272,128]{1,0:T(8,128)(2,1)S(1)} %shard_map.66.refs_0_.refs_4_, bf16[256,2048]{1,0:T(8,128)(2,1)S(1)} %shard_map.67.refs_1_.refs_2_.refs_3_), custom_call_target="tpu_custom_call" | custom-call | flops 268435456 | bytes 1048576 | tf_op jit(solution)/shard_map/pallas_call | solution.py:229
  31.6 0.7 %shard_map.69.refs_1_ = f32[1,16,256]{2,1,0:T(8,128)S(1)} custom-call(bf16[144,128]{1,0:T(8,128)(2,1)S(1)} %collective-permute-done.9.refs_0_.refs_5_, bf16[144,128]{1,0:T(8,128)(2,1)S(1)} %collective-permute-done.10.refs_1_.refs_6_, bf16[256,2048]{1,0:T(8,128)(2,1)S(1)} %shard_map.67.refs_1_.refs_2_.refs_3_), custom_call_target="tpu_custom_call" | custom-call | flops 268435456 | bytes 1048576 | tf_op jit(solution)/shard_map/pallas_call | solution.py:229
  32.4 0.7 %shard_map.70.refs_2_ = f32[1,16,256]{2,1,0:T(8,128)S(1)} custom-call(bf16[272,128]{1,0:T(8,128)(2,1)S(1)} %collective-permute-done.11.refs_0_.refs_7_, bf16[256,2048]{1,0:T(8,128)(2,1)S(1)} %shard_map.67.refs_1_.refs_2_.refs_3_), custom_call_target="tpu_custom_call" | custom-call | flops 268435456 | bytes 1048576 | tf_op jit(solution)/shard_map/pallas_call | solution.py:229
  33.1 0.8 %shard_map.71 = (f32[40,128]{1,0:T(8,128)S(1)}, f32[40,128]{1,0:T(8,128)S(1)}, f32[40,128]{1,0:T(8,128)S(1)}, f32[40,128]{1,0:T(8,128)S(1)}) custom-call(f32[1,16,256]{2,1,0:T(8,128)S(1)} %shard_map.68.refs_0_, f32[1,16,256]{2,1,0:T(8,128)S(1)} %shard_map.69.refs_1_, f32[1,16,256]{2,1,0:T(8,128)S(1)} %shard_map.70.refs_2_, ...), custom_call_target="tpu_custom_call" | custom-call | flops 268435456 | bytes 1048576 | tf_op jit(solution)/shard_map/pallas_call | solution.py:229
  34.0 0.6 %collective-permute-start.15 = (f32[40,128]{1,0:T(8,128)S(1)}, f32[40,128]{1,0:T(8,128)S(1)}, u32[]{:S(2)}, u32[]{:S(2)}) collective-permute-start(f32[40,128]{1,0:T(8,128)S(1)} %get-tuple-element.18), channel_id=1, source_target_pairs={{0,16},{8,24},{16,0},{24,8},{1,17},{9,25},{17,1},{25,9},{2,18},{10... | collective-permute-start | bytes 61448 | tf_op jit(solution)/shard_map/ppermute | solution.py:18
  34.6 1.2 %collective-permute-start.16 = (f32[40,128]{1,0:T(8,128)S(1)}, f32[40,128]{1,0:T(8,128)S(1)}, u32[]{:S(2)}, u32[]{:S(2)}) collective-permute-start(f32[40,128]{1,0:T(8,128)S(1)} %get-tuple-element.19), channel_id=1, source_target_pairs={{0,8},{8,0},{16,24},{24,16},{1,9},{9,1},{17,25},{25,17},{2,10},{10... | collective-permute-start | bytes 61448 | tf_op jit(solution)/shard_map/ppermute | solution.py:18
  35.8 1.3 %collective-permute-done.14.refs_1_ = f32[40,128]{1,0:T(8,128)S(1)} collective-permute-done((f32[40,128]{1,0:T(8,128)S(1)}, f32[40,128]{1,0:T(8,128)S(1)}, u32[]{:S(2)}, u32[]{:S(2)}) %collective-permute-start.14) | collective-permute-done | bytes 20512 | tf_op jit(solution)/shard_map/ppermute | solution.py:18
  37.2 0.7 %collective-permute-done.15.refs_2_ = f32[40,128]{1,0:T(8,128)S(1)} collective-permute-done((f32[40,128]{1,0:T(8,128)S(1)}, f32[40,128]{1,0:T(8,128)S(1)}, u32[]{:S(2)}, u32[]{:S(2)}) %collective-permute-start.15) | collective-permute-done | bytes 20512 | tf_op jit(solution)/shard_map/ppermute | solution.py:18
  37.8 0.6 %shard_map.72 = (f32[1,16,256]{2,1,0:T(8,128)}, f32[1,1]{1,0:T(1,128)}) custom-call(f32[40,128]{1,0:T(8,128)S(1)} %get-tuple-element.16.refs_0_, f32[40,128]{1,0:T(8,128)S(1)} %collective-permute-done.14.refs_1_, f32[40,128]{1,0:T(8,128)S(1)} %collective-permute-done.15.refs_2_, f32[40,128]{1,0:T(8,128)S(1)} %collective-permute-done.16.refs_3_), custom_call_target="tpu_custom_call" | custom-call | tf_op jit(solution)/shard_map/pallas_call | solution.py:229
  (27 shorter events, 0.4 us)
Async XLA Ops:
  0.6 3.2 %copy-start = (bf16[128,16,256]{2,1,0:T(8,128)(2,1)S(1)}, bf16[128,16,256]{2,1,0:T(8,128)(2,1)}, u32[]{:S(2)}) copy-start(bf16[128,16,256]{2,1,0:T(8,128)(2,1)} %kernel_ref.1) | copy-start | bytes 3145732
  0.6 4.9 %collective-permute-start = (bf16[1,16,256]{2,1,0:T(8,128)(2,1)}, bf16[1,16,256]{2,1,0:T(8,128)(2,1)S(1)}, u32[]{:S(2)}, u32[]{:S(2)}) collective-permute-start(bf16[1,16,256]{2,1,0:T(8,128)(2,1)} %refs_0_.5), channel_id=1, source_target_pairs={{0,8},{8,0},{16,24},{24,16},{1,9},{9,1},{17,25},{25,17},{2,10},{10... | collective-permute-start | bytes 24584 | tf_op jit(solution)/shard_map/ppermute | solution.py:18
  1.2 4.4 %collective-permute-start.1 = (bf16[1,16,256]{2,1,0:T(8,128)(2,1)}, bf16[1,16,256]{2,1,0:T(8,128)(2,1)S(1)}, u32[]{:S(2)}, u32[]{:S(2)}) collective-permute-start(bf16[1,16,256]{2,1,0:T(8,128)(2,1)} %refs_0_.5), channel_id=1, source_target_pairs={{0,16},{8,24},{16,0},{24,8},{1,17},{9,25},{17,1},{25,9},{2,18},{10... | collective-permute-start | bytes 24584 | tf_op jit(solution)/shard_map/ppermute | solution.py:18
  3.7 3.3 %collective-permute-start.2 = (bf16[1,16,256]{2,1,0:T(8,128)(2,1)}, bf16[1,16,256]{2,1,0:T(8,128)(2,1)S(1)}, u32[]{:S(2)}, u32[]{:S(2)}) collective-permute-start(bf16[1,16,256]{2,1,0:T(8,128)(2,1)} %refs_0_.5), channel_id=1, source_target_pairs={{0,24},{8,16},{16,8},{24,0},{1,25},{9,17},{17,9},{25,1},{2,26},{10... | collective-permute-start | bytes 24584 | tf_op jit(solution)/shard_map/ppermute | solution.py:18
  3.8 1.0 %slice-start = ((bf16[128,16,256]{2,1,0:T(8,128)(2,1)}), bf16[128,16,128]{2,1,0:T(8,128)(2,1)S(1)}, s32[]{:S(2)}) async-start(bf16[128,16,256]{2,1,0:T(8,128)(2,1)} %kernel_ref.1), calls=%async_computation | async-start | bytes 1048576 | tf_op jit(solution)/shard_map/slice | solution.py:259
  4.8 2.2 %copy-start.1 = (bf16[1,16,256]{2,1,0:T(8,128)(2,1)S(1)}, bf16[1,16,256]{2,1,0:T(8,128)(2,1)}, u32[]{:S(2)}) copy-start(bf16[1,16,256]{2,1,0:T(8,128)(2,1)} %refs_0_.5) | copy-start | bytes 24580
  7.5 2.7 %copy-start.2 = (f32[4,128,256]{2,1,0:T(8,128)S(1)}, f32[4,128,256]{2,1,0:T(8,128)}, u32[]{:S(2)}) copy-start(f32[4,128,256]{2,1,0:T(8,128)} %refs_6_.1) | copy-start | bytes 1572868
  7.5 4.3 %collective-permute-start.4 = (bf16[256,128]{1,0:T(8,128)(2,1)S(1)}, bf16[256,128]{1,0:T(8,128)(2,1)S(1)}, u32[]{:S(2)}, u32[]{:S(2)}) collective-permute-start(bf16[256,128]{1,0:T(8,128)(2,1)S(1)} %shard_map.63), channel_id=1, source_target_pairs={{0,1},{1,0},{2,3},{3,2},{4,5},{5,4},{6,7},{7,6},{8,9},{9,8},{10,11... | collective-permute-start | bytes 196616 | tf_op jit(solution)/shard_map/ppermute | solution.py:18
  9.6 0.7 %copy-start.3 = (f32[128]{0:T(128)S(1)}, f32[128]{0:T(128)}, u32[]{:S(2)}) copy-start(f32[128]{0:T(128)} %param.7) | copy-start | bytes 1540
  9.6 6.0 %collective-permute-start.3 = (bf16[256,128]{1,0:T(8,128)(2,1)S(1)}, bf16[256,128]{1,0:T(8,128)(2,1)S(1)}, u32[]{:S(2)}, u32[]{:S(2)}) collective-permute-start(bf16[256,128]{1,0:T(8,128)(2,1)S(1)} %shard_map.61), channel_id=1, source_target_pairs={{0,1},{1,0},{2,3},{3,2},{4,5},{5,4},{6,7},{7,6},{8,9},{9,8},{10,11... | collective-permute-start | bytes 196616 | tf_op jit(solution)/shard_map/ppermute | solution.py:18
  11.9 5.9 %collective-permute-start.5 = (bf16[128,128]{1,0:T(8,128)(2,1)S(1)}, bf16[128,128]{1,0:T(8,128)(2,1)S(1)}, u32[]{:S(2)}, u32[]{:S(2)}) collective-permute-start(bf16[128,128]{1,0:T(8,128)(2,1)S(1)} %get-tuple-element.13), channel_id=1, source_target_pairs={{0,6},{1,7},{2,4},{3,5},{4,2},{5,3},{6,0},{7,1},{8,14},{9,15},{10,... | collective-permute-start | bytes 98312 | tf_op jit(solution)/shard_map/ppermute | solution.py:18
  15.5 4.8 %collective-permute-start.6 = (bf16[128,128]{1,0:T(8,128)(2,1)S(1)}, bf16[128,128]{1,0:T(8,128)(2,1)S(1)}, u32[]{:S(2)}, u32[]{:S(2)}) collective-permute-start(bf16[128,128]{1,0:T(8,128)(2,1)S(1)} %get-tuple-element.14), channel_id=1, source_target_pairs={{0,4},{1,5},{2,6},{3,7},{4,0},{5,1},{6,2},{7,3},{8,12},{9,13},{10,... | collective-permute-start | bytes 98312 | tf_op jit(solution)/shard_map/ppermute | solution.py:18
  15.5 4.8 %collective-permute-start.7 = (bf16[128,128]{1,0:T(8,128)(2,1)S(1)}, bf16[128,128]{1,0:T(8,128)(2,1)S(1)}, u32[]{:S(2)}, u32[]{:S(2)}) collective-permute-start(bf16[128,128]{1,0:T(8,128)(2,1)S(1)} %get-tuple-element.15), channel_id=1, source_target_pairs={{0,2},{1,3},{2,0},{3,1},{4,6},{5,7},{6,4},{7,5},{8,10},{9,11},{10,... | collective-permute-start | bytes 98312 | tf_op jit(solution)/shard_map/ppermute | solution.py:18
  20.4 4.5 %collective-permute-start.8 = (bf16[144,128]{1,0:T(8,128)(2,1)S(1)}, bf16[144,128]{1,0:T(8,128)(2,1)S(1)}, u32[]{:S(2)}, u32[]{:S(2)}) collective-permute-start(bf16[144,128]{1,0:T(8,128)(2,1)S(1)} %shard_map.65.refs_0_), channel_id=1, source_target_pairs={{0,2},{1,3},{2,0},{3,1},{4,6},{5,7},{6,4},{7,5},{8,10},{9,11},{10,... | collective-permute-start | bytes 110600 | tf_op jit(solution)/shard_map/ppermute | solution.py:18
  20.5 6.8 %collective-permute-start.9 = (bf16[144,128]{1,0:T(8,128)(2,1)S(1)}, bf16[144,128]{1,0:T(8,128)(2,1)S(1)}, u32[]{:S(2)}, u32[]{:S(2)}) collective-permute-start(bf16[144,128]{1,0:T(8,128)(2,1)S(1)} %shard_map.65.refs_0_), channel_id=1, source_target_pairs={{0,4},{1,5},{2,6},{3,7},{4,0},{5,1},{6,2},{7,3},{8,12},{9,13},{10,... | collective-permute-start | bytes 110600 | tf_op jit(solution)/shard_map/ppermute | solution.py:18
  22.6 5.8 %collective-permute-start.10 = (bf16[144,128]{1,0:T(8,128)(2,1)S(1)}, bf16[144,128]{1,0:T(8,128)(2,1)S(1)}, u32[]{:S(2)}, u32[]{:S(2)}) collective-permute-start(bf16[144,128]{1,0:T(8,128)(2,1)S(1)} %shard_map.65.refs_0_), channel_id=1, source_target_pairs={{0,6},{1,7},{2,4},{3,5},{4,2},{5,3},{6,0},{7,1},{8,14},{9,15},{10,... | collective-permute-start | bytes 110600 | tf_op jit(solution)/shard_map/ppermute | solution.py:18
  24.9 7.5 %collective-permute-start.11 = (bf16[272,128]{1,0:T(8,128)(2,1)S(1)}, bf16[272,128]{1,0:T(8,128)(2,1)S(1)}, u32[]{:S(2)}, u32[]{:S(2)}) collective-permute-start(bf16[272,128]{1,0:T(8,128)(2,1)S(1)} %shard_map.66.refs_0_.refs_4_), channel_id=1, source_target_pairs={{0,1},{1,0},{2,3},{3,2},{4,5},{5,4},{6,7},{7,6},{8,9},{9,8},{10,11... | collective-permute-start | bytes 208904 | tf_op jit(solution)/shard_map/ppermute | solution.py:18
  27.3 5.8 %collective-permute-start.12 = (bf16[144,128]{1,0:T(8,128)(2,1)S(1)}, bf16[144,128]{1,0:T(8,128)(2,1)S(1)}, u32[]{:S(2)}, u32[]{:S(2)}) collective-permute-start(bf16[144,128]{1,0:T(8,128)(2,1)S(1)} %collective-permute-done.9.refs_0_.refs_5_), channel_id=1, source_target_pairs={{0,1},{1,0},{2,3},{3,2},{4,5},{5,4},{6,7},{7,6},{8,9},{9,8},{10,11... | collective-permute-start | bytes 110600 | tf_op jit(solution)/shard_map/ppermute | solution.py:18
  28.4 4.7 %collective-permute-start.13 = (bf16[144,128]{1,0:T(8,128)(2,1)S(1)}, bf16[144,128]{1,0:T(8,128)(2,1)S(1)}, u32[]{:S(2)}, u32[]{:S(2)}) collective-permute-start(bf16[144,128]{1,0:T(8,128)(2,1)S(1)} %collective-permute-done.10.refs_1_.refs_6_), channel_id=1, source_target_pairs={{0,1},{1,0},{2,3},{3,2},{4,5},{5,4},{6,7},{7,6},{8,9},{9,8},{10,11... | collective-permute-start | bytes 110600 | tf_op jit(solution)/shard_map/ppermute | solution.py:18
  33.9 3.3 %collective-permute-start.14 = (f32[40,128]{1,0:T(8,128)S(1)}, f32[40,128]{1,0:T(8,128)S(1)}, u32[]{:S(2)}, u32[]{:S(2)}) collective-permute-start(f32[40,128]{1,0:T(8,128)S(1)} %get-tuple-element.17), channel_id=1, source_target_pairs={{0,24},{8,16},{16,8},{24,0},{1,25},{9,17},{17,9},{25,1},{2,26},{10... | collective-permute-start | bytes 61448 | tf_op jit(solution)/shard_map/ppermute | solution.py:18
  34.0 3.8 %collective-permute-start.15 = (f32[40,128]{1,0:T(8,128)S(1)}, f32[40,128]{1,0:T(8,128)S(1)}, u32[]{:S(2)}, u32[]{:S(2)}) collective-permute-start(f32[40,128]{1,0:T(8,128)S(1)} %get-tuple-element.18), channel_id=1, source_target_pairs={{0,16},{8,24},{16,0},{24,8},{1,17},{9,25},{17,1},{25,9},{2,18},{10... | collective-permute-start | bytes 61448 | tf_op jit(solution)/shard_map/ppermute | solution.py:18
  34.6 3.2 %collective-permute-start.16 = (f32[40,128]{1,0:T(8,128)S(1)}, f32[40,128]{1,0:T(8,128)S(1)}, u32[]{:S(2)}, u32[]{:S(2)}) collective-permute-start(f32[40,128]{1,0:T(8,128)S(1)} %get-tuple-element.19), channel_id=1, source_target_pairs={{0,8},{8,0},{16,24},{24,16},{1,9},{9,1},{17,25},{25,17},{2,10},{10... | collective-permute-start | bytes 61448 | tf_op jit(solution)/shard_map/ppermute | solution.py:18

commit v9 on v8

--- a/solution.py
+++ b/solution.py
@@ -325,32 +325,35 @@
         joined = struct(((end - start) * rows + EXTRA_ROWS, sensors), jnp.bfloat16)
         pieces.append(parts[start] if end - start == 1 else call(join_body, joined, parts[start:end]))
     groups = [[piece] for piece in pieces[:-n_last]] + [pieces[-n_last:]]
-    others = [[[swap(piece, "par", away) for piece in group] for group in groups] for away in range(1, near)]
 
     of_group = of_block // n_groups
     scratch = [
         pltpu.VMEM((of_group, lags * sensors, steps), jnp.bfloat16),
         pltpu.VMEM((of_group * steps, sensors), jnp.float32),
     ]
+    least_cost = pl.CostEstimate(flops=0, bytes_accessed=0, transcendentals=0)
     left = call(
         functools.partial(left_body, lags),
         struct((steps // lags * points, lags * sensors), jnp.bfloat16),
         xs,
         VMEM_LIMIT,
-        cost_estimate=pl.CostEstimate(flops=0, bytes_accessed=kernel.size, transcendentals=0),
+        cost_estimate=least_cost,
     )
-    every = groups + [group for some in others for group in some]
-    done = [
-        call(
+
+    def adjoint_piece(i, group):
+        return call(
             functools.partial(adjoint_piece_body, i % n_groups * slots, slots, lags),
             struct((of_group, points, steps), jnp.float32),
             (*group, left),
             VMEM_LIMIT,
             scratch_shapes=scratch,
-            cost_estimate=piece_cost,
+            cost_estimate=least_cost if i < n_groups - 1 else cost,
         )
-        for i, group in enumerate(every[:-1])
-    ]
+
+    done = [adjoint_piece(g, groups[g]) for g in range(n_groups - 1)]
+    others = [[[swap(piece, "par", away) for piece in group] for group in groups] for away in range(1, near)]
+    every = groups + [group for some in others for group in some]
+    done += [adjoint_piece(i, every[i]) for i in range(len(done), len(every) - 1)]
     partials = call(
         functools.partial(adjoint_last_body, near, slots, lags, n_groups, n_last),
         [struct((steps // lanes * points + MISFIT_ROWS, lanes), jnp.float32)] * vectors,

time: 38.6 us -> 38.3 us (level)
  transfers between devices with their start and end apart: 17 -> 17, of which waited for: 7 -> 8; matrix products, arithmetic and copies ran while one was open for 2% -> 2% of each run, Pallas kernels for 12% -> 12%
where the time goes in v9:
time: 38.3 us; the launch traced here: 38.1 us
  starting transfers between devices  21 us (55%)
  waiting for transfers between devices  8.69 us (23%)
  Pallas kernels  6.42 us (17%)
  local copies, waits for them, and re-layouts  1.21 us (3%)
  between operations  0.8 us (2%)
    ppermute x17, starting transfers between devices, swap(): lax.ppermute(value, axis, [(i, i ^ step) for i in range(lax.axis_size(axi...  21 us
    ppermute x17, waiting for transfers between devices, swap(): lax.ppermute(value, axis, [(i, i ^ step) for i in range(lax.axis_size(axi...  8.69 us
    pallas_call x14, Pallas kernels, call(): pl.pallas_call(body, out_shape=out_shape, out_specs=jax.tree.map(lambda _...  6.42 us
    unnamed x9, local copies, waits for them, and re-layouts  0.83 us
  transfers between devices with their start and end apart: 17, of which 8 were waited for; matrix products, arithmetic and copies ran while one was open for 2% of the time, Pallas kernels for 12%

profile of v9, /device:TPU:0, one launch (start us, length us, event | category | flops | bytes accessed | tf_op | source)
XLA Modules:
  0.0 38.1 jit_solution(11592672366295345191)
XLA Ops:
  0.6 0.5 %collective-permute-start = (bf16[1,16,256]{2,1,0:T(8,128)(2,1)}, bf16[1,16,256]{2,1,0:T(8,128)(2,1)S(1)}, u32[]{:S(2)}, u32[]{:S(2)}) collective-permute-start(bf16[1,16,256]{2,1,0:T(8,128)(2,1)} %refs_0_.5), channel_id=1, source_target_pairs={{0,8},{8,0},{16,24},{24,16},{1,9},{9,1},{17,25},{25,17},{2,10},{10... | collective-permute-start | bytes 24584 | tf_op jit(solution)/shard_map/ppermute | solution.py:18
  1.2 2.6 %collective-permute-start.1 = (bf16[1,16,256]{2,1,0:T(8,128)(2,1)}, bf16[1,16,256]{2,1,0:T(8,128)(2,1)S(1)}, u32[]{:S(2)}, u32[]{:S(2)}) collective-permute-start(bf16[1,16,256]{2,1,0:T(8,128)(2,1)} %refs_0_.5), channel_id=1, source_target_pairs={{0,16},{8,24},{16,0},{24,8},{1,17},{9,25},{17,1},{25,9},{2,18},{10... | collective-permute-start | bytes 24584 | tf_op jit(solution)/shard_map/ppermute | solution.py:18
  3.8 0.6 %shard_map.59.refs_5_.refs_1_ = bf16[128,16,128]{2,1,0:T(8,128)(2,1)S(1)} custom-call(bf16[128,16,256]{2,1,0:T(8,128)(2,1)S(1)} %copy-done), custom_call_target="tpu_custom_call" | custom-call | bytes 1572864 | tf_op jit(solution)/shard_map/pallas_call | solution.py:229
  4.5 0.4 %slice-done = bf16[128,16,128]{2,1,0:T(8,128)(2,1)S(1)} async-done(((bf16[128,16,256]{2,1,0:T(8,128)(2,1)}), bf16[128,16,128]{2,1,0:T(8,128)(2,1)S(1)}, s32[]{:S(2)}) %slice-start) | async-done | bytes 524312 | tf_op jit(solution)/shard_map/slice | solution.py:259
  4.8 0.7 %copy.7 = bf16[128,16,128]{0,1,2:T(8,128)(2,1)S(1)} copy(bf16[128,16,128]{2,1,0:T(8,128)(2,1)S(1)} %slice-done) | data formatting | bytes 1048576
  5.6 1.4 %collective-permute-done.2.refs_3_ = bf16[1,16,256]{2,1,0:T(8,128)(2,1)S(1)} collective-permute-done((bf16[1,16,256]{2,1,0:T(8,128)(2,1)}, bf16[1,16,256]{2,1,0:T(8,128)(2,1)S(1)}, u32[]{:S(2)}, u32[]{:S(2)}) %collective-permute-start.2) | collective-permute-done | bytes 8224 | tf_op jit(solution)/shard_map/ppermute | solution.py:18
  7.0 0.5 %shard_map.63 = bf16[256,128]{1,0:T(8,128)(2,1)S(1)} custom-call(bf16[1,16,256]{2,1,0:T(8,128)(2,1)S(1)} %copy-done.1, bf16[1,16,256]{2,1,0:T(8,128)(2,1)S(1)} %collective-permute-done.refs_1_, bf16[1,16,256]{2,1,0:T(8,128)(2,1)S(1)} %collective-permute-done.1.refs_2_, bf16[1,16,256]{2,1,0:T(8,128)(2,1)S(1)} %collective-permute-done.2.refs_3_, ...), custom_call_target="tpu_custom_call" | custom-call | flops 268435456 | bytes 1048576 | tf_op jit(solution)/shard_map/pallas_call | solution.py:229
  7.5 1.6 %collective-permute-start.4 = (bf16[256,128]{1,0:T(8,128)(2,1)S(1)}, bf16[256,128]{1,0:T(8,128)(2,1)S(1)}, u32[]{:S(2)}, u32[]{:S(2)}) collective-permute-start(bf16[256,128]{1,0:T(8,128)(2,1)S(1)} %shard_map.63), channel_id=1, source_target_pairs={{0,1},{1,0},{2,3},{3,2},{4,5},{5,4},{6,7},{7,6},{8,9},{9,8},{10,11... | collective-permute-start | bytes 196616 | tf_op jit(solution)/shard_map/ppermute | solution.py:18
  9.1 0.5 %shard_map.61 = bf16[256,128]{1,0:T(8,128)(2,1)S(1)} custom-call(bf16[1,16,256]{2,1,0:T(8,128)(2,1)S(1)} %copy-done.1, bf16[1,16,256]{2,1,0:T(8,128)(2,1)S(1)} %collective-permute-done.refs_1_, bf16[1,16,256]{2,1,0:T(8,128)(2,1)S(1)} %collective-permute-done.1.refs_2_, bf16[1,16,256]{2,1,0:T(8,128)(2,1)S(1)} %collective-permute-done.2.refs_3_, ...), custom_call_target="tpu_custom_call" | custom-call | flops 268435456 | bytes 1048576 | tf_op jit(solution)/shard_map/pallas_call | solution.py:229
  9.6 0.6 %collective-permute-start.3 = (bf16[256,128]{1,0:T(8,128)(2,1)S(1)}, bf16[256,128]{1,0:T(8,128)(2,1)S(1)}, u32[]{:S(2)}, u32[]{:S(2)}) collective-permute-start(bf16[256,128]{1,0:T(8,128)(2,1)S(1)} %shard_map.61), channel_id=1, source_target_pairs={{0,1},{1,0},{2,3},{3,2},{4,5},{5,4},{6,7},{7,6},{8,9},{9,8},{10,11... | collective-permute-start | bytes 196616 | tf_op jit(solution)/shard_map/ppermute | solution.py:18
  10.2 1.0 %shard_map.60.own_ref = f32[520,128]{1,0:T(8,128)S(1)} custom-call(bf16[1,16,256]{2,1,0:T(8,128)(2,1)S(1)} %copy-done.1, bf16[1,16,256]{2,1,0:T(8,128)(2,1)S(1)} %collective-permute-done.refs_1_, bf16[1,16,256]{2,1,0:T(8,128)(2,1)S(1)} %collective-permute-done.1.refs_2_, bf16[1,16,256]{2,1,0:T(8,128)(2,1)S(1)} %collective-permute-done.2.refs_3_, ...), custom_call_target="tpu_custom_call" | custom-call | flops 536870912 | bytes 1048576 | tf_op jit(solution)/shard_map/pallas_call | solution.py:229
  11.2 0.6 %collective-permute-done.4.refs_0_ = bf16[256,128]{1,0:T(8,128)(2,1)S(1)} collective-permute-done((bf16[256,128]{1,0:T(8,128)(2,1)S(1)}, bf16[256,128]{1,0:T(8,128)(2,1)S(1)}, u32[]{:S(2)}, u32[]{:S(2)}) %collective-permute-start.4) | collective-permute-done | bytes 65568 | tf_op jit(solution)/shard_map/ppermute | solution.py:18
  11.9 3.7 %collective-permute-start.5 = (bf16[128,128]{1,0:T(8,128)(2,1)S(1)}, bf16[128,128]{1,0:T(8,128)(2,1)S(1)}, u32[]{:S(2)}, u32[]{:S(2)}) collective-permute-start(bf16[128,128]{1,0:T(8,128)(2,1)S(1)} %get-tuple-element.13), channel_id=1, source_target_pairs={{0,6},{1,7},{2,4},{3,5},{4,2},{5,3},{6,0},{7,1},{8,14},{9,15},{10,... | collective-permute-start | bytes 98312 | tf_op jit(solution)/shard_map/ppermute | solution.py:18
  15.5 0.8 %collective-permute-start.7 = (bf16[128,128]{1,0:T(8,128)(2,1)S(1)}, bf16[128,128]{1,0:T(8,128)(2,1)S(1)}, u32[]{:S(2)}, u32[]{:S(2)}) collective-permute-start(bf16[128,128]{1,0:T(8,128)(2,1)S(1)} %get-tuple-element.15), channel_id=1, source_target_pairs={{0,2},{1,3},{2,0},{3,1},{4,6},{5,7},{6,4},{7,5},{8,10},{9,11},{10,... | collective-permute-start | bytes 98312 | tf_op jit(solution)/shard_map/ppermute | solution.py:18
  16.4 1.4 %collective-permute-done.5.refs_0_ = bf16[128,128]{1,0:T(8,128)(2,1)S(1)} collective-permute-done((bf16[128,128]{1,0:T(8,128)(2,1)S(1)}, bf16[128,128]{1,0:T(8,128)(2,1)S(1)}, u32[]{:S(2)}, u32[]{:S(2)}) %collective-permute-start.5) | collective-permute-done | bytes 32800 | tf_op jit(solution)/shard_map/ppermute | solution.py:18
  17.8 2.5 %collective-permute-done.6.refs_1_ = bf16[128,128]{1,0:T(8,128)(2,1)S(1)} collective-permute-done((bf16[128,128]{1,0:T(8,128)(2,1)S(1)}, bf16[128,128]{1,0:T(8,128)(2,1)S(1)}, u32[]{:S(2)}, u32[]{:S(2)}) %collective-permute-start.6) | collective-permute-done | bytes 32800 | tf_op jit(solution)/shard_map/ppermute | solution.py:18
  20.5 2.2 %collective-permute-start.9 = (bf16[144,128]{1,0:T(8,128)(2,1)S(1)}, bf16[144,128]{1,0:T(8,128)(2,1)S(1)}, u32[]{:S(2)}, u32[]{:S(2)}) collective-permute-start(bf16[144,128]{1,0:T(8,128)(2,1)S(1)} %shard_map.65.refs_0_), channel_id=1, source_target_pairs={{0,4},{1,5},{2,6},{3,7},{4,0},{5,1},{6,2},{7,3},{8,12},{9,13},{10,... | collective-permute-start | bytes 110600 | tf_op jit(solution)/shard_map/ppermute | solution.py:18
  22.6 2.2 %collective-permute-start.10 = (bf16[144,128]{1,0:T(8,128)(2,1)S(1)}, bf16[144,128]{1,0:T(8,128)(2,1)S(1)}, u32[]{:S(2)}, u32[]{:S(2)}) collective-permute-start(bf16[144,128]{1,0:T(8,128)(2,1)S(1)} %shard_map.65.refs_0_), channel_id=1, source_target_pairs={{0,6},{1,7},{2,4},{3,5},{4,2},{5,3},{6,0},{7,1},{8,14},{9,15},{10,... | collective-permute-start | bytes 110600 | tf_op jit(solution)/shard_map/ppermute | solution.py:18
  24.9 2.3 %collective-permute-start.11 = (bf16[272,128]{1,0:T(8,128)(2,1)S(1)}, bf16[272,128]{1,0:T(8,128)(2,1)S(1)}, u32[]{:S(2)}, u32[]{:S(2)}) collective-permute-start(bf16[272,128]{1,0:T(8,128)(2,1)S(1)} %shard_map.66.refs_0_.refs_4_), channel_id=1, source_target_pairs={{0,1},{1,0},{2,3},{3,2},{4,5},{5,4},{6,7},{7,6},{8,9},{9,8},{10,11... | collective-permute-start | bytes 208904 | tf_op jit(solution)/shard_map/ppermute | solution.py:18
  27.1 0.2 shard_map.67.refs_1_.refs_2_.refs_3_
  27.3 0.7 %shard_map.68.refs_0_ = f32[1,16,256]{2,1,0:T(8,128)S(1)} custom-call(bf16[272,128]{1,0:T(8,128)(2,1)S(1)} %shard_map.66.refs_0_.refs_4_, bf16[256,2048]{1,0:T(8,128)(2,1)S(1)} %shard_map.67.refs_1_.refs_2_.refs_3_), custom_call_target="tpu_custom_call" | custom-call | tf_op jit(solution)/shard_map/pallas_call | solution.py:229
  28.1 0.3 collective-permute-done.10.refs_1_.refs_6_
  28.4 2.5 %collective-permute-start.13 = (bf16[144,128]{1,0:T(8,128)(2,1)S(1)}, bf16[144,128]{1,0:T(8,128)(2,1)S(1)}, u32[]{:S(2)}, u32[]{:S(2)}) collective-permute-start(bf16[144,128]{1,0:T(8,128)(2,1)S(1)} %collective-permute-done.10.refs_1_.refs_6_), channel_id=1, source_target_pairs={{0,1},{1,0},{2,3},{3,2},{4,5},{5,4},{6,7},{7,6},{8,9},{9,8},{10,11... | collective-permute-start | bytes 110600 | tf_op jit(solution)/shard_map/ppermute | solution.py:18
  30.9 0.7 %shard_map.69.refs_1_ = f32[1,16,256]{2,1,0:T(8,128)S(1)} custom-call(bf16[144,128]{1,0:T(8,128)(2,1)S(1)} %collective-permute-done.9.refs_0_.refs_5_, bf16[144,128]{1,0:T(8,128)(2,1)S(1)} %collective-permute-done.10.refs_1_.refs_6_, bf16[256,2048]{1,0:T(8,128)(2,1)S(1)} %shard_map.67.refs_1_.refs_2_.refs_3_), custom_call_target="tpu_custom_call" | custom-call | flops 536870912 | bytes 1048576 | tf_op jit(solution)/shard_map/pallas_call | solution.py:229
  31.6 0.7 %shard_map.70.refs_2_ = f32[1,16,256]{2,1,0:T(8,128)S(1)} custom-call(bf16[272,128]{1,0:T(8,128)(2,1)S(1)} %collective-permute-done.11.refs_0_.refs_7_, bf16[256,2048]{1,0:T(8,128)(2,1)S(1)} %shard_map.67.refs_1_.refs_2_.refs_3_), custom_call_target="tpu_custom_call" | custom-call | flops 536870912 | bytes 1048576 | tf_op jit(solution)/shard_map/pallas_call | solution.py:229
  32.4 0.4 %collective-permute-done.13.refs_9_ = bf16[144,128]{1,0:T(8,128)(2,1)S(1)} collective-permute-done((bf16[144,128]{1,0:T(8,128)(2,1)S(1)}, bf16[144,128]{1,0:T(8,128)(2,1)S(1)}, u32[]{:S(2)}, u32[]{:S(2)}) %collective-permute-start.13) | collective-permute-done | bytes 36896 | tf_op jit(solution)/shard_map/ppermute | solution.py:18
  32.8 0.8 %shard_map.71 = (f32[40,128]{1,0:T(8,128)S(1)}, f32[40,128]{1,0:T(8,128)S(1)}, f32[40,128]{1,0:T(8,128)S(1)}, f32[40,128]{1,0:T(8,128)S(1)}) custom-call(f32[1,16,256]{2,1,0:T(8,128)S(1)} %shard_map.68.refs_0_, f32[1,16,256]{2,1,0:T(8,128)S(1)} %shard_map.69.refs_1_, f32[1,16,256]{2,1,0:T(8,128)S(1)} %shard_map.70.refs_2_, ...), custom_call_target="tpu_custom_call" | custom-call | flops 268435456 | bytes 1048576 | tf_op jit(solution)/shard_map/pallas_call | solution.py:229
  33.7 0.6 %collective-permute-start.15 = (f32[40,128]{1,0:T(8,128)S(1)}, f32[40,128]{1,0:T(8,128)S(1)}, u32[]{:S(2)}, u32[]{:S(2)}) collective-permute-start(f32[40,128]{1,0:T(8,128)S(1)} %get-tuple-element.18), channel_id=1, source_target_pairs={{0,16},{8,24},{16,0},{24,8},{1,17},{9,25},{17,1},{25,9},{2,18},{10... | collective-permute-start | bytes 61448 | tf_op jit(solution)/shard_map/ppermute | solution.py:18
  34.3 1.2 %collective-permute-start.16 = (f32[40,128]{1,0:T(8,128)S(1)}, f32[40,128]{1,0:T(8,128)S(1)}, u32[]{:S(2)}, u32[]{:S(2)}) collective-permute-start(f32[40,128]{1,0:T(8,128)S(1)} %get-tuple-element.19), channel_id=1, source_target_pairs={{0,8},{8,0},{16,24},{24,16},{1,9},{9,1},{17,25},{25,17},{2,10},{10... | collective-permute-start | bytes 61448 | tf_op jit(solution)/shard_map/ppermute | solution.py:18
  35.5 1.3 %collective-permute-done.14.refs_1_ = f32[40,128]{1,0:T(8,128)S(1)} collective-permute-done((f32[40,128]{1,0:T(8,128)S(1)}, f32[40,128]{1,0:T(8,128)S(1)}, u32[]{:S(2)}, u32[]{:S(2)}) %collective-permute-start.14) | collective-permute-done | bytes 20512 | tf_op jit(solution)/shard_map/ppermute | solution.py:18
  36.8 0.7 %collective-permute-done.15.refs_2_ = f32[40,128]{1,0:T(8,128)S(1)} collective-permute-done((f32[40,128]{1,0:T(8,128)S(1)}, f32[40,128]{1,0:T(8,128)S(1)}, u32[]{:S(2)}, u32[]{:S(2)}) %collective-permute-start.15) | collective-permute-done | bytes 20512 | tf_op jit(solution)/shard_map/ppermute | solution.py:18
  37.5 0.6 %shard_map.72 = (f32[1,16,256]{2,1,0:T(8,128)}, f32[1,1]{1,0:T(1,128)}) custom-call(f32[40,128]{1,0:T(8,128)S(1)} %get-tuple-element.16.refs_0_, f32[40,128]{1,0:T(8,128)S(1)} %collective-permute-done.14.refs_1_, f32[40,128]{1,0:T(8,128)S(1)} %collective-permute-done.15.refs_2_, f32[40,128]{1,0:T(8,128)S(1)} %collective-permute-done.16.refs_3_), custom_call_target="tpu_custom_call" | custom-call | tf_op jit(solution)/shard_map/pallas_call | solution.py:229
  (27 shorter events, 0.5 us)
Async XLA Ops:
  0.6 3.2 %copy-start = (bf16[128,16,256]{2,1,0:T(8,128)(2,1)S(1)}, bf16[128,16,256]{2,1,0:T(8,128)(2,1)}, u32[]{:S(2)}) copy-start(bf16[128,16,256]{2,1,0:T(8,128)(2,1)} %kernel_ref.1) | copy-start | bytes 3145732
  0.6 4.9 %collective-permute-start = (bf16[1,16,256]{2,1,0:T(8,128)(2,1)}, bf16[1,16,256]{2,1,0:T(8,128)(2,1)S(1)}, u32[]{:S(2)}, u32[]{:S(2)}) collective-permute-start(bf16[1,16,256]{2,1,0:T(8,128)(2,1)} %refs_0_.5), channel_id=1, source_target_pairs={{0,8},{8,0},{16,24},{24,16},{1,9},{9,1},{17,25},{25,17},{2,10},{10... | collective-permute-start | bytes 24584 | tf_op jit(solution)/shard_map/ppermute | solution.py:18
  1.2 4.4 %collective-permute-start.1 = (bf16[1,16,256]{2,1,0:T(8,128)(2,1)}, bf16[1,16,256]{2,1,0:T(8,128)(2,1)S(1)}, u32[]{:S(2)}, u32[]{:S(2)}) collective-permute-start(bf16[1,16,256]{2,1,0:T(8,128)(2,1)} %refs_0_.5), channel_id=1, source_target_pairs={{0,16},{8,24},{16,0},{24,8},{1,17},{9,25},{17,1},{25,9},{2,18},{10... | collective-permute-start | bytes 24584 | tf_op jit(solution)/shard_map/ppermute | solution.py:18
  3.7 3.3 %collective-permute-start.2 = (bf16[1,16,256]{2,1,0:T(8,128)(2,1)}, bf16[1,16,256]{2,1,0:T(8,128)(2,1)S(1)}, u32[]{:S(2)}, u32[]{:S(2)}) collective-permute-start(bf16[1,16,256]{2,1,0:T(8,128)(2,1)} %refs_0_.5), channel_id=1, source_target_pairs={{0,24},{8,16},{16,8},{24,0},{1,25},{9,17},{17,9},{25,1},{2,26},{10... | collective-permute-start | bytes 24584 | tf_op jit(solution)/shard_map/ppermute | solution.py:18
  3.8 1.0 %slice-start = ((bf16[128,16,256]{2,1,0:T(8,128)(2,1)}), bf16[128,16,128]{2,1,0:T(8,128)(2,1)S(1)}, s32[]{:S(2)}) async-start(bf16[128,16,256]{2,1,0:T(8,128)(2,1)} %kernel_ref.1), calls=%async_computation | async-start | bytes 1048576 | tf_op jit(solution)/shard_map/slice | solution.py:259
  4.8 2.2 %copy-start.1 = (bf16[1,16,256]{2,1,0:T(8,128)(2,1)S(1)}, bf16[1,16,256]{2,1,0:T(8,128)(2,1)}, u32[]{:S(2)}) copy-start(bf16[1,16,256]{2,1,0:T(8,128)(2,1)} %refs_0_.5) | copy-start | bytes 24580
  7.5 2.7 %copy-start.2 = (f32[4,128,256]{2,1,0:T(8,128)S(1)}, f32[4,128,256]{2,1,0:T(8,128)}, u32[]{:S(2)}) copy-start(f32[4,128,256]{2,1,0:T(8,128)} %refs_6_.1) | copy-start | bytes 1572868
  7.5 4.3 %collective-permute-start.4 = (bf16[256,128]{1,0:T(8,128)(2,1)S(1)}, bf16[256,128]{1,0:T(8,128)(2,1)S(1)}, u32[]{:S(2)}, u32[]{:S(2)}) collective-permute-start(bf16[256,128]{1,0:T(8,128)(2,1)S(1)} %shard_map.63), channel_id=1, source_target_pairs={{0,1},{1,0},{2,3},{3,2},{4,5},{5,4},{6,7},{7,6},{8,9},{9,8},{10,11... | collective-permute-start | bytes 196616 | tf_op jit(solution)/shard_map/ppermute | solution.py:18
  9.6 0.7 %copy-start.3 = (f32[128]{0:T(128)S(1)}, f32[128]{0:T(128)}, u32[]{:S(2)}) copy-start(f32[128]{0:T(128)} %param.7) | copy-start | bytes 1540
  9.6 6.0 %collective-permute-start.3 = (bf16[256,128]{1,0:T(8,128)(2,1)S(1)}, bf16[256,128]{1,0:T(8,128)(2,1)S(1)}, u32[]{:S(2)}, u32[]{:S(2)}) collective-permute-start(bf16[256,128]{1,0:T(8,128)(2,1)S(1)} %shard_map.61), channel_id=1, source_target_pairs={{0,1},{1,0},{2,3},{3,2},{4,5},{5,4},{6,7},{7,6},{8,9},{9,8},{10,11... | collective-permute-start | bytes 196616 | tf_op jit(solution)/shard_map/ppermute | solution.py:18
  11.9 5.9 %collective-permute-start.5 = (bf16[128,128]{1,0:T(8,128)(2,1)S(1)}, bf16[128,128]{1,0:T(8,128)(2,1)S(1)}, u32[]{:S(2)}, u32[]{:S(2)}) collective-permute-start(bf16[128,128]{1,0:T(8,128)(2,1)S(1)} %get-tuple-element.13), channel_id=1, source_target_pairs={{0,6},{1,7},{2,4},{3,5},{4,2},{5,3},{6,0},{7,1},{8,14},{9,15},{10,... | collective-permute-start | bytes 98312 | tf_op jit(solution)/shard_map/ppermute | solution.py:18
  15.5 4.8 %collective-permute-start.6 = (bf16[128,128]{1,0:T(8,128)(2,1)S(1)}, bf16[128,128]{1,0:T(8,128)(2,1)S(1)}, u32[]{:S(2)}, u32[]{:S(2)}) collective-permute-start(bf16[128,128]{1,0:T(8,128)(2,1)S(1)} %get-tuple-element.14), channel_id=1, source_target_pairs={{0,4},{1,5},{2,6},{3,7},{4,0},{5,1},{6,2},{7,3},{8,12},{9,13},{10,... | collective-permute-start | bytes 98312 | tf_op jit(solution)/shard_map/ppermute | solution.py:18
  15.5 4.8 %collective-permute-start.7 = (bf16[128,128]{1,0:T(8,128)(2,1)S(1)}, bf16[128,128]{1,0:T(8,128)(2,1)S(1)}, u32[]{:S(2)}, u32[]{:S(2)}) collective-permute-start(bf16[128,128]{1,0:T(8,128)(2,1)S(1)} %get-tuple-element.15), channel_id=1, source_target_pairs={{0,2},{1,3},{2,0},{3,1},{4,6},{5,7},{6,4},{7,5},{8,10},{9,11},{10,... | collective-permute-start | bytes 98312 | tf_op jit(solution)/shard_map/ppermute | solution.py:18
  20.4 4.5 %collective-permute-start.8 = (bf16[144,128]{1,0:T(8,128)(2,1)S(1)}, bf16[144,128]{1,0:T(8,128)(2,1)S(1)}, u32[]{:S(2)}, u32[]{:S(2)}) collective-permute-start(bf16[144,128]{1,0:T(8,128)(2,1)S(1)} %shard_map.65.refs_0_), channel_id=1, source_target_pairs={{0,2},{1,3},{2,0},{3,1},{4,6},{5,7},{6,4},{7,5},{8,10},{9,11},{10,... | collective-permute-start | bytes 110600 | tf_op jit(solution)/shard_map/ppermute | solution.py:18
  20.5 7.6 %collective-permute-start.9 = (bf16[144,128]{1,0:T(8,128)(2,1)S(1)}, bf16[144,128]{1,0:T(8,128)(2,1)S(1)}, u32[]{:S(2)}, u32[]{:S(2)}) collective-permute-start(bf16[144,128]{1,0:T(8,128)(2,1)S(1)} %shard_map.65.refs_0_), channel_id=1, source_target_pairs={{0,4},{1,5},{2,6},{3,7},{4,0},{5,1},{6,2},{7,3},{8,12},{9,13},{10,... | collective-permute-start | bytes 110600 | tf_op jit(solution)/shard_map/ppermute | solution.py:18
  22.6 5.8 %collective-permute-start.10 = (bf16[144,128]{1,0:T(8,128)(2,1)S(1)}, bf16[144,128]{1,0:T(8,128)(2,1)S(1)}, u32[]{:S(2)}, u32[]{:S(2)}) collective-permute-start(bf16[144,128]{1,0:T(8,128)(2,1)S(1)} %shard_map.65.refs_0_), channel_id=1, source_target_pairs={{0,6},{1,7},{2,4},{3,5},{4,2},{5,3},{6,0},{7,1},{8,14},{9,15},{10,... | collective-permute-start | bytes 110600 | tf_op jit(solution)/shard_map/ppermute | solution.py:18
  24.9 6.7 %collective-permute-start.11 = (bf16[272,128]{1,0:T(8,128)(2,1)S(1)}, bf16[272,128]{1,0:T(8,128)(2,1)S(1)}, u32[]{:S(2)}, u32[]{:S(2)}) collective-permute-start(bf16[272,128]{1,0:T(8,128)(2,1)S(1)} %shard_map.66.refs_0_.refs_4_), channel_id=1, source_target_pairs={{0,1},{1,0},{2,3},{3,2},{4,5},{5,4},{6,7},{7,6},{8,9},{9,8},{10,11... | collective-permute-start | bytes 208904 | tf_op jit(solution)/shard_map/ppermute | solution.py:18
  28.1 4.3 %collective-permute-start.12 = (bf16[144,128]{1,0:T(8,128)(2,1)S(1)}, bf16[144,128]{1,0:T(8,128)(2,1)S(1)}, u32[]{:S(2)}, u32[]{:S(2)}) collective-permute-start(bf16[144,128]{1,0:T(8,128)(2,1)S(1)} %collective-permute-done.9.refs_0_.refs_5_), channel_id=1, source_target_pairs={{0,1},{1,0},{2,3},{3,2},{4,5},{5,4},{6,7},{7,6},{8,9},{9,8},{10,11... | collective-permute-start | bytes 110600 | tf_op jit(solution)/shard_map/ppermute | solution.py:18
  28.4 4.4 %collective-permute-start.13 = (bf16[144,128]{1,0:T(8,128)(2,1)S(1)}, bf16[144,128]{1,0:T(8,128)(2,1)S(1)}, u32[]{:S(2)}, u32[]{:S(2)}) collective-permute-start(bf16[144,128]{1,0:T(8,128)(2,1)S(1)} %collective-permute-done.10.refs_1_.refs_6_), channel_id=1, source_target_pairs={{0,1},{1,0},{2,3},{3,2},{4,5},{5,4},{6,7},{7,6},{8,9},{9,8},{10,11... | collective-permute-start | bytes 110600 | tf_op jit(solution)/shard_map/ppermute | solution.py:18
  33.6 3.3 %collective-permute-start.14 = (f32[40,128]{1,0:T(8,128)S(1)}, f32[40,128]{1,0:T(8,128)S(1)}, u32[]{:S(2)}, u32[]{:S(2)}) collective-permute-start(f32[40,128]{1,0:T(8,128)S(1)} %get-tuple-element.17), channel_id=1, source_target_pairs={{0,24},{8,16},{16,8},{24,0},{1,25},{9,17},{17,9},{25,1},{2,26},{10... | collective-permute-start | bytes 61448 | tf_op jit(solution)/shard_map/ppermute | solution.py:18
  33.7 3.8 %collective-permute-start.15 = (f32[40,128]{1,0:T(8,128)S(1)}, f32[40,128]{1,0:T(8,128)S(1)}, u32[]{:S(2)}, u32[]{:S(2)}) collective-permute-start(f32[40,128]{1,0:T(8,128)S(1)} %get-tuple-element.18), channel_id=1, source_target_pairs={{0,16},{8,24},{16,0},{24,8},{1,17},{9,25},{17,1},{25,9},{2,18},{10... | collective-permute-start | bytes 61448 | tf_op jit(solution)/shard_map/ppermute | solution.py:18
  34.3 3.2 %collective-permute-start.16 = (f32[40,128]{1,0:T(8,128)S(1)}, f32[40,128]{1,0:T(8,128)S(1)}, u32[]{:S(2)}, u32[]{:S(2)}) collective-permute-start(f32[40,128]{1,0:T(8,128)S(1)} %get-tuple-element.19), channel_id=1, source_target_pairs={{0,8},{8,0},{16,24},{24,16},{1,9},{9,1},{17,25},{25,17},{2,10},{10... | collective-permute-start | bytes 61448 | tf_op jit(solution)/shard_map/ppermute | solution.py:18

commit v10 on v9

--- a/solution.py
+++ b/solution.py
@@ -9,7 +9,6 @@
 
 EXTRA_ROWS = 16
 WEIGHT_ROWS = 8
-MISFIT_ROWS = 8
 VMEM_LIMIT = 24 * 1024 * 1024
 SMALL_LIMIT = 4 * 1024 * 1024
 
@@ -196,7 +195,7 @@
     extra = 0.0
     for ref in groups:
         extra += ref[ref.shape[0] - EXTRA_ROWS :, :].astype(jnp.float32)
-    squared = jnp.full((MISFIT_ROWS, lanes), jnp.sum(extra), jnp.float32)
+    squared = three_parts(jnp.full((1, lanes), jnp.sum(extra), jnp.float32))
     for i, ref in enumerate(done):
         away, group = i // n_groups, (place ^ (i % n_groups * slots)) // slots
         for v in range(of_group):
@@ -206,8 +205,9 @@
         slots_ref[(block ^ (near - 1)) * of_block + v] = total
     for v, ref in enumerate(outs):
         for i in range(steps // lanes):
-            ref[i * points : (i + 1) * points, :] = slots_ref[v, :, i * lanes : (i + 1) * lanes]
-        ref[steps // lanes * points :, :] = squared
+            some = slots_ref[v, :, i * lanes : (i + 1) * lanes]
+            ref[i * points : (i + 1) * points, :] = some.astype(ref.dtype)
+        ref[steps // lanes * points :, :] = squared.astype(ref.dtype)
 
 
 def total_body(scale, *refs):
@@ -216,11 +216,11 @@
     lanes = terms[0].shape[1]
     total = terms[0][...]
     for term in terms[1:]:
-        total += term[...]
+        total += term[...].astype(jnp.float32)
     for i in range(steps // lanes):
         gradient_ref[0, :, i * lanes : (i + 1) * lanes] = total[i * points : (i + 1) * points]
     at = steps // lanes * points
-    misfit_ref[...] = total[at : at + 1, :1] * scale
+    misfit_ref[...] = jnp.sum(total[at:, :1], axis=0, keepdims=True) * scale
 
 
 def call(body, out_shape, operands, limit=SMALL_LIMIT, **options):
@@ -317,7 +317,7 @@
         first = far - len(terms) - 1
         terms += [swap(out, "par", b * near) for b, out in zip(range(first, 0, -1), outs[::-1])]
     residual = call(residual_body, struct((rows + EXTRA_ROWS, sensors), jnp.bfloat16), (own, *terms))
-    parts = [residual] + [swap(residual, "par", b * near) for b in range(1, far)]
+    parts = [residual] + [swap(residual, "par", b * near) for b in range(far - 1, 0, -1)][::-1]
     n_last = 2 if slots % 2 == 0 else 1
     starts = [*range(0, far - slots, slots), *range(far - slots, far, slots // n_last), far]
     pieces = []
@@ -356,7 +356,7 @@
     done += [adjoint_piece(i, every[i]) for i in range(len(done), len(every) - 1)]
     partials = call(
         functools.partial(adjoint_last_body, near, slots, lags, n_groups, n_last),
-        [struct((steps // lanes * points + MISFIT_ROWS, lanes), jnp.float32)] * vectors,
+        [struct((steps // lanes * points + EXTRA_ROWS, lanes), jnp.bfloat16 if v else jnp.float32) for v in range(vectors)],
         (*done, left, *[piece for group in every for piece in group]),
         VMEM_LIMIT,
         scratch_shapes=[pltpu.VMEM((vectors, points, steps), jnp.float32)] + scratch,

time: 38.3 us -> 38.2 us (level)
  no operation moved by 1% of the time
where the time goes in v10:
time: 38.2 us; the launch traced here: 38 us
  starting transfers between devices  21 us (55%)
  waiting for transfers between devices  8.61 us (23%)
  Pallas kernels  6.41 us (17%)
  local copies, waits for them, and re-layouts  1.21 us (3%)
  between operations  0.8 us (2%)
    ppermute x17, starting transfers between devices, swap(): lax.ppermute(value, axis, [(i, i ^ step) for i in range(lax.axis_size(axi...  21 us
    ppermute x17, waiting for transfers between devices, swap(): lax.ppermute(value, axis, [(i, i ^ step) for i in range(lax.axis_size(axi...  8.61 us
    pallas_call x14, Pallas kernels, call(): pl.pallas_call(body, out_shape=out_shape, out_specs=jax.tree.map(lambda _...  6.41 us
    unnamed x9, local copies, waits for them, and re-layouts  0.83 us
  transfers between devices with their start and end apart: 17, of which 8 were waited for; matrix products, arithmetic and copies ran while one was open for 2% of the time, Pallas kernels for 12%

profile of v10, /device:TPU:0, one launch (start us, length us, event | category | flops | bytes accessed | tf_op | source)
XLA Modules:
  0.0 38.0 jit_solution(17312139453470955054)
XLA Ops:
  0.6 0.5 %collective-permute-start = (bf16[1,16,256]{2,1,0:T(8,128)(2,1)}, bf16[1,16,256]{2,1,0:T(8,128)(2,1)S(1)}, u32[]{:S(2)}, u32[]{:S(2)}) collective-permute-start(bf16[1,16,256]{2,1,0:T(8,128)(2,1)} %refs_0_.5), channel_id=1, source_target_pairs={{0,8},{8,0},{16,24},{24,16},{1,9},{9,1},{17,25},{25,17},{2,10},{10... | collective-permute-start | bytes 24584 | tf_op jit(solution)/shard_map/ppermute | solution.py:17
  1.2 2.6 %collective-permute-start.1 = (bf16[1,16,256]{2,1,0:T(8,128)(2,1)}, bf16[1,16,256]{2,1,0:T(8,128)(2,1)S(1)}, u32[]{:S(2)}, u32[]{:S(2)}) collective-permute-start(bf16[1,16,256]{2,1,0:T(8,128)(2,1)} %refs_0_.5), channel_id=1, source_target_pairs={{0,16},{8,24},{16,0},{24,8},{1,17},{9,25},{17,1},{25,9},{2,18},{10... | collective-permute-start | bytes 24584 | tf_op jit(solution)/shard_map/ppermute | solution.py:17
  3.8 0.6 %shard_map.59.refs_5_.refs_1_ = bf16[128,16,128]{2,1,0:T(8,128)(2,1)S(1)} custom-call(bf16[128,16,256]{2,1,0:T(8,128)(2,1)S(1)} %copy-done), custom_call_target="tpu_custom_call" | custom-call | bytes 1572864 | tf_op jit(solution)/shard_map/pallas_call | solution.py:229
  4.5 0.4 %slice-done = bf16[128,16,128]{2,1,0:T(8,128)(2,1)S(1)} async-done(((bf16[128,16,256]{2,1,0:T(8,128)(2,1)}), bf16[128,16,128]{2,1,0:T(8,128)(2,1)S(1)}, s32[]{:S(2)}) %slice-start) | async-done | bytes 524312 | tf_op jit(solution)/shard_map/slice | solution.py:259
  4.8 0.7 %copy.7 = bf16[128,16,128]{0,1,2:T(8,128)(2,1)S(1)} copy(bf16[128,16,128]{2,1,0:T(8,128)(2,1)S(1)} %slice-done) | data formatting | bytes 1048576
  5.6 1.4 %collective-permute-done.2.refs_3_ = bf16[1,16,256]{2,1,0:T(8,128)(2,1)S(1)} collective-permute-done((bf16[1,16,256]{2,1,0:T(8,128)(2,1)}, bf16[1,16,256]{2,1,0:T(8,128)(2,1)S(1)}, u32[]{:S(2)}, u32[]{:S(2)}) %collective-permute-start.2) | collective-permute-done | bytes 8224 | tf_op jit(solution)/shard_map/ppermute | solution.py:17
  7.0 0.5 %shard_map.63 = bf16[256,128]{1,0:T(8,128)(2,1)S(1)} custom-call(bf16[1,16,256]{2,1,0:T(8,128)(2,1)S(1)} %copy-done.1, bf16[1,16,256]{2,1,0:T(8,128)(2,1)S(1)} %collective-permute-done.refs_1_, bf16[1,16,256]{2,1,0:T(8,128)(2,1)S(1)} %collective-permute-done.1.refs_2_, bf16[1,16,256]{2,1,0:T(8,128)(2,1)S(1)} %collective-permute-done.2.refs_3_, ...), custom_call_target="tpu_custom_call" | custom-call | flops 268435456 | bytes 1048576 | tf_op jit(solution)/shard_map/pallas_call | solution.py:229
  7.5 1.6 %collective-permute-start.4 = (bf16[256,128]{1,0:T(8,128)(2,1)S(1)}, bf16[256,128]{1,0:T(8,128)(2,1)S(1)}, u32[]{:S(2)}, u32[]{:S(2)}) collective-permute-start(bf16[256,128]{1,0:T(8,128)(2,1)S(1)} %shard_map.63), channel_id=1, source_target_pairs={{0,1},{1,0},{2,3},{3,2},{4,5},{5,4},{6,7},{7,6},{8,9},{9,8},{10,11... | collective-permute-start | bytes 196616 | tf_op jit(solution)/shard_map/ppermute | solution.py:17
  9.1 0.5 %shard_map.61 = bf16[256,128]{1,0:T(8,128)(2,1)S(1)} custom-call(bf16[1,16,256]{2,1,0:T(8,128)(2,1)S(1)} %copy-done.1, bf16[1,16,256]{2,1,0:T(8,128)(2,1)S(1)} %collective-permute-done.refs_1_, bf16[1,16,256]{2,1,0:T(8,128)(2,1)S(1)} %collective-permute-done.1.refs_2_, bf16[1,16,256]{2,1,0:T(8,128)(2,1)S(1)} %collective-permute-done.2.refs_3_, ...), custom_call_target="tpu_custom_call" | custom-call | flops 268435456 | bytes 1048576 | tf_op jit(solution)/shard_map/pallas_call | solution.py:229
  9.6 0.6 %collective-permute-start.3 = (bf16[256,128]{1,0:T(8,128)(2,1)S(1)}, bf16[256,128]{1,0:T(8,128)(2,1)S(1)}, u32[]{:S(2)}, u32[]{:S(2)}) collective-permute-start(bf16[256,128]{1,0:T(8,128)(2,1)S(1)} %shard_map.61), channel_id=1, source_target_pairs={{0,1},{1,0},{2,3},{3,2},{4,5},{5,4},{6,7},{7,6},{8,9},{9,8},{10,11... | collective-permute-start | bytes 196616 | tf_op jit(solution)/shard_map/ppermute | solution.py:17
  10.2 1.0 %shard_map.60.own_ref = f32[520,128]{1,0:T(8,128)S(1)} custom-call(bf16[1,16,256]{2,1,0:T(8,128)(2,1)S(1)} %copy-done.1, bf16[1,16,256]{2,1,0:T(8,128)(2,1)S(1)} %collective-permute-done.refs_1_, bf16[1,16,256]{2,1,0:T(8,128)(2,1)S(1)} %collective-permute-done.1.refs_2_, bf16[1,16,256]{2,1,0:T(8,128)(2,1)S(1)} %collective-permute-done.2.refs_3_, ...), custom_call_target="tpu_custom_call" | custom-call | flops 536870912 | bytes 1048576 | tf_op jit(solution)/shard_map/pallas_call | solution.py:229
  11.2 0.6 %collective-permute-done.4.refs_0_ = bf16[256,128]{1,0:T(8,128)(2,1)S(1)} collective-permute-done((bf16[256,128]{1,0:T(8,128)(2,1)S(1)}, bf16[256,128]{1,0:T(8,128)(2,1)S(1)}, u32[]{:S(2)}, u32[]{:S(2)}) %collective-permute-start.4) | collective-permute-done | bytes 65568 | tf_op jit(solution)/shard_map/ppermute | solution.py:17
  11.9 3.7 %collective-permute-start.5 = (bf16[128,128]{1,0:T(8,128)(2,1)S(1)}, bf16[128,128]{1,0:T(8,128)(2,1)S(1)}, u32[]{:S(2)}, u32[]{:S(2)}) collective-permute-start(bf16[128,128]{1,0:T(8,128)(2,1)S(1)} %get-tuple-element.13), channel_id=1, source_target_pairs={{0,6},{1,7},{2,4},{3,5},{4,2},{5,3},{6,0},{7,1},{8,14},{9,15},{10,... | collective-permute-start | bytes 98312 | tf_op jit(solution)/shard_map/ppermute | solution.py:17
  15.5 0.8 %collective-permute-start.7 = (bf16[128,128]{1,0:T(8,128)(2,1)S(1)}, bf16[128,128]{1,0:T(8,128)(2,1)S(1)}, u32[]{:S(2)}, u32[]{:S(2)}) collective-permute-start(bf16[128,128]{1,0:T(8,128)(2,1)S(1)} %get-tuple-element.15), channel_id=1, source_target_pairs={{0,2},{1,3},{2,0},{3,1},{4,6},{5,7},{6,4},{7,5},{8,10},{9,11},{10,... | collective-permute-start | bytes 98312 | tf_op jit(solution)/shard_map/ppermute | solution.py:17
  16.4 1.4 %collective-permute-done.5.refs_0_ = bf16[128,128]{1,0:T(8,128)(2,1)S(1)} collective-permute-done((bf16[128,128]{1,0:T(8,128)(2,1)S(1)}, bf16[128,128]{1,0:T(8,128)(2,1)S(1)}, u32[]{:S(2)}, u32[]{:S(2)}) %collective-permute-start.5) | collective-permute-done | bytes 32800 | tf_op jit(solution)/shard_map/ppermute | solution.py:17
  17.8 2.5 %collective-permute-done.6.refs_1_ = bf16[128,128]{1,0:T(8,128)(2,1)S(1)} collective-permute-done((bf16[128,128]{1,0:T(8,128)(2,1)S(1)}, bf16[128,128]{1,0:T(8,128)(2,1)S(1)}, u32[]{:S(2)}, u32[]{:S(2)}) %collective-permute-start.6) | collective-permute-done | bytes 32800 | tf_op jit(solution)/shard_map/ppermute | solution.py:17
  20.5 2.2 %collective-permute-start.9 = (bf16[144,128]{1,0:T(8,128)(2,1)S(1)}, bf16[144,128]{1,0:T(8,128)(2,1)S(1)}, u32[]{:S(2)}, u32[]{:S(2)}) collective-permute-start(bf16[144,128]{1,0:T(8,128)(2,1)S(1)} %shard_map.65.refs_0_), channel_id=1, source_target_pairs={{0,4},{1,5},{2,6},{3,7},{4,0},{5,1},{6,2},{7,3},{8,12},{9,13},{10,... | collective-permute-start | bytes 110600 | tf_op jit(solution)/shard_map/ppermute | solution.py:17
  22.6 2.2 %collective-permute-start.10 = (bf16[144,128]{1,0:T(8,128)(2,1)S(1)}, bf16[144,128]{1,0:T(8,128)(2,1)S(1)}, u32[]{:S(2)}, u32[]{:S(2)}) collective-permute-start(bf16[144,128]{1,0:T(8,128)(2,1)S(1)} %shard_map.65.refs_0_), channel_id=1, source_target_pairs={{0,6},{1,7},{2,4},{3,5},{4,2},{5,3},{6,0},{7,1},{8,14},{9,15},{10,... | collective-permute-start | bytes 110600 | tf_op jit(solution)/shard_map/ppermute | solution.py:17
  24.9 2.3 %collective-permute-start.11 = (bf16[272,128]{1,0:T(8,128)(2,1)S(1)}, bf16[272,128]{1,0:T(8,128)(2,1)S(1)}, u32[]{:S(2)}, u32[]{:S(2)}) collective-permute-start(bf16[272,128]{1,0:T(8,128)(2,1)S(1)} %shard_map.66.refs_0_.refs_4_), channel_id=1, source_target_pairs={{0,1},{1,0},{2,3},{3,2},{4,5},{5,4},{6,7},{7,6},{8,9},{9,8},{10,11... | collective-permute-start | bytes 208904 | tf_op jit(solution)/shard_map/ppermute | solution.py:17
  27.1 0.2 shard_map.67.refs_1_.refs_2_.refs_3_
  27.3 0.7 %shard_map.68.refs_0_ = f32[1,16,256]{2,1,0:T(8,128)S(1)} custom-call(bf16[272,128]{1,0:T(8,128)(2,1)S(1)} %shard_map.66.refs_0_.refs_4_, bf16[256,2048]{1,0:T(8,128)(2,1)S(1)} %shard_map.67.refs_1_.refs_2_.refs_3_), custom_call_target="tpu_custom_call" | custom-call | tf_op jit(solution)/shard_map/pallas_call | solution.py:229
  28.1 0.3 collective-permute-done.10.refs_1_.refs_6_
  28.4 2.5 %collective-permute-start.13 = (bf16[144,128]{1,0:T(8,128)(2,1)S(1)}, bf16[144,128]{1,0:T(8,128)(2,1)S(1)}, u32[]{:S(2)}, u32[]{:S(2)}) collective-permute-start(bf16[144,128]{1,0:T(8,128)(2,1)S(1)} %collective-permute-done.10.refs_1_.refs_6_), channel_id=1, source_target_pairs={{0,1},{1,0},{2,3},{3,2},{4,5},{5,4},{6,7},{7,6},{8,9},{9,8},{10,11... | collective-permute-start | bytes 110600 | tf_op jit(solution)/shard_map/ppermute | solution.py:17
  30.9 0.7 %shard_map.69.refs_1_ = f32[1,16,256]{2,1,0:T(8,128)S(1)} custom-call(bf16[144,128]{1,0:T(8,128)(2,1)S(1)} %collective-permute-done.9.refs_0_.refs_5_, bf16[144,128]{1,0:T(8,128)(2,1)S(1)} %collective-permute-done.10.refs_1_.refs_6_, bf16[256,2048]{1,0:T(8,128)(2,1)S(1)} %shard_map.67.refs_1_.refs_2_.refs_3_), custom_call_target="tpu_custom_call" | custom-call | flops 536870912 | bytes 1048576 | tf_op jit(solution)/shard_map/pallas_call | solution.py:229
  31.6 0.7 %shard_map.70.refs_2_ = f32[1,16,256]{2,1,0:T(8,128)S(1)} custom-call(bf16[272,128]{1,0:T(8,128)(2,1)S(1)} %collective-permute-done.11.refs_0_.refs_7_, bf16[256,2048]{1,0:T(8,128)(2,1)S(1)} %shard_map.67.refs_1_.refs_2_.refs_3_), custom_call_target="tpu_custom_call" | custom-call | flops 536870912 | bytes 1048576 | tf_op jit(solution)/shard_map/pallas_call | solution.py:229
  32.4 0.4 %collective-permute-done.13.refs_9_ = bf16[144,128]{1,0:T(8,128)(2,1)S(1)} collective-permute-done((bf16[144,128]{1,0:T(8,128)(2,1)S(1)}, bf16[144,128]{1,0:T(8,128)(2,1)S(1)}, u32[]{:S(2)}, u32[]{:S(2)}) %collective-permute-start.13) | collective-permute-done | bytes 36896 | tf_op jit(solution)/shard_map/ppermute | solution.py:17
  32.8 0.8 %shard_map.71 = (f32[48,128]{1,0:T(8,128)S(1)}, bf16[48,128]{1,0:T(8,128)(2,1)S(1)}, bf16[48,128]{1,0:T(8,128)(2,1)S(1)}, bf16[48,128]{1,0:T(8,128)(2,1)S(1)}) custom-call(f32[1,16,256]{2,1,0:T(8,128)S(1)} %shard_map.68.refs_0_, f32[1,16,256]{2,1,0:T(8,128)S(1)} %shard_map.69.refs_1_, f32[1,16,256]{2,1,0:T(8,128)S(1)} %shard_map.70.refs_2_, ...), custom_call_target="tpu_custom_call" | custom-call | flops 268435456 | bytes 1048576 | tf_op jit(solution)/shard_map/pallas_call | solution.py:229
  33.7 0.6 %collective-permute-start.15 = (bf16[48,128]{1,0:T(8,128)(2,1)S(1)}, bf16[48,128]{1,0:T(8,128)(2,1)S(1)}, u32[]{:S(2)}, u32[]{:S(2)}) collective-permute-start(bf16[48,128]{1,0:T(8,128)(2,1)S(1)} %get-tuple-element.18), channel_id=1, source_target_pairs={{0,16},{8,24},{16,0},{24,8},{1,17},{9,25},{17,1},{25,9},{2,18},{10... | collective-permute-start | bytes 36872 | tf_op jit(solution)/shard_map/ppermute | solution.py:17
  34.3 1.2 %collective-permute-start.16 = (bf16[48,128]{1,0:T(8,128)(2,1)S(1)}, bf16[48,128]{1,0:T(8,128)(2,1)S(1)}, u32[]{:S(2)}, u32[]{:S(2)}) collective-permute-start(bf16[48,128]{1,0:T(8,128)(2,1)S(1)} %get-tuple-element.19), channel_id=1, source_target_pairs={{0,8},{8,0},{16,24},{24,16},{1,9},{9,1},{17,25},{25,17},{2,10},{10... | collective-permute-start | bytes 36872 | tf_op jit(solution)/shard_map/ppermute | solution.py:17
  35.5 1.3 %collective-permute-done.14.refs_1_ = bf16[48,128]{1,0:T(8,128)(2,1)S(1)} collective-permute-done((bf16[48,128]{1,0:T(8,128)(2,1)S(1)}, bf16[48,128]{1,0:T(8,128)(2,1)S(1)}, u32[]{:S(2)}, u32[]{:S(2)}) %collective-permute-start.14) | collective-permute-done | bytes 12320 | tf_op jit(solution)/shard_map/ppermute | solution.py:17
  36.8 0.7 %collective-permute-done.15.refs_2_ = bf16[48,128]{1,0:T(8,128)(2,1)S(1)} collective-permute-done((bf16[48,128]{1,0:T(8,128)(2,1)S(1)}, bf16[48,128]{1,0:T(8,128)(2,1)S(1)}, u32[]{:S(2)}, u32[]{:S(2)}) %collective-permute-start.15) | collective-permute-done | bytes 12320 | tf_op jit(solution)/shard_map/ppermute | solution.py:17
  37.4 0.6 %shard_map.72 = (f32[1,16,256]{2,1,0:T(8,128)}, f32[1,1]{1,0:T(1,128)}) custom-call(f32[48,128]{1,0:T(8,128)S(1)} %get-tuple-element.16.refs_0_, bf16[48,128]{1,0:T(8,128)(2,1)S(1)} %collective-permute-done.14.refs_1_, bf16[48,128]{1,0:T(8,128)(2,1)S(1)} %collective-permute-done.15.refs_2_, bf16[48,128]{1,0:T(8,128)(2,1)S(1)} %collective-permute-done.16.refs_3_), custom_call_target="tpu_custom_call" | custom-call | tf_op jit(solution)/shard_map/pallas_call | solution.py:229
  (27 shorter events, 0.5 us)
Async XLA Ops:
  0.6 3.2 %copy-start = (bf16[128,16,256]{2,1,0:T(8,128)(2,1)S(1)}, bf16[128,16,256]{2,1,0:T(8,128)(2,1)}, u32[]{:S(2)}) copy-start(bf16[128,16,256]{2,1,0:T(8,128)(2,1)} %kernel_ref.1) | copy-start | bytes 3145732
  0.6 4.9 %collective-permute-start = (bf16[1,16,256]{2,1,0:T(8,128)(2,1)}, bf16[1,16,256]{2,1,0:T(8,128)(2,1)S(1)}, u32[]{:S(2)}, u32[]{:S(2)}) collective-permute-start(bf16[1,16,256]{2,1,0:T(8,128)(2,1)} %refs_0_.5), channel_id=1, source_target_pairs={{0,8},{8,0},{16,24},{24,16},{1,9},{9,1},{17,25},{25,17},{2,10},{10... | collective-permute-start | bytes 24584 | tf_op jit(solution)/shard_map/ppermute | solution.py:17
  1.2 4.4 %collective-permute-start.1 = (bf16[1,16,256]{2,1,0:T(8,128)(2,1)}, bf16[1,16,256]{2,1,0:T(8,128)(2,1)S(1)}, u32[]{:S(2)}, u32[]{:S(2)}) collective-permute-start(bf16[1,16,256]{2,1,0:T(8,128)(2,1)} %refs_0_.5), channel_id=1, source_target_pairs={{0,16},{8,24},{16,0},{24,8},{1,17},{9,25},{17,1},{25,9},{2,18},{10... | collective-permute-start | bytes 24584 | tf_op jit(solution)/shard_map/ppermute | solution.py:17
  3.7 3.3 %collective-permute-start.2 = (bf16[1,16,256]{2,1,0:T(8,128)(2,1)}, bf16[1,16,256]{2,1,0:T(8,128)(2,1)S(1)}, u32[]{:S(2)}, u32[]{:S(2)}) collective-permute-start(bf16[1,16,256]{2,1,0:T(8,128)(2,1)} %refs_0_.5), channel_id=1, source_target_pairs={{0,24},{8,16},{16,8},{24,0},{1,25},{9,17},{17,9},{25,1},{2,26},{10... | collective-permute-start | bytes 24584 | tf_op jit(solution)/shard_map/ppermute | solution.py:17
  3.8 1.0 %slice-start = ((bf16[128,16,256]{2,1,0:T(8,128)(2,1)}), bf16[128,16,128]{2,1,0:T(8,128)(2,1)S(1)}, s32[]{:S(2)}) async-start(bf16[128,16,256]{2,1,0:T(8,128)(2,1)} %kernel_ref.1), calls=%async_computation | async-start | bytes 1048576 | tf_op jit(solution)/shard_map/slice | solution.py:259
  4.8 2.2 %copy-start.1 = (bf16[1,16,256]{2,1,0:T(8,128)(2,1)S(1)}, bf16[1,16,256]{2,1,0:T(8,128)(2,1)}, u32[]{:S(2)}) copy-start(bf16[1,16,256]{2,1,0:T(8,128)(2,1)} %refs_0_.5) | copy-start | bytes 24580
  7.5 2.7 %copy-start.2 = (f32[4,128,256]{2,1,0:T(8,128)S(1)}, f32[4,128,256]{2,1,0:T(8,128)}, u32[]{:S(2)}) copy-start(f32[4,128,256]{2,1,0:T(8,128)} %refs_6_.1) | copy-start | bytes 1572868
  7.5 4.3 %collective-permute-start.4 = (bf16[256,128]{1,0:T(8,128)(2,1)S(1)}, bf16[256,128]{1,0:T(8,128)(2,1)S(1)}, u32[]{:S(2)}, u32[]{:S(2)}) collective-permute-start(bf16[256,128]{1,0:T(8,128)(2,1)S(1)} %shard_map.63), channel_id=1, source_target_pairs={{0,1},{1,0},{2,3},{3,2},{4,5},{5,4},{6,7},{7,6},{8,9},{9,8},{10,11... | collective-permute-start | bytes 196616 | tf_op jit(solution)/shard_map/ppermute | solution.py:17
  9.6 0.7 %copy-start.3 = (f32[128]{0:T(128)S(1)}, f32[128]{0:T(128)}, u32[]{:S(2)}) copy-start(f32[128]{0:T(128)} %param.7) | copy-start | bytes 1540
  9.6 6.0 %collective-permute-start.3 = (bf16[256,128]{1,0:T(8,128)(2,1)S(1)}, bf16[256,128]{1,0:T(8,128)(2,1)S(1)}, u32[]{:S(2)}, u32[]{:S(2)}) collective-permute-start(bf16[256,128]{1,0:T(8,128)(2,1)S(1)} %shard_map.61), channel_id=1, source_target_pairs={{0,1},{1,0},{2,3},{3,2},{4,5},{5,4},{6,7},{7,6},{8,9},{9,8},{10,11... | collective-permute-start | bytes 196616 | tf_op jit(solution)/shard_map/ppermute | solution.py:17
  11.9 5.9 %collective-permute-start.5 = (bf16[128,128]{1,0:T(8,128)(2,1)S(1)}, bf16[128,128]{1,0:T(8,128)(2,1)S(1)}, u32[]{:S(2)}, u32[]{:S(2)}) collective-permute-start(bf16[128,128]{1,0:T(8,128)(2,1)S(1)} %get-tuple-element.13), channel_id=1, source_target_pairs={{0,6},{1,7},{2,4},{3,5},{4,2},{5,3},{6,0},{7,1},{8,14},{9,15},{10,... | collective-permute-start | bytes 98312 | tf_op jit(solution)/shard_map/ppermute | solution.py:17
  15.5 4.8 %collective-permute-start.6 = (bf16[128,128]{1,0:T(8,128)(2,1)S(1)}, bf16[128,128]{1,0:T(8,128)(2,1)S(1)}, u32[]{:S(2)}, u32[]{:S(2)}) collective-permute-start(bf16[128,128]{1,0:T(8,128)(2,1)S(1)} %get-tuple-element.14), channel_id=1, source_target_pairs={{0,4},{1,5},{2,6},{3,7},{4,0},{5,1},{6,2},{7,3},{8,12},{9,13},{10,... | collective-permute-start | bytes 98312 | tf_op jit(solution)/shard_map/ppermute | solution.py:17
  15.5 4.8 %collective-permute-start.7 = (bf16[128,128]{1,0:T(8,128)(2,1)S(1)}, bf16[128,128]{1,0:T(8,128)(2,1)S(1)}, u32[]{:S(2)}, u32[]{:S(2)}) collective-permute-start(bf16[128,128]{1,0:T(8,128)(2,1)S(1)} %get-tuple-element.15), channel_id=1, source_target_pairs={{0,2},{1,3},{2,0},{3,1},{4,6},{5,7},{6,4},{7,5},{8,10},{9,11},{10,... | collective-permute-start | bytes 98312 | tf_op jit(solution)/shard_map/ppermute | solution.py:17
  20.4 4.5 %collective-permute-start.8 = (bf16[144,128]{1,0:T(8,128)(2,1)S(1)}, bf16[144,128]{1,0:T(8,128)(2,1)S(1)}, u32[]{:S(2)}, u32[]{:S(2)}) collective-permute-start(bf16[144,128]{1,0:T(8,128)(2,1)S(1)} %shard_map.65.refs_0_), channel_id=1, source_target_pairs={{0,2},{1,3},{2,0},{3,1},{4,6},{5,7},{6,4},{7,5},{8,10},{9,11},{10,... | collective-permute-start | bytes 110600 | tf_op jit(solution)/shard_map/ppermute | solution.py:17
  20.5 7.6 %collective-permute-start.9 = (bf16[144,128]{1,0:T(8,128)(2,1)S(1)}, bf16[144,128]{1,0:T(8,128)(2,1)S(1)}, u32[]{:S(2)}, u32[]{:S(2)}) collective-permute-start(bf16[144,128]{1,0:T(8,128)(2,1)S(1)} %shard_map.65.refs_0_), channel_id=1, source_target_pairs={{0,4},{1,5},{2,6},{3,7},{4,0},{5,1},{6,2},{7,3},{8,12},{9,13},{10,... | collective-permute-start | bytes 110600 | tf_op jit(solution)/shard_map/ppermute | solution.py:17
  22.6 5.8 %collective-permute-start.10 = (bf16[144,128]{1,0:T(8,128)(2,1)S(1)}, bf16[144,128]{1,0:T(8,128)(2,1)S(1)}, u32[]{:S(2)}, u32[]{:S(2)}) collective-permute-start(bf16[144,128]{1,0:T(8,128)(2,1)S(1)} %shard_map.65.refs_0_), channel_id=1, source_target_pairs={{0,6},{1,7},{2,4},{3,5},{4,2},{5,3},{6,0},{7,1},{8,14},{9,15},{10,... | collective-permute-start | bytes 110600 | tf_op jit(solution)/shard_map/ppermute | solution.py:17
  24.9 6.7 %collective-permute-start.11 = (bf16[272,128]{1,0:T(8,128)(2,1)S(1)}, bf16[272,128]{1,0:T(8,128)(2,1)S(1)}, u32[]{:S(2)}, u32[]{:S(2)}) collective-permute-start(bf16[272,128]{1,0:T(8,128)(2,1)S(1)} %shard_map.66.refs_0_.refs_4_), channel_id=1, source_target_pairs={{0,1},{1,0},{2,3},{3,2},{4,5},{5,4},{6,7},{7,6},{8,9},{9,8},{10,11... | collective-permute-start | bytes 208904 | tf_op jit(solution)/shard_map/ppermute | solution.py:17
  28.0 4.3 %collective-permute-start.12 = (bf16[144,128]{1,0:T(8,128)(2,1)S(1)}, bf16[144,128]{1,0:T(8,128)(2,1)S(1)}, u32[]{:S(2)}, u32[]{:S(2)}) collective-permute-start(bf16[144,128]{1,0:T(8,128)(2,1)S(1)} %collective-permute-done.9.refs_0_.refs_5_), channel_id=1, source_target_pairs={{0,1},{1,0},{2,3},{3,2},{4,5},{5,4},{6,7},{7,6},{8,9},{9,8},{10,11... | collective-permute-start | bytes 110600 | tf_op jit(solution)/shard_map/ppermute | solution.py:17
  28.4 4.4 %collective-permute-start.13 = (bf16[144,128]{1,0:T(8,128)(2,1)S(1)}, bf16[144,128]{1,0:T(8,128)(2,1)S(1)}, u32[]{:S(2)}, u32[]{:S(2)}) collective-permute-start(bf16[144,128]{1,0:T(8,128)(2,1)S(1)} %collective-permute-done.10.refs_1_.refs_6_), channel_id=1, source_target_pairs={{0,1},{1,0},{2,3},{3,2},{4,5},{5,4},{6,7},{7,6},{8,9},{9,8},{10,11... | collective-permute-start | bytes 110600 | tf_op jit(solution)/shard_map/ppermute | solution.py:17
  33.6 3.2 %collective-permute-start.14 = (bf16[48,128]{1,0:T(8,128)(2,1)S(1)}, bf16[48,128]{1,0:T(8,128)(2,1)S(1)}, u32[]{:S(2)}, u32[]{:S(2)}) collective-permute-start(bf16[48,128]{1,0:T(8,128)(2,1)S(1)} %get-tuple-element.17), channel_id=1, source_target_pairs={{0,24},{8,16},{16,8},{24,0},{1,25},{9,17},{17,9},{25,1},{2,26},{10... | collective-permute-start | bytes 36872 | tf_op jit(solution)/shard_map/ppermute | solution.py:17
  33.7 3.8 %collective-permute-start.15 = (bf16[48,128]{1,0:T(8,128)(2,1)S(1)}, bf16[48,128]{1,0:T(8,128)(2,1)S(1)}, u32[]{:S(2)}, u32[]{:S(2)}) collective-permute-start(bf16[48,128]{1,0:T(8,128)(2,1)S(1)} %get-tuple-element.18), channel_id=1, source_target_pairs={{0,16},{8,24},{16,0},{24,8},{1,17},{9,25},{17,1},{25,9},{2,18},{10... | collective-permute-start | bytes 36872 | tf_op jit(solution)/shard_map/ppermute | solution.py:17
  34.3 3.1 %collective-permute-start.16 = (bf16[48,128]{1,0:T(8,128)(2,1)S(1)}, bf16[48,128]{1,0:T(8,128)(2,1)S(1)}, u32[]{:S(2)}, u32[]{:S(2)}) collective-permute-start(bf16[48,128]{1,0:T(8,128)(2,1)S(1)} %get-tuple-element.19), channel_id=1, source_target_pairs={{0,8},{8,0},{16,24},{24,16},{1,9},{9,1},{17,25},{25,17},{2,10},{10... | collective-permute-start | bytes 36872 | tf_op jit(solution)/shard_map/ppermute | solution.py:17
